TPU v7x, 512 devices: a whole 4x4x16 slice. The times are simulated.
512 devices in a mesh: seq: 64 (over z, x), head: 8 (over y, core).
Axes of the slice: x: 4, y: 4, z: 16, core: 2. Of those that a mesh axis runs over, the one named last changes fastest.
Arguments:
- query_rows: bfloat16 [16384, 4096], P('seq', 'head'), may hold values from -6 to 6
- key_rows: bfloat16 [16384, 4096], P('seq', 'head'), may hold values from -6 to 6
- value_rows: bfloat16 [16384, 4096], P('seq', 'head'), may hold values from -110 to 110
- feat_query: bfloat16 [32, 128, 128], P('head'), may hold values from -0.5 to 0.5
- feat_key: bfloat16 [32, 128, 128], P('head'), may hold values from -0.5 to 0.5
- norm_gain: float32 [4096], P('head'), may hold values from 0.25 to 1.75
- grad_out: bfloat16 [16384, 4096], P('seq', 'head'), may hold values from -6 to 6
Outputs:
- attended: bfloat16 [16384, 4096], P('seq', 'head')
- grad_query: bfloat16 [16384, 4096], P('seq', 'head')
- grad_key: bfloat16 [16384, 4096], P('seq', 'head')
- grad_value: bfloat16 [16384, 4096], P('seq', 'head')
- grad_feat_query: float32 [32, 128, 128], P('head')
- grad_feat_key: float32 [32, 128, 128], P('head')
- grad_gain: float32 [4096], P('head')
All inputs are finite; a program needn't handle non-finite values.
Results may differ from a plain program's by a relative error of at most 0.017.
Values may be sent and summed in bfloat16 or wider, within the bound.
No kernel may reach another device: no remote copies, remote signals or barrier semaphores. Data moves between devices by JAX's collectives and lax.ppermute only.
A program may use at most 128 MiB of HBM per device.

v0:
```python
import jax
import jax.numpy as jnp
from jax import lax
from jax.sharding import PartitionSpec as P

EPSILON = 1e-05


def prefix(x, axis, join, neutral, backward):
    count = lax.axis_size(axis)
    place = lax.axis_index(axis)
    ahead = count - 1 - place if backward else place
    gathered = lax.all_gather(x.astype(jnp.bfloat16), axis)
    state = jnp.zeros_like(x) + jnp.asarray(neutral, x.dtype)

    def one(turn, state):
        source = count - 1 - turn if backward else turn
        return join(state, lax.dynamic_index_in_dim(gathered, source, 0, False).astype(x.dtype))

    return lax.fori_loop(0, ahead, one, state)


def silu_slope(pre_act):
    sigmoid_val = jax.nn.sigmoid(pre_act)
    return sigmoid_val * (1.0 + pre_act * (1.0 - sigmoid_val))


def featurize(block, weights):
    pre_act = jnp.einsum("thd,hde->the", block, weights, preferred_element_type=jnp.float32)
    return (pre_act, jax.nn.silu(pre_act).astype(jnp.bfloat16))


def add_states(earlier, latter):
    return earlier + latter


def shards(query_rows, key_rows, value_rows, feat_query, feat_key, norm_gain, grad_out):
    token_count = query_rows.shape[0]
    head_local = feat_query.shape[0]
    head_size = feat_query.shape[1]
    full_width = head_local * head_size * lax.axis_size("head")
    shape_heads = (token_count, head_local, head_size)
    queries = query_rows.reshape(shape_heads)
    keys_local = key_rows.reshape(shape_heads)
    values = value_rows.reshape(shape_heads)
    cotangent = grad_out.reshape(shape_heads)
    gain_cols = norm_gain.reshape(head_local, head_size)
    positions = jnp.arange(token_count)
    causal = (positions[:, None] >= positions[None, :])[None]
    query_pre, query_feat = featurize(queries, feat_query)
    key_pre, key_feat = featurize(keys_local, feat_key)
    local_state = jnp.einsum("thd,the->hde", key_feat, values, preferred_element_type=jnp.float32)
    carried_state = prefix(local_state, "seq", add_states, jnp.zeros_like(local_state), False)
    carried_round = carried_state.astype(jnp.bfloat16)
    scores = jnp.einsum("thd,shd->hts", query_feat, key_feat, preferred_element_type=jnp.float32)
    scores = jnp.where(causal, scores, 0.0).astype(jnp.bfloat16)
    intra = jnp.einsum("hts,she->the", scores, values, preferred_element_type=jnp.float32)
    pre_norm = intra + jnp.einsum(
        "thd,hde->the", query_feat, carried_round, preferred_element_type=jnp.float32
    )
    square_total = lax.psum(jnp.sum(pre_norm * pre_norm, axis=(1, 2)), "head")
    rms_rows = jnp.sqrt(square_total / full_width + EPSILON)
    normed = pre_norm / rms_rows[:, None, None]
    attended = (normed * gain_cols).astype(jnp.bfloat16).reshape(token_count, -1)
    cotan_wide = cotangent.astype(jnp.float32)
    scaled = cotan_wide * gain_cols
    slope_total = lax.psum(jnp.sum(scaled * normed, axis=(1, 2)), "head")
    delta_pre = (
        (scaled - normed * (slope_total / full_width)[:, None, None]) / rms_rows[:, None, None]
    ).astype(jnp.bfloat16)
    gain_local = jnp.sum(cotan_wide * normed, axis=0).reshape(-1)
    back_local = jnp.einsum(
        "thd,the->hde", query_feat, delta_pre, preferred_element_type=jnp.float32
    )
    later_state = prefix(back_local, "seq", add_states, jnp.zeros_like(back_local), True)
    later_round = later_state.astype(jnp.bfloat16)
    back_scores = jnp.where(
        causal,
        jnp.einsum("the,she->hts", delta_pre, values, preferred_element_type=jnp.float32),
        0.0,
    ).astype(jnp.bfloat16)
    query_grad = jnp.einsum(
        "hts,shd->thd", back_scores, key_feat, preferred_element_type=jnp.float32
    ) + jnp.einsum("the,hde->thd", delta_pre, carried_round, preferred_element_type=jnp.float32)
    query_pre_grad = (query_grad * silu_slope(query_pre)).astype(jnp.bfloat16)
    grad_query = (
        jnp.einsum("the,hde->thd", query_pre_grad, feat_query, preferred_element_type=jnp.float32)
        .astype(jnp.bfloat16)
        .reshape(token_count, -1)
    )
    query_weight_part = jnp.einsum(
        "thd,the->hde", queries, query_pre_grad, preferred_element_type=jnp.float32
    )
    key_grad = jnp.einsum(
        "hts,thd->shd", back_scores, query_feat, preferred_element_type=jnp.float32
    ) + jnp.einsum("the,hde->thd", values, later_round, preferred_element_type=jnp.float32)
    key_pre_grad = (key_grad * silu_slope(key_pre)).astype(jnp.bfloat16)
    grad_key = (
        jnp.einsum("the,hde->thd", key_pre_grad, feat_key, preferred_element_type=jnp.float32)
        .astype(jnp.bfloat16)
        .reshape(token_count, -1)
    )
    key_weight_part = jnp.einsum(
        "thd,the->hde", keys_local, key_pre_grad, preferred_element_type=jnp.float32
    )
    grad_value = (
        (
            jnp.einsum("hts,the->she", scores, delta_pre, preferred_element_type=jnp.float32)
            + jnp.einsum("thd,hde->the", key_feat, later_round, preferred_element_type=jnp.float32)
        )
        .astype(jnp.bfloat16)
        .reshape(token_count, -1)
    )
    grad_feat_query, grad_feat_key, grad_gain = lax.psum(
        (query_weight_part, key_weight_part, gain_local), "seq"
    )
    return (attended, grad_query, grad_key, grad_value, grad_feat_query, grad_feat_key, grad_gain)


def solution(mesh):
    in_specs = (
        P("seq", "head"),
        P("seq", "head"),
        P("seq", "head"),
        P("head", None, None),
        P("head", None, None),
        P("head"),
        P("seq", "head"),
    )
    out_specs = (
        P("seq", "head"),
        P("seq", "head"),
        P("seq", "head"),
        P("seq", "head"),
        P("head", None, None),
        P("head", None, None),
        P("head"),
    )
    return jax.shard_map(shards, mesh=mesh, in_specs=in_specs, out_specs=out_specs, check_vma=False)
```

profile of v0, /device:TPU:8, one launch (start us, length us, event | category | flops | bytes accessed | tf_op | source)
XLA Modules:
  0.0 736.9 jit_solution(6816294012118932483)
XLA Ops:
  7.2 2.2 multiply_convert_fusion.1
  10.4 1.1 copy.52
  11.5 2.1 multiply_convert_fusion.2
  14.3 158.9 %all-gather.5.cloned.1.call-done = bf16[256,128,128]{2,1,0:T(8,128)(2,1)} async-done(((bf16[4,128,128]{2,1,0:T(8,128)(2,1)}), bf16[256,128,128]{2,1,0:T(8,128)(2,1)}) %all-gather.5.cloned.1.call-update) | async-done | bytes 8388624 | tf_op jit(solution)/shard_map/all_gather | solution.py:13
  173.5 10.0 %psum.35 = f32[256]{0:T(256)S(1)} all-reduce(f32[256]{0:T(256)S(1)} %get-tuple-element.128), channel_id=1, replica_groups=mesh['seq'=64,'head'=8] {'head'}, use_global_device_ids=true, to_apply=%region_3.4 | all-reduce | flops 256 | bytes 2048 | tf_op jit(solution)/shard_map/psum | solution.py:61
  183.8 12.4 %psum.36 = f32[256]{0:T(256)S(1)} all-reduce(f32[256]{0:T(256)S(1)} %get-tuple-element.103), channel_id=1, replica_groups=mesh['seq'=64,'head'=8] {'head'}, use_global_device_ids=true, to_apply=%region_5.6 | all-reduce | flops 256 | bytes 2048 | tf_op jit(solution)/shard_map/psum | solution.py:67
  198.0 1.3 fusion.7
  199.3 1.9 convolution_bitcast_fusion.5
  201.7 205.9 %all-gather.7.cloned.1.call-done = bf16[256,128,128]{2,1,0:T(8,128)(2,1)} async-done(((bf16[4,128,128]{2,1,0:T(8,128)(2,1)}), bf16[256,128,128]{2,1,0:T(8,128)(2,1)}) %all-gather.7.cloned.1.call-update) | async-done | bytes 8388624 | tf_op jit(solution)/shard_map/all_gather | solution.py:13
  407.6 62.1 %while.23 = (s32[]{:T(128)}, f32[4,128,128]{2,1,0:T(8,128)S(1)}, s32[]{:T(128)}, bf16[64,4,128,128]{3,2,1,0:T(8,128)(2,1)}, s32[]{:T(128)}, /*index=5*/s32[]{:T(128)}, s32[]{:T(128)}, s32[]{:T(128)}) while((s32[]{:T(128)}, f32[4,128,128]{2,1,0:T(8,128)S(1)}, s32[]{:T(128)}, bf16[64,4,128,128]{3,2,1,0:T(8,128)(2,1)}, s32[]{:T(128)}, ...), condition=%wide.region_7.8_spmd, body=%wide.region_6.7_spmd.sunk | while | flops 131078 | bytes 655503 | solution.py:20
  407.6 1.0 convert_add_fusion.5
  408.6 1.0 convert_add_fusion.5
  409.6 1.0 convert_add_fusion.5
  410.6 1.0 convert_add_fusion.5
  411.5 1.0 convert_add_fusion.5
  412.5 1.0 convert_add_fusion.5
  413.5 1.0 convert_add_fusion.5
  414.5 1.0 convert_add_fusion.5
  415.5 1.0 convert_add_fusion.5
  416.5 1.0 convert_add_fusion.5
  417.5 1.0 convert_add_fusion.5
  418.5 1.0 convert_add_fusion.5
  419.4 1.0 convert_add_fusion.5
  420.4 1.0 convert_add_fusion.5
  421.4 1.0 convert_add_fusion.5
  422.4 1.0 convert_add_fusion.5
  423.4 1.0 convert_add_fusion.5
  424.4 1.0 convert_add_fusion.5
  425.4 1.0 convert_add_fusion.5
  426.3 1.0 convert_add_fusion.5
  427.3 1.0 convert_add_fusion.5
  428.3 1.0 convert_add_fusion.5
  429.3 1.0 convert_add_fusion.5
  430.3 1.0 convert_add_fusion.5
  431.3 1.0 convert_add_fusion.5
  434.2 1.0 convert_add_fusion.5
  438.2 1.0 convert_add_fusion.5
  443.1 1.0 convert_add_fusion.5
  448.0 1.0 convert_add_fusion.5
  453.0 1.0 convert_add_fusion.5
  456.9 1.0 convert_add_fusion.5
  461.8 1.0 convert_add_fusion.5
  466.8 1.0 convert_add_fusion.5
  469.7 1.3 fusion.8
  473.9 138.6 %psum.39 = f32[512]{0:T(512)} all-reduce(f32[512]{0:T(512)S(1)} %bitcast.136), channel_id=1, replica_groups=mesh['seq'=64,'head'=8] {'seq'}, use_global_device_ids=true, to_apply=%region_11.12 | all-reduce | flops 512 | bytes 4096 | tf_op jit(solution)/shard_map/psum | solution.py:114
  614.7 112.1 %all-reduce.3.cloned.1.call-done = (f32[4,128,128]{1,2,0:T(8,128)}, f32[4,128,128]{1,2,0:T(8,128)}) async-done(((f32[4,128,128]{1,2,0:T(8,128)}, f32[4,128,128]{1,2,0:T(8,128)}), (f32[4,128,128]{1,2,0:T(8,128)}, f32[4,128,128]{1,2,0:T(8,128)})) %all-reduce.3.cloned.1.call-update) | async-done | bytes 524304 | tf_op jit(solution)/shard_map/psum | solution.py:114
  726.8 1.8 copy.68
  728.6 1.8 copy.69
  (71 shorter events, 38.4 us)
Async XLA Ops:
  7.2 2.2 copy-start
  7.2 176.3 %copy-start.4 = (f32[512]{0:T(512)S(1)}, f32[512]{0:T(512)}, u32[]{:S(2)}) copy-start(f32[512]{0:T(512)} %param.16) | copy-start | bytes 6148
  7.2 166.0 %all-gather.5.cloned.1.call-start = ((), (), s32[]{:S(2)}) async-start(), calls=%async_computation | async-start | bytes 8519680 | tf_op jit(solution)/shard_map/all_gather | solution.py:13
  10.3 397.2 %all-gather.7.cloned.1.call-start = ((), (), s32[]{:S(2)}) async-start(), calls=%async_computation.1 | async-start | bytes 8519680 | tf_op jit(solution)/shard_map/all_gather | solution.py:13
  196.3 274.8 %copy-start.1 = (bf16[256,512]{1,0:T(8,128)(2,1)S(1)}, bf16[256,512]{1,0:T(8,128)(2,1)}, u32[]{:S(2)}) copy-start(bf16[256,512]{1,0:T(8,128)(2,1)} %param.12) | copy-start | bytes 786436
  197.2 529.6 %all-reduce.3.cloned.1.call-start = ((), (), s32[]{:S(2)}) async-start(), calls=%async_computation.2 | async-start | bytes 1048576 | tf_op jit(solution)/shard_map/psum | solution.py:114
  197.3 274.7 %copy-start.2 = (bf16[4,128,128]{2,1,0:T(8,128)(2,1)S(1)}, bf16[4,128,128]{2,1,0:T(8,128)(2,1)}, u32[]{:S(2)}) copy-start(bf16[4,128,128]{2,1,0:T(8,128)(2,1)} %param.14) | copy-start | bytes 393220
  199.3 414.4 %copy-start.3 = (bf16[4,128,128]{2,1,0:T(8,128)(2,1)S(1)}, bf16[4,128,128]{2,1,0:T(8,128)(2,1)}, u32[]{:S(2)}) copy-start(bf16[4,128,128]{2,1,0:T(8,128)(2,1)} %param.15) | copy-start | bytes 393220
Sparse Core Ops, SparseCore 0:
  11.5 161.5 all-gather.4
  197.4 210.1 all-gather.6
  472.1 254.6 all-reduce.2
where the time goes:
time: 738 us; the launch traced here: 737 us
  waiting for transfers between devices  477 us (65%)
  blocking collectives  161 us (22%)
  other arithmetic  61.2 us (8%)
  matrix products  14.3 us (2%)
  between operations  13.9 us (2%)
  local copies, waits for them, and re-layouts  8.1 us (1%)
    all_gather x2, waiting for transfers between devices, prefix(): gathered = lax.all_gather(x.astype(jnp.bfloat16), axis)  365 us
    psum x1, blocking collectives, shards(): lax.psum((query_weight_part, key_weight_part, gain_local), 'seq')  139 us
    psum x1, waiting for transfers between devices, shards(): lax.psum((query_weight_part, key_weight_part, gain_local), 'seq')  112 us
    add x63, other arithmetic, add_states(): return earlier + latter  60.7 us
  transfers between devices with their start and end apart: 3, of which 3 were waited for; matrix products, arithmetic and copies ran while one was open for 2% of the time, Pallas kernels for 0%

commit v1 on v0

v1 whole, which is shorter than its diff:
```python
import jax
import jax.numpy as jnp
from jax import lax
from jax.sharding import Mesh, PartitionSpec as P

EPSILON = 1e-05
BF = jnp.bfloat16
F32 = jnp.float32
NEAR = 8


def swap(x, axis):
    return lax.all_to_all(x, axis, 0, 0)


def everyone(x, axis):
    return swap(jnp.broadcast_to(x[None], (lax.axis_size(axis),) + x.shape), axis)


def masked_sum(parts, backward):
    place = lax.axis_index("far")
    index = jnp.arange(parts.shape[0])
    keep = index > place if backward else index < place
    return jnp.sum(jnp.where(keep[:, None, None], parts.astype(F32), 0.0), axis=0)


def within(parts, backward):
    count = parts.shape[0]
    order = range(count - 1, -1, -1) if backward else range(count)
    total = jnp.zeros(parts.shape[1:], F32)
    sums = [None] * count
    for i in order:
        sums[i] = total
        total = total + parts[i].astype(F32)
    return jnp.stack(sums), total


def silu_slope(pre_act):
    sigmoid_val = jax.nn.sigmoid(pre_act)
    return sigmoid_val * (1.0 + pre_act * (1.0 - sigmoid_val))


def featurize(block, weights):
    pre_act = jnp.einsum("thd,hde->the", block, weights, preferred_element_type=F32)
    return (pre_act, jax.nn.silu(pre_act).astype(BF))


def shards(query_rows, key_rows, value_rows, feat_query, feat_key, norm_gain, grad_out):
    token_count = query_rows.shape[0]
    head_local = feat_query.shape[0]
    head_size = feat_query.shape[1]
    near = lax.axis_size("near")
    far = lax.axis_size("far")
    full_width = head_local * head_size * lax.axis_size("head")
    shape_heads = (token_count, head_local, head_size)
    chunk = head_local * head_size // near
    queries = query_rows.reshape(shape_heads)
    keys_local = key_rows.reshape(shape_heads)
    values = value_rows.reshape(shape_heads)
    cotangent = grad_out.reshape(shape_heads)
    gain_cols = norm_gain.reshape(head_local, head_size)
    positions = jnp.arange(token_count)
    causal = (positions[:, None] >= positions[None, :])[None]
    key_pre, key_feat = featurize(keys_local, feat_key)
    local_state = jnp.einsum("thd,the->hde", key_feat, values, preferred_element_type=F32)
    parts = swap(local_state.astype(BF).reshape(near, chunk, head_size), "near")
    sums, total = within(parts, False)
    offset = masked_sum(everyone(total.astype(BF), "far"), False)
    carried_round = swap((sums + offset).astype(BF), "near").reshape(
        head_local, head_size, head_size
    )
    query_pre, query_feat = featurize(queries, feat_query)
    scores = jnp.einsum("thd,shd->hts", query_feat, key_feat, preferred_element_type=F32)
    scores = jnp.where(causal, scores, 0.0).astype(BF)
    intra = jnp.einsum("hts,she->the", scores, values, preferred_element_type=F32)
    pre_norm = intra + jnp.einsum(
        "thd,hde->the", query_feat, carried_round, preferred_element_type=F32
    )
    cotan_wide = cotangent.astype(F32)
    scaled = cotan_wide * gain_cols
    rows = jnp.stack(
        [jnp.sum(pre_norm * pre_norm, axis=(1, 2)), jnp.sum(scaled * pre_norm, axis=(1, 2))]
    )
    rows = jnp.sum(everyone(rows, "head"), axis=0)
    rms_rows = jnp.sqrt(rows[0] / full_width + EPSILON)
    slope = rows[1] / rms_rows / full_width
    normed = pre_norm / rms_rows[:, None, None]
    attended = (normed * gain_cols).astype(BF).reshape(token_count, -1)
    delta_pre = ((scaled - normed * slope[:, None, None]) / rms_rows[:, None, None]).astype(BF)
    gain_local = jnp.sum(cotan_wide * normed, axis=0).reshape(-1)
    back_local = jnp.einsum("thd,the->hde", query_feat, delta_pre, preferred_element_type=F32)
    back_scores = jnp.where(
        causal,
        jnp.einsum("the,she->hts", delta_pre, values, preferred_element_type=F32),
        0.0,
    ).astype(BF)
    query_grad = jnp.einsum(
        "hts,shd->thd", back_scores, key_feat, preferred_element_type=F32
    ) + jnp.einsum("the,hde->thd", delta_pre, carried_round, preferred_element_type=F32)
    query_pre_grad = (query_grad * silu_slope(query_pre)).astype(BF)
    grad_query = (
        jnp.einsum("the,hde->thd", query_pre_grad, feat_query, preferred_element_type=F32)
        .astype(BF)
        .reshape(token_count, -1)
    )
    query_weight_part = jnp.einsum(
        "thd,the->hde", queries, query_pre_grad, preferred_element_type=F32
    )
    gain_rows = 16
    gain_pad = jnp.zeros((near, gain_rows * head_size), F32)
    gain_pad = gain_pad.at[:, : gain_local.shape[0] // near].set(gain_local.reshape(near, -1))
    payload = jnp.concatenate(
        [
            back_local.astype(BF).reshape(near, chunk, head_size),
            query_weight_part.astype(BF).reshape(near, chunk, head_size),
            gain_pad.astype(BF).reshape(near, gain_rows, head_size),
        ],
        axis=1,
    )
    parts = swap(payload, "near")
    sums, total = within(parts[:, :chunk], True)
    side = jnp.sum(parts[:, chunk:].astype(F32), axis=0).astype(BF)
    slim = chunk // far
    payload = jnp.concatenate(
        [
            jnp.broadcast_to(total.astype(BF)[None], (far, chunk, head_size)),
            side[:chunk].reshape(far, slim, head_size),
            jnp.broadcast_to(side[None, chunk : chunk + 8], (far, 8, head_size)),
        ],
        axis=1,
    )
    parts_far = swap(payload, "far")
    offset = masked_sum(parts_far[:, :chunk], True)
    side = jnp.sum(parts_far[:, chunk:].astype(F32), axis=0).astype(BF)
    later_round = swap((sums + offset).astype(BF), "near").reshape(
        head_local, head_size, head_size
    )
    key_grad = jnp.einsum(
        "hts,thd->shd", back_scores, query_feat, preferred_element_type=F32
    ) + jnp.einsum("the,hde->thd", values, later_round, preferred_element_type=F32)
    key_pre_grad = (key_grad * silu_slope(key_pre)).astype(BF)
    key_weight_part = jnp.einsum(
        "thd,the->hde", keys_local, key_pre_grad, preferred_element_type=F32
    )
    parts = swap(key_weight_part.astype(BF).reshape(near, chunk, head_size), "near")
    total = jnp.sum(parts.astype(F32), axis=0).astype(BF)
    parts = everyone(jnp.concatenate([total, side[:slim]], axis=0), "far")
    total = jnp.sum(parts[:, :chunk].astype(F32), axis=0).astype(BF)
    done = everyone(
        jnp.concatenate([total, parts[:, chunk:].reshape(chunk, head_size), side[slim:]], axis=0),
        "near",
    ).astype(F32)
    grad_feat_key = done[:, :chunk].reshape(feat_key.shape)
    grad_feat_query = done[:, chunk : 2 * chunk].reshape(feat_query.shape)
    grad_gain = done[:, 2 * chunk, : gain_local.shape[0] // near].reshape(-1)
    grad_key = (
        jnp.einsum("the,hde->thd", key_pre_grad, feat_key, preferred_element_type=F32)
        .astype(BF)
        .reshape(token_count, -1)
    )
    grad_value = (
        (
            jnp.einsum("hts,the->she", scores, delta_pre, preferred_element_type=F32)
            + jnp.einsum("thd,hde->the", key_feat, later_round, preferred_element_type=F32)
        )
        .astype(BF)
        .reshape(token_count, -1)
    )
    return (attended, grad_query, grad_key, grad_value, grad_feat_query, grad_feat_key, grad_gain)


def solution(mesh):
    seq, head = mesh.devices.shape
    split = Mesh(mesh.devices.reshape(seq // NEAR, NEAR, head), ("far", "near", "head"))
    wide = P(("far", "near"), "head")
    per_head = P("head", None, None)
    in_specs = (wide, wide, wide, per_head, per_head, P("head"), wide)
    out_specs = (wide, wide, wide, wide, per_head, per_head, P("head"))
    return jax.shard_map(shards, mesh=split, in_specs=in_specs, out_specs=out_specs, check_vma=False)
```

time: 738 us -> 157 us (0.21)
  waiting for transfers between devices: 477 us -> 59.9 us
  blocking collectives: 161 us -> 17.4 us
  other arithmetic: 61.2 us -> 10.1 us
  starting transfers between devices: 0.12 us -> 45.6 us
  between operations: 13.9 us -> 1.08 us
    all_gather x2 -> x0, waiting for transfers between devices: 365 us -> none  [prefix(): gathered = lax.all_gather(x.astype(jnp.bfloat16), axis)]
    psum x3 -> x0, blocking collectives: 161 us -> none  [the longest x1 139 us: shards(): lax.psum((query_weight_part, key_weight_part, gain_local), 'seq')]
    psum x1 -> x0, waiting for transfers between devices: 112 us -> none  [shards(): lax.psum((query_weight_part, key_weight_part, gain_local), 'seq')]
    add x63 -> x0, other arithmetic: 60.7 us -> none  [add_states(): return earlier + latter]
    all_to_all x0 -> x9, waiting for transfers between devices: none -> 59.9 us  [swap(): return lax.all_to_all(x, axis, 0, 0)]
    all_to_all x0 -> x9, starting transfers between devices: none -> 45.6 us  [swap(): return lax.all_to_all(x, axis, 0, 0)]
    all_to_all x0 -> x1, blocking collectives: none -> 17.4 us  [swap(): return lax.all_to_all(x, axis, 0, 0)]
  transfers between devices with their start and end apart: 3 -> 9, of which waited for: 3 -> 9; matrix products, arithmetic and copies ran while one was open for 2% -> 8% of each run, Pallas kernels for 0% -> 0%
where the time goes in v1:
time: 157 us; the launch traced here: 156 us
  waiting for transfers between devices  59.9 us (38%)
  starting transfers between devices  45.6 us (29%)
  blocking collectives  17.4 us (11%)
  local copies, waits for them, and re-layouts  12.1 us (8%)
  other arithmetic  10.1 us (6%)
  matrix products  9.68 us (6%)
    all_to_all x9, waiting for transfers between devices, swap(): return lax.all_to_all(x, axis, 0, 0)  59.9 us
    all_to_all x9, starting transfers between devices, swap(): return lax.all_to_all(x, axis, 0, 0)  45.6 us
    all_to_all x1, blocking collectives, swap(): return lax.all_to_all(x, axis, 0, 0)  17.4 us
    unnamed x33, local copies, waits for them, and re-layouts  6.45 us
    unnamed x10, other arithmetic  3.76 us
  transfers between devices with their start and end apart: 9, of which 9 were waited for; matrix products, arithmetic and copies ran while one was open for 8% of the time, Pallas kernels for 0%

profile of v1, /device:TPU:8, one launch (start us, length us, event | category | flops | bytes accessed | tf_op | source)
XLA Modules:
  0.0 156.0 jit_solution(13100995014641875931)
XLA Ops:
  0.7 1.1 copy.146
  1.8 1.1 multiply_convert_fusion.1
  2.9 0.9 convolution_convert_fusion.5
  3.8 5.8 %all-to-all-start = ((bf16[8,64,128]{2,1,0:T(8,128)(2,1)}), bf16[8,64,128]{2,1,0:T(8,128)(2,1)S(1)}, u32[]{:S(2)}, u32[]{:S(2)}) async-start(bf16[8,64,128]{2,1,0:T(8,128)(2,1)} %bitcast.3), calls=%async_computation | async-start | bytes 262144 | tf_op jit(solution)/shard_map/all_to_all | solution.py:13
  9.7 0.8 copy-done.2
  10.7 0.7 copy-done.6
  11.4 1.1 multiply_convert_fusion.2
  12.5 3.6 %all-to-all-done = bf16[8,64,128]{2,1,0:T(8,128)(2,1)S(1)} async-done(((bf16[8,64,128]{2,1,0:T(8,128)(2,1)}), bf16[8,64,128]{2,1,0:T(8,128)(2,1)S(1)}, u32[]{:S(2)}, u32[]{:S(2)}) %all-to-all-start) | async-done | bytes 131104 | tf_op jit(solution)/shard_map/all_to_all | solution.py:13
  16.2 0.7 broadcast_in_dim.91
  16.9 14.2 %all-to-all-start.1 = ((bf16[8,64,128]{2,1,0:T(8,128)(2,1)}), bf16[8,64,128]{2,1,0:T(8,128)(2,1)S(1)}, u32[]{:S(2)}, u32[]{:S(2)}) async-start(bf16[8,64,128]{2,1,0:T(8,128)(2,1)} %broadcast_in_dim.91), calls=%async_computation.1 | async-start | bytes 262144 | tf_op jit(solution)/shard_map/all_to_all | solution.py:13
  31.1 13.7 %all-to-all-done.1 = bf16[8,64,128]{2,1,0:T(8,128)(2,1)S(1)} async-done(((bf16[8,64,128]{2,1,0:T(8,128)(2,1)}), bf16[8,64,128]{2,1,0:T(8,128)(2,1)S(1)}, u32[]{:S(2)}, u32[]{:S(2)}) %all-to-all-start.1) | async-done | bytes 131104 | tf_op jit(solution)/shard_map/all_to_all | solution.py:13
  44.9 0.7 add_convert_fusion.1
  45.6 3.5 %all-to-all-start.2 = ((bf16[8,64,128]{2,1,0:T(8,128)(2,1)}), bf16[8,64,128]{2,1,0:T(8,128)(2,1)S(1)}, u32[]{:S(2)}, u32[]{:S(2)}) async-start(bf16[8,64,128]{2,1,0:T(8,128)(2,1)} %add_convert_fusion.1), calls=%async_computation.2 | async-start | bytes 262144 | tf_op jit(solution)/shard_map/all_to_all | solution.py:13
  49.8 5.9 %all-to-all-done.2 = bf16[8,64,128]{2,1,0:T(8,128)(2,1)S(1)} async-done(((bf16[8,64,128]{2,1,0:T(8,128)(2,1)}), bf16[8,64,128]{2,1,0:T(8,128)(2,1)S(1)}, u32[]{:S(2)}, u32[]{:S(2)}) %all-to-all-start.2) | async-done | bytes 131104 | tf_op jit(solution)/shard_map/all_to_all | solution.py:13
  56.7 4.9 %all-to-all-start.3 = ((f32[8,2,256]{2,1,0:T(2,128)}), f32[8,2,256]{2,1,0:T(2,128)S(1)}, u32[]{:S(2)}, u32[]{:S(2)}) async-start(f32[8,2,256]{2,1,0:T(2,128)} %broadcast_in_dim.93), calls=%async_computation.3 | async-start | bytes 32768 | tf_op jit(solution)/shard_map/all_to_all | solution.py:13
  61.6 0.6 compare_reduce_fusion
  62.2 3.3 %all-to-all-done.3 = f32[8,2,256]{2,1,0:T(2,128)S(1)} async-done(((f32[8,2,256]{2,1,0:T(2,128)}), f32[8,2,256]{2,1,0:T(2,128)S(1)}, u32[]{:S(2)}, u32[]{:S(2)}) %all-to-all-start.3) | async-done | bytes 16416 | tf_op jit(solution)/shard_map/all_to_all | solution.py:13
  65.6 0.9 divide_convert_fusion
  67.3 0.7 copy-done.11
  68.6 0.7 select_convert_fusion
  69.4 0.7 pad_maximum_fusion
  70.1 3.4 %all-to-all-start.4 = ((bf16[8,144,128]{2,1,0:T(8,128)(2,1)}), bf16[8,144,128]{2,1,0:T(8,128)(2,1)S(1)}, u32[]{:S(2)}, u32[]{:S(2)}) async-start(bf16[8,144,128]{2,1,0:T(8,128)(2,1)} %pad_maximum_fusion), calls=%async_computation.4 | async-start | bytes 589824 | tf_op jit(solution)/shard_map/all_to_all | solution.py:13
  73.5 7.7 %all-to-all-done.4 = bf16[8,144,128]{2,1,0:T(8,128)(2,1)S(1)} async-done(((bf16[8,144,128]{2,1,0:T(8,128)(2,1)}), bf16[8,144,128]{2,1,0:T(8,128)(2,1)S(1)}, u32[]{:S(2)}, u32[]{:S(2)}) %all-to-all-start.4) | async-done | bytes 294944 | tf_op jit(solution)/shard_map/all_to_all | solution.py:13
  81.3 0.7 pad_maximum_fusion.1
  82.0 3.4 %all-to-all-start.5 = ((bf16[8,80,128]{2,1,0:T(8,128)(2,1)}), bf16[8,80,128]{2,1,0:T(8,128)(2,1)S(1)}, u32[]{:S(2)}, u32[]{:S(2)}) async-start(bf16[8,80,128]{2,1,0:T(8,128)(2,1)} %pad_maximum_fusion.1), calls=%async_computation.5 | async-start | bytes 327680 | tf_op jit(solution)/shard_map/all_to_all | solution.py:13
  85.4 0.6 constant_dynamic-update-slice_fusion.13
  87.3 0.6 constant_dynamic-update-slice_fusion.10
  87.9 0.6 constant_dynamic-update-slice_fusion.9
  88.5 0.6 constant_dynamic-update-slice_fusion.8
  90.4 10.9 %all-to-all-done.5 = bf16[8,80,128]{2,1,0:T(8,128)(2,1)S(1)} async-done(((bf16[8,80,128]{2,1,0:T(8,128)(2,1)}), bf16[8,80,128]{2,1,0:T(8,128)(2,1)S(1)}, u32[]{:S(2)}, u32[]{:S(2)}) %all-to-all-start.5) | async-done | bytes 163872 | tf_op jit(solution)/shard_map/all_to_all | solution.py:13
  101.4 1.6 %add_convert_fusion = bf16[8,64,128]{2,1,0:T(8,128)(2,1)} fusion(f32[8,64,128]{2,1,0:T(8,128)} %constant_dynamic-update-slice_fusion.7, f32[64,128]{1,0:T(8,128)S(1)} %select_reduce_fusion), kind=kLoop, calls=%fused_computation.39 | loop fusion | flops 131072 | bytes 425984 | tf_op jit(solution)/shard_map/convert_element_type | solution.py:135
  103.0 3.5 %all-to-all-start.6 = ((bf16[8,64,128]{2,1,0:T(8,128)(2,1)}), bf16[8,64,128]{2,1,0:T(8,128)(2,1)S(1)}, u32[]{:S(2)}, u32[]{:S(2)}) async-start(bf16[8,64,128]{2,1,0:T(8,128)(2,1)} %add_convert_fusion), calls=%async_computation.6 | async-start | bytes 262144 | tf_op jit(solution)/shard_map/all_to_all | solution.py:13
  106.5 1.0 fusion.26
  107.5 5.6 %all-to-all-done.6 = bf16[8,64,128]{2,1,0:T(8,128)(2,1)S(1)} async-done(((bf16[8,64,128]{2,1,0:T(8,128)(2,1)}), bf16[8,64,128]{2,1,0:T(8,128)(2,1)S(1)}, u32[]{:S(2)}, u32[]{:S(2)}) %all-to-all-start.6) | async-done | bytes 131104 | tf_op jit(solution)/shard_map/all_to_all | solution.py:13
  113.1 1.5 fusion.8
  114.6 0.9 convolution_convert_fusion.2
  115.4 3.4 %all-to-all-start.7 = ((bf16[8,64,128]{2,1,0:T(8,128)(2,1)}), bf16[8,64,128]{2,1,0:T(8,128)(2,1)S(1)}, u32[]{:S(2)}, u32[]{:S(2)}) async-start(bf16[8,64,128]{2,1,0:T(8,128)(2,1)} %bitcast.29), calls=%async_computation.7 | async-start | bytes 262144 | tf_op jit(solution)/shard_map/all_to_all | solution.py:13
  118.9 6.5 %all-to-all-done.7 = bf16[8,64,128]{2,1,0:T(8,128)(2,1)S(1)} async-done(((bf16[8,64,128]{2,1,0:T(8,128)(2,1)}), bf16[8,64,128]{2,1,0:T(8,128)(2,1)S(1)}, u32[]{:S(2)}, u32[]{:S(2)}) %all-to-all-start.7) | async-done | bytes 131104 | tf_op jit(solution)/shard_map/all_to_all | solution.py:13
  125.4 17.4 %all_to_all.50 = bf16[8,72,128]{2,1,0:T(8,128)(2,1)S(1)} all-to-all(bf16[8,72,128]{2,1,0:T(8,128)(2,1)S(1)} %broadcast_in_dim.98), channel_id=1, replica_groups=mesh['far'=8,'near'=8,'head'=8] {'far'}, dimensions={0} | all-to-all | bytes 294912 | tf_op jit(solution)/shard_map/all_to_all | solution.py:13
  142.9 0.7 broadcast_in_dim.99
  143.6 3.5 %all-to-all-start.9 = ((bf16[8,136,128]{2,1,0:T(8,128)(2,1)}), bf16[8,136,128]{2,1,0:T(8,128)(2,1)S(1)}, u32[]{:S(2)}, u32[]{:S(2)}) async-start(bf16[8,136,128]{2,1,0:T(8,128)(2,1)} %broadcast_in_dim.99), calls=%async_computation.9 | async-start | bytes 557056 | tf_op jit(solution)/shard_map/all_to_all | solution.py:13
  147.4 0.8 copy.124
  148.4 0.8 copy.123
  149.7 0.8 copy.126
  150.9 0.8 copy.125
  151.7 2.7 %all-to-all-done.9 = bf16[8,136,128]{2,1,0:T(8,128)(2,1)S(1)} async-done(((bf16[8,136,128]{2,1,0:T(8,128)(2,1)}), bf16[8,136,128]{2,1,0:T(8,128)(2,1)S(1)}, u32[]{:S(2)}, u32[]{:S(2)}) %all-to-all-start.9) | async-done | bytes 278560 | tf_op jit(solution)/shard_map/all_to_all | solution.py:13
  154.5 0.7 reshape_squeeze.3
  155.1 0.8 fusion.23
  (75 shorter events, 7.5 us)
Async XLA Ops:
  0.6 2.3 %copy-start = (bf16[256,512]{1,0:T(8,128)(2,1)S(1)}, bf16[256,512]{1,0:T(8,128)(2,1)}, u32[]{:S(2)}) copy-start(bf16[256,512]{1,0:T(8,128)(2,1)} %param.11) | copy-start | bytes 786436
  0.6 1.2 copy-start.8
  3.8 5.8 %copy-start.5 = (bf16[256,512]{1,0:T(8,128)(2,1)S(1)}, bf16[256,512]{1,0:T(8,128)(2,1)}, u32[]{:S(2)}) copy-start(bf16[256,512]{1,0:T(8,128)(2,1)} %param.9) | copy-start | bytes 786436
  3.8 12.4 %all-to-all-start = ((bf16[8,64,128]{2,1,0:T(8,128)(2,1)}), bf16[8,64,128]{2,1,0:T(8,128)(2,1)S(1)}, u32[]{:S(2)}, u32[]{:S(2)}) async-start(bf16[8,64,128]{2,1,0:T(8,128)(2,1)} %bitcast.3), calls=%async_computation | async-start | bytes 262144 | tf_op jit(solution)/shard_map/all_to_all | solution.py:13
  9.6 1.0 copy-start.2
  10.5 0.9 copy-start.6
  10.7 38.4 %copy-start.3 = (pred[256,256]{1,0:T(8,128)(4,1)}, pred[256,256]{1,0:T(8,128)(4,1)S(1)}, u32[]{:S(2)}) copy-start(pred[256,256]{1,0:T(8,128)(4,1)S(1)} %iota_compare_fusion) | copy-start | bytes 196612
  16.9 28.0 %all-to-all-start.1 = ((bf16[8,64,128]{2,1,0:T(8,128)(2,1)}), bf16[8,64,128]{2,1,0:T(8,128)(2,1)S(1)}, u32[]{:S(2)}, u32[]{:S(2)}) async-start(bf16[8,64,128]{2,1,0:T(8,128)(2,1)} %broadcast_in_dim.91), calls=%async_computation.1 | async-start | bytes 262144 | tf_op jit(solution)/shard_map/all_to_all | solution.py:13
  45.6 10.1 %all-to-all-start.2 = ((bf16[8,64,128]{2,1,0:T(8,128)(2,1)}), bf16[8,64,128]{2,1,0:T(8,128)(2,1)S(1)}, u32[]{:S(2)}, u32[]{:S(2)}) async-start(bf16[8,64,128]{2,1,0:T(8,128)(2,1)} %add_convert_fusion.1), calls=%async_computation.2 | async-start | bytes 262144 | tf_op jit(solution)/shard_map/all_to_all | solution.py:13
  49.8 5.9 %copy-start.10 = (f32[512]{0:T(512)S(1)}, f32[512]{0:T(512)}, u32[]{:S(2)}) copy-start(f32[512]{0:T(512)} %param.14) | copy-start | bytes 6148
  56.7 8.8 %all-to-all-start.3 = ((f32[8,2,256]{2,1,0:T(2,128)}), f32[8,2,256]{2,1,0:T(2,128)S(1)}, u32[]{:S(2)}, u32[]{:S(2)}) async-start(f32[8,2,256]{2,1,0:T(2,128)} %broadcast_in_dim.93), calls=%async_computation.3 | async-start | bytes 32768 | tf_op jit(solution)/shard_map/all_to_all | solution.py:13
  65.5 0.9 copy-start.4
  67.0 1.0 copy-start.11
  70.1 11.1 %all-to-all-start.4 = ((bf16[8,144,128]{2,1,0:T(8,128)(2,1)}), bf16[8,144,128]{2,1,0:T(8,128)(2,1)S(1)}, u32[]{:S(2)}, u32[]{:S(2)}) async-start(bf16[8,144,128]{2,1,0:T(8,128)(2,1)} %pad_maximum_fusion), calls=%async_computation.4 | async-start | bytes 589824 | tf_op jit(solution)/shard_map/all_to_all | solution.py:13
  82.0 19.2 %all-to-all-start.5 = ((bf16[8,80,128]{2,1,0:T(8,128)(2,1)}), bf16[8,80,128]{2,1,0:T(8,128)(2,1)S(1)}, u32[]{:S(2)}, u32[]{:S(2)}) async-start(bf16[8,80,128]{2,1,0:T(8,128)(2,1)} %pad_maximum_fusion.1), calls=%async_computation.5 | async-start | bytes 327680 | tf_op jit(solution)/shard_map/all_to_all | solution.py:13
  103.0 10.1 %all-to-all-start.6 = ((bf16[8,64,128]{2,1,0:T(8,128)(2,1)}), bf16[8,64,128]{2,1,0:T(8,128)(2,1)S(1)}, u32[]{:S(2)}, u32[]{:S(2)}) async-start(bf16[8,64,128]{2,1,0:T(8,128)(2,1)} %add_convert_fusion), calls=%async_computation.6 | async-start | bytes 262144 | tf_op jit(solution)/shard_map/all_to_all | solution.py:13
  115.4 9.9 %all-to-all-start.7 = ((bf16[8,64,128]{2,1,0:T(8,128)(2,1)}), bf16[8,64,128]{2,1,0:T(8,128)(2,1)S(1)}, u32[]{:S(2)}, u32[]{:S(2)}) async-start(bf16[8,64,128]{2,1,0:T(8,128)(2,1)} %bitcast.29), calls=%async_computation.7 | async-start | bytes 262144 | tf_op jit(solution)/shard_map/all_to_all | solution.py:13
  143.6 3.6 %copy-start.7 = (bf16[4,128,128]{2,1,0:T(8,128)(2,1)S(1)}, bf16[4,128,128]{2,1,0:T(8,128)(2,1)}, u32[]{:S(2)}) copy-start(bf16[4,128,128]{2,1,0:T(8,128)(2,1)} %param.12) | copy-start | bytes 393220
  143.6 10.8 %all-to-all-start.9 = ((bf16[8,136,128]{2,1,0:T(8,128)(2,1)}), bf16[8,136,128]{2,1,0:T(8,128)(2,1)S(1)}, u32[]{:S(2)}, u32[]{:S(2)}) async-start(bf16[8,136,128]{2,1,0:T(8,128)(2,1)} %broadcast_in_dim.99), calls=%async_computation.9 | async-start | bytes 557056 | tf_op jit(solution)/shard_map/all_to_all | solution.py:13
  147.4 1.0 copy-start.1
  149.7 0.9 copy-start.9

commit v2 on v0

v2 whole, which is shorter than its diff:
```python
import jax
import jax.numpy as jnp
from jax import lax
from jax.experimental import pallas as pl
from jax.experimental.pallas import tpu as pltpu
from jax.sharding import Mesh, PartitionSpec as P

EPSILON = 1e-05
BF = jnp.bfloat16
F32 = jnp.float32
NEAR = 8
GAIN_ROWS = 16
STAT_ROWS = 8
VMEM_BYTES = 24 * 1024 * 1024


def swap(x, axis):
    return lax.all_to_all(x, axis, 0, 0)


def run(kernel, outs, ins, after=(), flops=10**8):
    count = len(ins)

    def body(*refs):
        kernel(*refs[:count], *refs[count + len(after) :])

    whole = pl.BlockSpec(memory_space=pltpu.VMEM)
    return pl.pallas_call(
        body,
        out_shape=[jax.ShapeDtypeStruct(shape, dtype) for shape, dtype in outs],
        in_specs=[whole] * count + [pl.BlockSpec(memory_space=pl.ANY)] * len(after),
        out_specs=[whole] * len(outs),
        compiler_params=pltpu.CompilerParams(vmem_limit_bytes=VMEM_BYTES),
        cost_estimate=pl.CostEstimate(flops=flops, bytes_accessed=10**6, transcendentals=0),
    )(*ins, *after)


def dot(a, b, over_a, over_b):
    return lax.dot_general(a, b, (((over_a,), (over_b,)), ((), ())), preferred_element_type=F32)


def silu_and_slope(x):
    g = 1.0 / (1.0 + jnp.exp(-x))
    return x * g, g * (1.0 + x * (1.0 - g))


def causal_mask(count):
    rows = lax.broadcasted_iota(jnp.int32, (count, count), 0)
    cols = lax.broadcasted_iota(jnp.int32, (count, count), 1)
    return rows >= cols


def shards(query_rows, key_rows, value_rows, feat_query, feat_key, norm_gain, grad_out):
    tokens, width = query_rows.shape
    heads, size = feat_query.shape[0], feat_query.shape[1]
    near, far = lax.axis_size("near"), lax.axis_size("far")
    full_width = width * lax.axis_size("head")
    chunk = heads * size // near
    slim = chunk // far
    per_head = near // heads
    gain_row = norm_gain.reshape(1, width)
    group = lax.axis_index("far").reshape(1)
    cols = [slice(h * size, (h + 1) * size) for h in range(heads)]

    def put_state(out_ref, h, value, row):
        for part in range(per_head):
            rows = value[part * chunk : (part + 1) * chunk]
            out_ref[h * per_head + part, row : row + chunk, :] = rows.astype(BF)

    def get_state(ref, h):
        parts = [ref[h * per_head + part] for part in range(per_head)]
        return jnp.concatenate(parts, axis=0)

    def state_kernel(k_ref, v_ref, w_ref, kf_ref, out_ref):
        for h, at in enumerate(cols):
            pre = dot(k_ref[:, at], w_ref[h], 1, 0)
            feat = (pre / (1.0 + jnp.exp(-pre))).astype(BF)
            kf_ref[:, at] = feat
            put_state(out_ref, h, dot(feat, v_ref[:, at], 0, 0), 0)

    key_feat, payload = run(
        state_kernel,
        [((tokens, width), BF), ((near, chunk, size), BF)],
        [key_rows, value_rows, feat_key],
    )
    parts = swap(payload, "near")

    def query_kernel(q_ref, wq_ref, k_ref, wk_ref, kf_ref, v_ref, qf_ref, qs_ref, ks_ref, sc_ref, intra_ref):
        mask = causal_mask(tokens)
        for h, at in enumerate(cols):
            act, slope = silu_and_slope(dot(q_ref[:, at], wq_ref[h], 1, 0))
            qs_ref[:, at] = slope
            feat = act.astype(BF)
            qf_ref[:, at] = feat
            ks_ref[:, at] = silu_and_slope(dot(k_ref[:, at], wk_ref[h], 1, 0))[1]
            scores = jnp.where(mask, dot(feat, kf_ref[:, at], 1, 1), 0.0).astype(BF)
            sc_ref[h] = scores
            intra_ref[:, at] = dot(scores, v_ref[:, at], 1, 0)

    query_feat, query_slope, key_slope, scores, intra = run(
        query_kernel,
        [
            ((tokens, width), BF),
            ((tokens, width), F32),
            ((tokens, width), F32),
            ((heads, tokens, tokens), BF),
            ((tokens, width), F32),
        ],
        [query_rows, feat_query, key_rows, feat_key, key_feat, value_rows],
        after=[group],
    )

    def total_kernel(in_ref, out_ref):
        total = in_ref[0].astype(F32)
        for i in range(1, near):
            total = total + in_ref[i].astype(F32)
        total = total.astype(BF)
        for i in range(out_ref.shape[0]):
            out_ref[i] = total

    (payload,) = run(total_kernel, [((far, chunk, size), BF)], [parts], after=[query_feat])
    parts_far = swap(payload, "far")

    def join(parts_ref, far_ref, group_ref, out_ref, backward):
        place = group_ref[0]
        state = jnp.zeros((chunk, size), F32)
        for i in range(far):
            keep = (i > place) if backward else (i < place)
            state = state + jnp.where(keep, far_ref[i][:chunk].astype(F32), 0.0)
        for i in range(near - 1, -1, -1) if backward else range(near):
            out_ref[i] = state.astype(BF)
            state = state + parts_ref[i][:chunk].astype(F32)

    def run_join(kernel, outs, ins):
        whole = pl.BlockSpec(memory_space=pltpu.VMEM)
        return pl.pallas_call(
            kernel,
            out_shape=[jax.ShapeDtypeStruct(shape, dtype) for shape, dtype in outs],
            in_specs=[whole] * (len(ins) - 1) + [pl.BlockSpec(memory_space=pltpu.SMEM)],
            out_specs=[whole] * len(outs),
            compiler_params=pltpu.CompilerParams(vmem_limit_bytes=VMEM_BYTES),
            cost_estimate=pl.CostEstimate(flops=10**6, bytes_accessed=10**6, transcendentals=0),
        )(*ins)

    def prior_kernel(parts_ref, far_ref, group_ref, out_ref):
        join(parts_ref, far_ref, group_ref, out_ref, False)

    (payload,) = run_join(prior_kernel, [((near, chunk, size), BF)], [parts, parts_far, group])
    prior = swap(payload, "near")

    def norm_kernel(qf_ref, p_ref, intra_ref, go_ref, gain_ref, pre_ref, out_ref):
        squares = jnp.zeros((tokens, size), F32)
        inner = jnp.zeros((tokens, size), F32)
        for h, at in enumerate(cols):
            pre = intra_ref[:, at] + dot(qf_ref[:, at], get_state(p_ref, h), 1, 0)
            pre_ref[:, at] = pre
            squares = squares + pre * pre
            inner = inner + go_ref[:, at].astype(F32) * gain_ref[:, at] * pre
        squares = jnp.sum(squares, axis=1, keepdims=True)
        inner = jnp.sum(inner, axis=1, keepdims=True)
        lane = lax.broadcasted_iota(jnp.int32, (tokens, size), 1)
        both = jnp.where(lane == 0, squares, jnp.where(lane == 1, inner, 0.0))
        rows = jnp.transpose(both)[:STAT_ROWS]
        for i in range(out_ref.shape[0]):
            out_ref[i] = rows

    peers = lax.axis_size("head")
    pre_norm, payload = run(
        norm_kernel,
        [((tokens, width), F32), ((peers, STAT_ROWS, tokens), F32)],
        [query_feat, prior, intra, grad_out, gain_row],
    )
    stats = swap(payload, "head")

    def row_factors(st_ref):
        rows = st_ref[0]
        for i in range(1, peers):
            rows = rows + st_ref[i]
        rows = jnp.concatenate([rows, jnp.zeros((size - STAT_ROWS, tokens), F32)], axis=0)
        both = jnp.transpose(rows)
        inverse = 1.0 / jnp.sqrt(both[:, 0:1] / full_width + EPSILON)
        return inverse, both[:, 1:2] * inverse / full_width

    def delta_kernel(
        st_ref, pre_ref, go_ref, gain_ref, qf_ref, v_ref, kf_ref, p_ref, qs_ref, q_ref,
        delta_ref, bs_ref, qg_ref, out_ref,
    ):
        inverse, slope = row_factors(st_ref)
        mask = causal_mask(tokens)
        gains = []
        for h, at in enumerate(cols):
            wide = go_ref[:, at].astype(F32)
            normed = pre_ref[:, at] * inverse
            delta = ((wide * gain_ref[:, at] - normed * slope) * inverse).astype(BF)
            delta_ref[:, at] = delta
            gains.append(jnp.sum(wide * normed, axis=0, keepdims=True))
            put_state(out_ref, h, dot(qf_ref[:, at], delta, 0, 0), 0)
            back = jnp.where(mask, dot(delta, v_ref[:, at], 1, 1), 0.0).astype(BF)
            bs_ref[h] = back
            grad = dot(back, kf_ref[:, at], 1, 0) + dot(delta, get_state(p_ref, h), 1, 1)
            grad = (grad * qs_ref[:, at]).astype(BF)
            qg_ref[:, at] = grad
            put_state(out_ref, h, dot(q_ref[:, at], grad, 0, 0), chunk)
        rest = [jnp.zeros((GAIN_ROWS - heads, size), F32)]
        rows = jnp.concatenate(gains + rest, axis=0).astype(BF)
        for i in range(near):
            out_ref[i, 2 * chunk :, :] = rows

    delta, back_scores, query_pre_grad, payload = run(
        delta_kernel,
        [
            ((tokens, width), BF),
            ((heads, tokens, tokens), BF),
            ((tokens, width), BF),
            ((near, 2 * chunk + GAIN_ROWS, size), BF),
        ],
        [stats, pre_norm, grad_out, gain_row, query_feat, value_rows, key_feat, prior, query_slope, query_rows],
    )
    parts = swap(payload, "near")

    def local_kernel(
        st_ref, pre_ref, gain_ref, qg_ref, wq_ref, bs_ref, qf_ref, sc_ref, delta_ref,
        att_ref, gq_ref, kg_ref, gv_ref,
    ):
        inverse, _ = row_factors(st_ref)
        for h, at in enumerate(cols):
            att_ref[:, at] = (pre_ref[:, at] * inverse * gain_ref[:, at]).astype(BF)
            gq_ref[:, at] = dot(qg_ref[:, at], wq_ref[h], 1, 1).astype(BF)
            kg_ref[:, at] = dot(bs_ref[h], qf_ref[:, at], 0, 0)
            gv_ref[:, at] = dot(sc_ref[h], delta_ref[:, at], 0, 0)

    attended, grad_query, key_grad_local, grad_value_local = run(
        local_kernel,
        [((tokens, width), BF), ((tokens, width), BF), ((tokens, width), F32), ((tokens, width), F32)],
        [stats, pre_norm, gain_row, query_pre_grad, feat_query, back_scores, query_feat, scores, delta],
    )

    def back_total_kernel(in_ref, out_ref):
        total = in_ref[0].astype(F32)
        for i in range(1, near):
            total = total + in_ref[i].astype(F32)
        head_rows, gains = total[:chunk], total[2 * chunk : 2 * chunk + 8]
        for i in range(far):
            part = total[chunk + i * slim : chunk + (i + 1) * slim]
            out_ref[i] = jnp.concatenate([head_rows, part, gains], axis=0).astype(BF)

    (payload,) = run(
        back_total_kernel, [((far, chunk + slim + 8, size), BF)], [parts], after=[grad_query]
    )
    parts_far = swap(payload, "far")

    def later_kernel(parts_ref, far_ref, group_ref, out_ref, side_ref):
        join(parts_ref, far_ref, group_ref, out_ref, True)
        side = far_ref[0].astype(F32)[chunk:]
        for i in range(1, far):
            side = side + far_ref[i].astype(F32)[chunk:]
        side_ref[...] = side

    payload, side = run_join(
        later_kernel,
        [((near, chunk, size), BF), ((slim + 8, size), F32)],
        [parts, parts_far, group],
    )
    grad_gain = side[slim : slim + heads].reshape(width)
    later = swap(payload, "near")

    def key_kernel(kg_ref, v_ref, l_ref, ks_ref, k_ref, kpg_ref, out_ref):
        for h, at in enumerate(cols):
            grad = kg_ref[:, at] + dot(v_ref[:, at], get_state(l_ref, h), 1, 1)
            grad = (grad * ks_ref[:, at]).astype(BF)
            kpg_ref[:, at] = grad
            put_state(out_ref, h, dot(k_ref[:, at], grad, 0, 0), 0)

    key_pre_grad, payload = run(
        key_kernel,
        [((tokens, width), BF), ((near, chunk, size), BF)],
        [key_grad_local, value_rows, later, key_slope, key_rows],
    )
    parts = swap(payload, "near")

    def last_kernel(kpg_ref, wk_ref, gv_ref, kf_ref, l_ref, gk_ref, out_ref):
        for h, at in enumerate(cols):
            gk_ref[:, at] = dot(kpg_ref[:, at], wk_ref[h], 1, 1).astype(BF)
            value = gv_ref[:, at] + dot(kf_ref[:, at], get_state(l_ref, h), 1, 0)
            out_ref[:, at] = value.astype(BF)

    grad_key, grad_value = run(
        last_kernel,
        [((tokens, width), BF), ((tokens, width), BF)],
        [key_pre_grad, feat_key, grad_value_local, key_feat, later],
    )

    def weight_total_kernel(in_ref, side_ref, out_ref):
        total = in_ref[0].astype(F32)
        for i in range(1, near):
            total = total + in_ref[i].astype(F32)
        pad = jnp.zeros((8, size), F32)
        total = jnp.concatenate([total, side_ref[:slim], pad], axis=0).astype(BF)
        for i in range(far):
            out_ref[i] = total

    (payload,) = run(
        weight_total_kernel,
        [((far, chunk + slim + 8, size), BF)],
        [parts, side],
        after=[grad_key],
    )
    parts_far = swap(payload, "far")

    def weight_kernel(far_ref, out_ref):
        total = far_ref[0].astype(F32)[:chunk]
        for i in range(1, far):
            total = total + far_ref[i].astype(F32)[:chunk]
        queries = [far_ref[i].astype(F32)[chunk : chunk + slim] for i in range(far)]
        total = jnp.concatenate([total] + queries, axis=0).astype(BF)
        for i in range(near):
            out_ref[i] = total

    (payload,) = run(weight_kernel, [((near, 2 * chunk, size), BF)], [parts_far])
    done = swap(payload, "near")

    def widen_kernel(in_ref, gq_ref, gk_ref):
        for h in range(heads):
            for part in range(per_head):
                rows = slice(part * chunk, (part + 1) * chunk)
                gk_ref[h, rows] = in_ref[h * per_head + part, :chunk].astype(F32)
                gq_ref[h, rows] = in_ref[h * per_head + part, chunk:].astype(F32)

    grad_feat_query, grad_feat_key = run(
        widen_kernel, [(feat_query.shape, F32), (feat_key.shape, F32)], [done]
    )
    return (attended, grad_query, grad_key, grad_value, grad_feat_query, grad_feat_key, grad_gain)


def solution(mesh):
    seq, head = mesh.devices.shape
    split = Mesh(mesh.devices.reshape(seq // NEAR, NEAR, head), ("far", "near", "head"))
    wide = P(("far", "near"), "head")
    per_head = P("head", None, None)
    in_specs = (wide, wide, wide, per_head, per_head, P("head"), wide)
    out_specs = (wide, wide, wide, wide, per_head, per_head, P("head"))
    return jax.shard_map(shards, mesh=split, in_specs=in_specs, out_specs=out_specs, check_vma=False)
```

time: 738 us -> 155 us (0.21)
  waiting for transfers between devices: 477 us -> 16.4 us
  blocking collectives: 161 us -> 94.9 us
  other arithmetic: 61.2 us -> 0 us
  starting transfers between devices: 0.12 us -> 16.1 us
  matrix products: 14.3 us -> 0 us
  between operations: 13.9 us -> 0.78 us
  Pallas kernels: 0 us -> 10.5 us
  local copies, waits for them, and re-layouts: 8.1 us -> 15.5 us
    all_gather x2 -> x0, waiting for transfers between devices: 365 us -> none  [prefix(): gathered = lax.all_gather(x.astype(jnp.bfloat16), axis)]
    psum x3 -> x0, blocking collectives: 161 us -> none  [the longest x1 139 us: shards(): lax.psum((query_weight_part, key_weight_part, gain_local), 'seq')]
    psum x1 -> x0, waiting for transfers between devices: 112 us -> none  [shards(): lax.psum((query_weight_part, key_weight_part, gain_local), 'seq')]
    all_to_all x0 -> x6, blocking collectives: none -> 94.9 us  [swap(): return lax.all_to_all(x, axis, 0, 0)]
    add x63 -> x0, other arithmetic: 60.7 us -> none  [add_states(): return earlier + latter]
    all_to_all x0 -> x4, waiting for transfers between devices: none -> 16.4 us  [swap(): return lax.all_to_all(x, axis, 0, 0)]
    all_to_all x0 -> x4, starting transfers between devices: none -> 16.1 us  [swap(): return lax.all_to_all(x, axis, 0, 0)]
    dot_general x18 -> x0, matrix products: 14.3 us -> none  [the longest x2 4.31 us: featurize(): jnp.einsum('thd,hde->the', block, weights, preferred_element_type=jnp.flo...]
  transfers between devices with their start and end apart: 3 -> 4, of which waited for: 3 -> 4; matrix products, arithmetic and copies ran while one was open for 2% -> 0% of each run, Pallas kernels for 0% -> 2%
where the time goes in v2:
time: 155 us; the launch traced here: 154 us
  blocking collectives  94.9 us (61%)
  waiting for transfers between devices  16.4 us (11%)
  starting transfers between devices  16.1 us (10%)
  local copies, waits for them, and re-layouts  15.5 us (10%)
  Pallas kernels  10.5 us (7%)
    all_to_all x6, blocking collectives, swap(): return lax.all_to_all(x, axis, 0, 0)  94.9 us
    all_to_all x4, waiting for transfers between devices, swap(): return lax.all_to_all(x, axis, 0, 0)  16.4 us
    all_to_all x4, starting transfers between devices, swap(): return lax.all_to_all(x, axis, 0, 0)  16.1 us
    unnamed x50, local copies, waits for them, and re-layouts  14.9 us
    pallas_call x12, Pallas kernels, run(): pl.pallas_call(body, out_shape=[jax.ShapeDtypeStruct(shape, dtype) for sh...  10.4 us
  transfers between devices with their start and end apart: 4, of which 4 were waited for; matrix products, arithmetic and copies ran while one was open for 0% of the time, Pallas kernels for 2%

profile of v2, /device:TPU:8, one launch (start us, length us, event | category | flops | bytes accessed | tf_op | source)
XLA Modules:
  0.0 154.1 jit_solution(18404776687384122091)
XLA Ops:
  0.6 0.0 copy-start
  0.6 0.9 copy-done
  1.6 0.9 copy-done.2
  2.5 0.9 copy-done.4
  3.4 1.1 shard_map.126
  4.6 5.8 %all-to-all-start = ((bf16[8,64,128]{2,1,0:T(8,128)(2,1)}), bf16[8,64,128]{2,1,0:T(8,128)(2,1)S(1)}, u32[]{:S(2)}, u32[]{:S(2)}) async-start(bf16[8,64,128]{2,1,0:T(8,128)(2,1)} %get-tuple-element.34), calls=%async_computation | async-start | bytes 262144 | tf_op jit(solution)/shard_map/all_to_all | solution.py:18
  10.4 0.0 copy-done.3
  10.4 0.0 copy-done.5
  10.4 0.0 copy-done.6
  10.4 0.0 copy-done.1
  10.4 0.0 copy-start.8
  10.4 0.9 copy-done.8
  11.3 1.1 shard_map.127
  12.5 0.8 copy-done.12
  13.2 0.8 copy-done.14
  14.1 2.9 %all-to-all-done.refs_0_.parts_ref = bf16[8,64,128]{2,1,0:T(8,128)(2,1)S(1)} async-done(((bf16[8,64,128]{2,1,0:T(8,128)(2,1)}), bf16[8,64,128]{2,1,0:T(8,128)(2,1)S(1)}, u32[]{:S(2)}, u32[]{:S(2)}) %all-to-all-start) | async-done | bytes 131104 | tf_op jit(solution)/shard_map/all_to_all | solution.py:18
  17.0 27.8 %all_to_all.50.far_ref = bf16[8,64,128]{2,1,0:T(8,128)(2,1)S(1)} all-to-all(bf16[8,64,128]{2,1,0:T(8,128)(2,1)S(1)} %shard_map.128), channel_id=1, replica_groups=mesh['far'=8,'near'=8,'head'=8] {'far'}, dimensions={0} | all-to-all | bytes 262144 | tf_op jit(solution)/shard_map/all_to_all | solution.py:18
  44.8 10.6 %all_to_all.51.refs_1_.refs_7_ = bf16[8,64,128]{2,1,0:T(8,128)(2,1)S(1)} all-to-all(bf16[8,64,128]{2,1,0:T(8,128)(2,1)S(1)} %shard_map.129), channel_id=1, replica_groups=mesh['far'=8,'near'=8,'head'=8] {'near'}, dimensions={0} | all-to-all | bytes 262144 | tf_op jit(solution)/shard_map/all_to_all | solution.py:18
  55.4 0.7 copy-done.24
  56.1 0.4 shard_map.130
  56.4 8.9 %all_to_all.52.refs_0_ = f32[8,8,256]{2,1,0:T(8,128)S(1)} all-to-all(f32[8,8,256]{2,1,0:T(8,128)S(1)} %get-tuple-element.36), channel_id=1, replica_groups=mesh['far'=8,'near'=8,'head'=8] {'head'}, dimensions={0} | all-to-all | bytes 131072 | tf_op jit(solution)/shard_map/all_to_all | solution.py:18
  65.3 2.4 %shard_map.131 = (bf16[256,512]{1,0:T(8,128)(2,1)S(1)}, bf16[4,256,256]{2,1,0:T(8,128)(2,1)S(1)}, bf16[256,512]{1,0:T(8,128)(2,1)S(1)}, bf16[8,144,128]{2,1,0:T(8,128)(2,1)}) custom-call(f32[8,8,256]{2,1,0:T(8,128)S(1)} %all_to_all.52.refs_0_, f32[256,512]{1,0:T(8,128)S(1)} %get-tuple-element.37.refs_1_, bf16[256,512]{1,0:T(8,128)(2,1)S(1)} %copy-done.7, ...), custom_call_target="tpu_custom_call" | custom-call | flops 100000000 | bytes 1000000 | tf_op jit(solution)/shard_map/pallas_call | solution.py:28
  67.8 0.8 copy-done.16
  68.6 0.7 copy-done.18
  69.3 0.7 copy-done.20
  70.0 3.6 %all-to-all-start.4 = ((bf16[8,144,128]{2,1,0:T(8,128)(2,1)}), bf16[8,144,128]{2,1,0:T(8,128)(2,1)S(1)}, u32[]{:S(2)}, u32[]{:S(2)}) async-start(bf16[8,144,128]{2,1,0:T(8,128)(2,1)} %get-tuple-element.46), calls=%async_computation.4 | async-start | bytes 589824 | tf_op jit(solution)/shard_map/all_to_all | solution.py:18
  73.6 1.0 copy-done.13
  74.6 1.0 copy-done.17
  75.6 0.9 copy-done.19
  76.6 0.9 copy-done.21
  77.5 1.3 shard_map.132
  78.9 0.8 copy-done.10
  79.6 1.5 all-to-all-done.4.refs_0_.parts_ref
  81.2 0.9 copy-done.23
  82.2 19.2 %all_to_all.53.far_ref = bf16[8,80,128]{2,1,0:T(8,128)(2,1)S(1)} all-to-all(bf16[8,80,128]{2,1,0:T(8,128)(2,1)S(1)} %shard_map.133), channel_id=1, replica_groups=mesh['far'=8,'near'=8,'head'=8] {'far'}, dimensions={0} | all-to-all | bytes 327680 | tf_op jit(solution)/shard_map/all_to_all | solution.py:18
  101.4 0.1 shard_map.134
  101.5 10.6 %all_to_all.54.refs_2_.refs_4_ = bf16[8,64,128]{2,1,0:T(8,128)(2,1)S(1)} all-to-all(bf16[8,64,128]{2,1,0:T(8,128)(2,1)S(1)} %get-tuple-element.47), channel_id=1, replica_groups=mesh['far'=8,'near'=8,'head'=8] {'near'}, dimensions={0} | all-to-all | bytes 262144 | tf_op jit(solution)/shard_map/all_to_all | solution.py:18
  112.1 1.2 shard_map.135
  113.4 3.4 %all-to-all-start.7 = ((bf16[8,64,128]{2,1,0:T(8,128)(2,1)}), bf16[8,64,128]{2,1,0:T(8,128)(2,1)S(1)}, u32[]{:S(2)}, u32[]{:S(2)}) async-start(bf16[8,64,128]{2,1,0:T(8,128)(2,1)} %get-tuple-element.53), calls=%async_computation.7 | async-start | bytes 262144 | tf_op jit(solution)/shard_map/all_to_all | solution.py:18
  116.7 1.1 shard_map.136
  117.8 5.5 %all-to-all-done.7.refs_0_ = bf16[8,64,128]{2,1,0:T(8,128)(2,1)S(1)} async-done(((bf16[8,64,128]{2,1,0:T(8,128)(2,1)}), bf16[8,64,128]{2,1,0:T(8,128)(2,1)S(1)}, u32[]{:S(2)}, u32[]{:S(2)}) %all-to-all-start.7) | async-done | bytes 131104 | tf_op jit(solution)/shard_map/all_to_all | solution.py:18
  123.3 0.9 copy-done.22
  124.2 17.8 %all_to_all.55.refs_0_ = bf16[8,80,128]{2,1,0:T(8,128)(2,1)S(1)} all-to-all(bf16[8,80,128]{2,1,0:T(8,128)(2,1)S(1)} %shard_map.137), channel_id=1, replica_groups=mesh['far'=8,'near'=8,'head'=8] {'far'}, dimensions={0} | all-to-all | bytes 327680 | tf_op jit(solution)/shard_map/all_to_all | solution.py:18
  142.0 0.7 shard_map.138
  142.7 3.4 %all-to-all-start.9 = ((bf16[8,128,128]{2,1,0:T(8,128)(2,1)}), bf16[8,128,128]{2,1,0:T(8,128)(2,1)S(1)}, u32[]{:S(2)}, u32[]{:S(2)}) async-start(bf16[8,128,128]{2,1,0:T(8,128)(2,1)} %shard_map.138), calls=%async_computation.9 | async-start | bytes 524288 | tf_op jit(solution)/shard_map/all_to_all | solution.py:18
  146.2 0.6 slice_bitcast_fusion
  146.7 6.6 %all-to-all-done.9.refs_0_ = bf16[8,128,128]{2,1,0:T(8,128)(2,1)S(1)} async-done(((bf16[8,128,128]{2,1,0:T(8,128)(2,1)}), bf16[8,128,128]{2,1,0:T(8,128)(2,1)S(1)}, u32[]{:S(2)}, u32[]{:S(2)}) %all-to-all-start.9) | async-done | bytes 262176 | tf_op jit(solution)/shard_map/all_to_all | solution.py:18
  153.3 0.8 shard_map.139
  (31 shorter events, 0.2 us)
Async XLA Ops:
  0.6 1.0 copy-start
  1.6 0.9 copy-start.2
  2.5 0.9 copy-start.4
  3.4 6.9 %copy-start.3 = (bf16[256,512]{1,0:T(8,128)(2,1)S(1)}, bf16[256,512]{1,0:T(8,128)(2,1)}, u32[]{:S(2)}) copy-start(bf16[256,512]{1,0:T(8,128)(2,1)} %refs_4_.3) | copy-start | bytes 786436
  3.4 6.9 %copy-start.5 = (bf16[4,128,128]{2,1,0:T(8,128)(2,1)S(1)}, bf16[4,128,128]{2,1,0:T(8,128)(2,1)}, u32[]{:S(2)}) copy-start(bf16[4,128,128]{2,1,0:T(8,128)(2,1)} %refs_1_.7) | copy-start | bytes 393220
  3.4 6.9 %copy-start.6 = (bf16[256,512]{1,0:T(8,128)(2,1)S(1)}, bf16[256,512]{1,0:T(8,128)(2,1)}, u32[]{:S(2)}) copy-start(bf16[256,512]{1,0:T(8,128)(2,1)} %refs_9_.1) | copy-start | bytes 786436
  4.6 5.8 %copy-start.1 = (bf16[256,512]{1,0:T(8,128)(2,1)S(1)}, bf16[256,512]{1,0:T(8,128)(2,1)}, u32[]{:S(2)}) copy-start(bf16[256,512]{1,0:T(8,128)(2,1)} %refs_1_.6) | copy-start | bytes 786436
  4.6 12.4 %all-to-all-start = ((bf16[8,64,128]{2,1,0:T(8,128)(2,1)}), bf16[8,64,128]{2,1,0:T(8,128)(2,1)S(1)}, u32[]{:S(2)}, u32[]{:S(2)}) async-start(bf16[8,64,128]{2,1,0:T(8,128)(2,1)} %get-tuple-element.34), calls=%async_computation | async-start | bytes 262144 | tf_op jit(solution)/shard_map/all_to_all | solution.py:18
  10.4 0.9 copy-start.8
  12.5 0.8 copy-start.12
  13.2 0.8 copy-start.14
  44.7 10.6 %copy-start.7 = (bf16[256,512]{1,0:T(8,128)(2,1)S(1)}, bf16[256,512]{1,0:T(8,128)(2,1)}, u32[]{:S(2)}) copy-start(bf16[256,512]{1,0:T(8,128)(2,1)} %refs_2_.5) | copy-start | bytes 786436
  55.4 0.7 copy-start.24
  56.1 9.3 %copy-start.15 = (f32[256,512]{1,0:T(8,128)S(1)}, f32[256,512]{1,0:T(8,128)}, u32[]{:S(2)}) copy-start(f32[256,512]{1,0:T(8,128)} %copy-done.14) | copy-start | bytes 1572868
  67.8 0.8 copy-start.16
  68.6 0.7 copy-start.18
  69.3 0.7 copy-start.20
  70.0 3.6 %copy-start.9 = (bf16[4,128,128]{2,1,0:T(8,128)(2,1)S(1)}, bf16[4,128,128]{2,1,0:T(8,128)(2,1)}, u32[]{:S(2)}) copy-start(bf16[4,128,128]{2,1,0:T(8,128)(2,1)} %refs_4_.2) | copy-start | bytes 393220
  70.0 11.2 %all-to-all-start.4 = ((bf16[8,144,128]{2,1,0:T(8,128)(2,1)}), bf16[8,144,128]{2,1,0:T(8,128)(2,1)S(1)}, u32[]{:S(2)}, u32[]{:S(2)}) async-start(bf16[8,144,128]{2,1,0:T(8,128)(2,1)} %get-tuple-element.46), calls=%async_computation.4 | async-start | bytes 589824 | tf_op jit(solution)/shard_map/all_to_all | solution.py:18
  73.6 1.0 copy-start.13
  74.6 1.0 copy-start.17
  75.6 0.9 copy-start.19
  76.6 0.9 copy-start.21
  78.9 0.8 copy-start.10
  81.2 1.0 copy-start.23
  82.2 29.9 %copy-start.11 = (f32[256,512]{1,0:T(8,128)S(1)}, f32[256,512]{1,0:T(8,128)}, u32[]{:S(2)}) copy-start(f32[256,512]{1,0:T(8,128)} %copy-done.10) | copy-start | bytes 1572868
  113.4 9.9 %all-to-all-start.7 = ((bf16[8,64,128]{2,1,0:T(8,128)(2,1)}), bf16[8,64,128]{2,1,0:T(8,128)(2,1)S(1)}, u32[]{:S(2)}, u32[]{:S(2)}) async-start(bf16[8,64,128]{2,1,0:T(8,128)(2,1)} %get-tuple-element.53), calls=%async_computation.7 | async-start | bytes 262144 | tf_op jit(solution)/shard_map/all_to_all | solution.py:18
  123.3 1.0 copy-start.22
  142.7 10.6 %all-to-all-start.9 = ((bf16[8,128,128]{2,1,0:T(8,128)(2,1)}), bf16[8,128,128]{2,1,0:T(8,128)(2,1)S(1)}, u32[]{:S(2)}, u32[]{:S(2)}) async-start(bf16[8,128,128]{2,1,0:T(8,128)(2,1)} %shard_map.138), calls=%async_computation.9 | async-start | bytes 524288 | tf_op jit(solution)/shard_map/all_to_all | solution.py:18

commit v3 on v2

--- a/solution.py
+++ b/solution.py
@@ -11,37 +11,52 @@
 NEAR = 8
 GAIN_ROWS = 16
 STAT_ROWS = 8
+TOKEN = ((8, 128), F32)
 VMEM_BYTES = 24 * 1024 * 1024
+WHOLE_VMEM = 64 * 1024 * 1024
 
 
 def swap(x, axis):
     return lax.all_to_all(x, axis, 0, 0)
 
 
-def run(kernel, outs, ins, after=(), flops=10**8):
-    count = len(ins)
+def run(kernel, outs, ins, after=(), fetch=(), limit=VMEM_BYTES):
+    count, copies = len(ins), len(fetch)
 
     def body(*refs):
-        kernel(*refs[:count], *refs[count + len(after) :])
+        sources = refs[count : count + copies]
+        outputs = refs[count + copies + len(after) : count + copies + len(after) + len(outs)]
+        if not copies:
+            return kernel(*refs[:count], *outputs)
+        held, sems = refs[-copies - 1 : -1], refs[-1]
+        moves = [pltpu.make_async_copy(sources[i], held[i], sems.at[i]) for i in range(copies)]
+        for move in moves:
+            move.start()
+        return kernel(*refs[:count], *held, *outputs, [move.wait for move in moves])
 
     whole = pl.BlockSpec(memory_space=pltpu.VMEM)
+    far_off = pl.BlockSpec(memory_space=pl.ANY)
+    scratch = [pltpu.VMEM(x.shape, x.dtype) for x in fetch]
     return pl.pallas_call(
         body,
         out_shape=[jax.ShapeDtypeStruct(shape, dtype) for shape, dtype in outs],
-        in_specs=[whole] * count + [pl.BlockSpec(memory_space=pl.ANY)] * len(after),
+        in_specs=[whole] * count
+        + [far_off] * copies
+        + [far_off] * len(after),
         out_specs=[whole] * len(outs),
-        compiler_params=pltpu.CompilerParams(vmem_limit_bytes=VMEM_BYTES),
-        cost_estimate=pl.CostEstimate(flops=flops, bytes_accessed=10**6, transcendentals=0),
-    )(*ins, *after)
+        scratch_shapes=scratch + [pltpu.SemaphoreType.DMA((copies,))] if copies else [],
+        compiler_params=pltpu.CompilerParams(vmem_limit_bytes=limit),
+        cost_estimate=pl.CostEstimate(flops=10**8, bytes_accessed=10**6, transcendentals=0),
+    )(*ins, *fetch, *after)
 
 
 def dot(a, b, over_a, over_b):
     return lax.dot_general(a, b, (((over_a,), (over_b,)), ((), ())), preferred_element_type=F32)
 
 
-def silu_and_slope(x):
+def silu_slope(x):
     g = 1.0 / (1.0 + jnp.exp(-x))
-    return x * g, g * (1.0 + x * (1.0 - g))
+    return g * (1.0 + x * (1.0 - g))
 
 
 def causal_mask(count):
@@ -71,42 +86,39 @@
         parts = [ref[h * per_head + part] for part in range(per_head)]
         return jnp.concatenate(parts, axis=0)
 
-    def state_kernel(k_ref, v_ref, w_ref, kf_ref, out_ref):
+    def state_kernel(w_ref, k_ref, v_ref, kf_ref, out_ref, waits):
+        waits[0]()
+        waits[1]()
         for h, at in enumerate(cols):
             pre = dot(k_ref[:, at], w_ref[h], 1, 0)
-            feat = (pre / (1.0 + jnp.exp(-pre))).astype(BF)
-            kf_ref[:, at] = feat
-            put_state(out_ref, h, dot(feat, v_ref[:, at], 0, 0), 0)
+            kf_ref[:, at] = (pre / (1.0 + jnp.exp(-pre))).astype(BF)
+        waits[2]()
+        for h, at in enumerate(cols):
+            put_state(out_ref, h, dot(kf_ref[:, at], v_ref[:, at], 0, 0), 0)
 
     key_feat, payload = run(
         state_kernel,
         [((tokens, width), BF), ((near, chunk, size), BF)],
-        [key_rows, value_rows, feat_key],
+        [],
+        fetch=[feat_key, key_rows, value_rows],
+        limit=WHOLE_VMEM,
     )
     parts = swap(payload, "near")
 
-    def query_kernel(q_ref, wq_ref, k_ref, wk_ref, kf_ref, v_ref, qf_ref, qs_ref, ks_ref, sc_ref, intra_ref):
+    def query_kernel(kf_ref, wq_ref, q_ref, v_ref, gain_ref, qf_ref, intra_ref, gain_out):
+        gain_out[...] = gain_ref[...]
         mask = causal_mask(tokens)
         for h, at in enumerate(cols):
-            act, slope = silu_and_slope(dot(q_ref[:, at], wq_ref[h], 1, 0))
-            qs_ref[:, at] = slope
-            feat = act.astype(BF)
+            pre = dot(q_ref[:, at], wq_ref[h], 1, 0)
+            feat = (pre / (1.0 + jnp.exp(-pre))).astype(BF)
             qf_ref[:, at] = feat
-            ks_ref[:, at] = silu_and_slope(dot(k_ref[:, at], wk_ref[h], 1, 0))[1]
             scores = jnp.where(mask, dot(feat, kf_ref[:, at], 1, 1), 0.0).astype(BF)
-            sc_ref[h] = scores
             intra_ref[:, at] = dot(scores, v_ref[:, at], 1, 0)
 
-    query_feat, query_slope, key_slope, scores, intra = run(
+    query_feat, intra, gain_row = run(
         query_kernel,
-        [
-            ((tokens, width), BF),
-            ((tokens, width), F32),
-            ((tokens, width), F32),
-            ((heads, tokens, tokens), BF),
-            ((tokens, width), F32),
-        ],
-        [query_rows, feat_query, key_rows, feat_key, key_feat, value_rows],
+        [((tokens, width), BF), ((tokens, width), F32), ((1, width), F32)],
+        [key_feat, feat_query, query_rows, value_rows, gain_row],
         after=[group],
     )
 
@@ -181,58 +193,58 @@
         inverse = 1.0 / jnp.sqrt(both[:, 0:1] / full_width + EPSILON)
         return inverse, both[:, 1:2] * inverse / full_width
 
-    def delta_kernel(
-        st_ref, pre_ref, go_ref, gain_ref, qf_ref, v_ref, kf_ref, p_ref, qs_ref, q_ref,
-        delta_ref, bs_ref, qg_ref, out_ref,
-    ):
+    def delta_of(at, inverse, slope, pre_ref, go_ref, gain_ref):
+        normed = pre_ref[:, at] * inverse
+        wide = go_ref[:, at].astype(F32)
+        return ((wide * gain_ref[:, at] - normed * slope) * inverse).astype(BF), wide, normed
+
+    def query_side(h, at, delta, mask, v_ref, kf_ref, p_ref, q_ref, wq_ref):
+        back = jnp.where(mask, dot(delta, v_ref[:, at], 1, 1), 0.0).astype(BF)
+        grad = dot(back, kf_ref[:, at], 1, 0) + dot(delta, get_state(p_ref, h), 1, 1)
+        return back, (grad * silu_slope(dot(q_ref[:, at], wq_ref[h], 1, 0))).astype(BF)
+
+    def delta_kernel(st_ref, pre_ref, go_ref, gain_ref, qf_ref, v_ref, kf_ref, p_ref, q_ref, wq_ref, out_ref):
         inverse, slope = row_factors(st_ref)
         mask = causal_mask(tokens)
         gains = []
         for h, at in enumerate(cols):
-            wide = go_ref[:, at].astype(F32)
-            normed = pre_ref[:, at] * inverse
-            delta = ((wide * gain_ref[:, at] - normed * slope) * inverse).astype(BF)
-            delta_ref[:, at] = delta
+            delta, wide, normed = delta_of(at, inverse, slope, pre_ref, go_ref, gain_ref)
             gains.append(jnp.sum(wide * normed, axis=0, keepdims=True))
             put_state(out_ref, h, dot(qf_ref[:, at], delta, 0, 0), 0)
-            back = jnp.where(mask, dot(delta, v_ref[:, at], 1, 1), 0.0).astype(BF)
-            bs_ref[h] = back
-            grad = dot(back, kf_ref[:, at], 1, 0) + dot(delta, get_state(p_ref, h), 1, 1)
-            grad = (grad * qs_ref[:, at]).astype(BF)
-            qg_ref[:, at] = grad
+            _, grad = query_side(h, at, delta, mask, v_ref, kf_ref, p_ref, q_ref, wq_ref)
             put_state(out_ref, h, dot(q_ref[:, at], grad, 0, 0), chunk)
         rest = [jnp.zeros((GAIN_ROWS - heads, size), F32)]
         rows = jnp.concatenate(gains + rest, axis=0).astype(BF)
         for i in range(near):
             out_ref[i, 2 * chunk :, :] = rows
 
-    delta, back_scores, query_pre_grad, payload = run(
+    (payload,) = run(
         delta_kernel,
-        [
-            ((tokens, width), BF),
-            ((heads, tokens, tokens), BF),
-            ((tokens, width), BF),
-            ((near, 2 * chunk + GAIN_ROWS, size), BF),
-        ],
-        [stats, pre_norm, grad_out, gain_row, query_feat, value_rows, key_feat, prior, query_slope, query_rows],
+        [((near, 2 * chunk + GAIN_ROWS, size), BF)],
+        [stats, pre_norm, grad_out, gain_row, query_feat, value_rows, key_feat, prior, query_rows, feat_query],
     )
     parts = swap(payload, "near")
 
     def local_kernel(
-        st_ref, pre_ref, gain_ref, qg_ref, wq_ref, bs_ref, qf_ref, sc_ref, delta_ref,
-        att_ref, gq_ref, kg_ref, gv_ref,
+        st_ref, pre_ref, go_ref, gain_ref, qf_ref, v_ref, kf_ref, p_ref, q_ref, wq_ref,
+        att_ref, gq_ref, kg_ref, gv_ref, token_ref,
     ):
-        inverse, _ = row_factors(st_ref)
-        for h, at in enumerate(cols):
-            att_ref[:, at] = (pre_ref[:, at] * inverse * gain_ref[:, at]).astype(BF)
-            gq_ref[:, at] = dot(qg_ref[:, at], wq_ref[h], 1, 1).astype(BF)
-            kg_ref[:, at] = dot(bs_ref[h], qf_ref[:, at], 0, 0)
-            gv_ref[:, at] = dot(sc_ref[h], delta_ref[:, at], 0, 0)
-
-    attended, grad_query, key_grad_local, grad_value_local = run(
+        token_ref[...] = jnp.zeros(token_ref.shape, F32)
+        inverse, slope = row_factors(st_ref)
+        mask = causal_mask(tokens)
+        for h, at in enumerate(cols):
+            delta, _, normed = delta_of(at, inverse, slope, pre_ref, go_ref, gain_ref)
+            att_ref[:, at] = (normed * gain_ref[:, at]).astype(BF)
+            back, grad = query_side(h, at, delta, mask, v_ref, kf_ref, p_ref, q_ref, wq_ref)
+            gq_ref[:, at] = dot(grad, wq_ref[h], 1, 1).astype(BF)
+            kg_ref[:, at] = dot(back, qf_ref[:, at], 0, 0)
+            scores = jnp.where(mask, dot(qf_ref[:, at], kf_ref[:, at], 1, 1), 0.0).astype(BF)
+            gv_ref[:, at] = dot(scores, delta, 0, 0)
+
+    attended, grad_query, key_grad_local, grad_value_local, token = run(
         local_kernel,
-        [((tokens, width), BF), ((tokens, width), BF), ((tokens, width), F32), ((tokens, width), F32)],
-        [stats, pre_norm, gain_row, query_pre_grad, feat_query, back_scores, query_feat, scores, delta],
+        [((tokens, width), BF)] * 2 + [((tokens, width), F32)] * 2 + [TOKEN],
+        [stats, pre_norm, grad_out, gain_row, query_feat, value_rows, key_feat, prior, query_rows, feat_query],
     )
 
     def back_total_kernel(in_ref, out_ref):
@@ -245,48 +257,51 @@
             out_ref[i] = jnp.concatenate([head_rows, part, gains], axis=0).astype(BF)
 
     (payload,) = run(
-        back_total_kernel, [((far, chunk + slim + 8, size), BF)], [parts], after=[grad_query]
+        back_total_kernel, [((far, chunk + slim + 8, size), BF)], [parts], after=[token]
     )
     parts_far = swap(payload, "far")
 
-    def later_kernel(parts_ref, far_ref, group_ref, out_ref, side_ref):
+    def later_kernel(parts_ref, far_ref, group_ref, out_ref, side_ref, gain_ref):
         join(parts_ref, far_ref, group_ref, out_ref, True)
         side = far_ref[0].astype(F32)[chunk:]
         for i in range(1, far):
             side = side + far_ref[i].astype(F32)[chunk:]
         side_ref[...] = side
-
-    payload, side = run_join(
+        for h, at in enumerate(cols):
+            gain_ref[:, at] = side[slim + h : slim + h + 1]
+
+    payload, side, gain_sum = run_join(
         later_kernel,
-        [((near, chunk, size), BF), ((slim + 8, size), F32)],
+        [((near, chunk, size), BF), ((slim + 8, size), F32), ((1, width), F32)],
         [parts, parts_far, group],
     )
-    grad_gain = side[slim : slim + heads].reshape(width)
+    grad_gain = gain_sum.reshape(width)
     later = swap(payload, "near")
 
-    def key_kernel(kg_ref, v_ref, l_ref, ks_ref, k_ref, kpg_ref, out_ref):
+    def key_kernel(kg_ref, v_ref, l_ref, wk_ref, k_ref, kpg_ref, out_ref):
         for h, at in enumerate(cols):
             grad = kg_ref[:, at] + dot(v_ref[:, at], get_state(l_ref, h), 1, 1)
-            grad = (grad * ks_ref[:, at]).astype(BF)
+            grad = (grad * silu_slope(dot(k_ref[:, at], wk_ref[h], 1, 0))).astype(BF)
             kpg_ref[:, at] = grad
             put_state(out_ref, h, dot(k_ref[:, at], grad, 0, 0), 0)
 
     key_pre_grad, payload = run(
         key_kernel,
         [((tokens, width), BF), ((near, chunk, size), BF)],
-        [key_grad_local, value_rows, later, key_slope, key_rows],
+        [key_grad_local, value_rows, later, feat_key, key_rows],
     )
     parts = swap(payload, "near")
 
-    def last_kernel(kpg_ref, wk_ref, gv_ref, kf_ref, l_ref, gk_ref, out_ref):
+    def last_kernel(kpg_ref, wk_ref, gv_ref, kf_ref, l_ref, gk_ref, out_ref, token_ref):
+        token_ref[...] = jnp.zeros(token_ref.shape, F32)
         for h, at in enumerate(cols):
             gk_ref[:, at] = dot(kpg_ref[:, at], wk_ref[h], 1, 1).astype(BF)
             value = gv_ref[:, at] + dot(kf_ref[:, at], get_state(l_ref, h), 1, 0)
             out_ref[:, at] = value.astype(BF)
 
-    grad_key, grad_value = run(
+    grad_key, grad_value, token = run(
         last_kernel,
-        [((tokens, width), BF), ((tokens, width), BF)],
+        [((tokens, width), BF), ((tokens, width), BF), TOKEN],
         [key_pre_grad, feat_key, grad_value_local, key_feat, later],
     )
 
@@ -303,7 +318,7 @@
         weight_total_kernel,
         [((far, chunk + slim + 8, size), BF)],
         [parts, side],
-        after=[grad_key],
+        after=[token, grad_gain],
     )
     parts_far = swap(payload, "far")
 

time: 155 us -> 148 us (0.955)
  local copies, waits for them, and re-layouts: 15.5 us -> 4.18 us
  blocking collectives: 94.9 us -> 104 us
  waiting for transfers between devices: 16.4 us -> 12 us
  starting transfers between devices: 16.1 us -> 12.6 us
  Pallas kernels: 10.5 us -> 13.8 us
    unnamed x50 -> x24, local copies, waits for them, and re-layouts: 14.9 us -> 4.18 us
    all_to_all x6 -> x7, blocking collectives: 94.9 us -> 104 us  [swap(): return lax.all_to_all(x, axis, 0, 0)]
    all_to_all x4 -> x3, waiting for transfers between devices: 16.4 us -> 12 us  [swap(): return lax.all_to_all(x, axis, 0, 0)]
    all_to_all x4 -> x3, starting transfers between devices: 16.1 us -> 12.6 us  [swap(): return lax.all_to_all(x, axis, 0, 0)]
    pallas_call x12, Pallas kernels: 10.4 us -> 13.2 us  [run(): pl.pallas_call(body, out_shape=[jax.ShapeDtypeStruct(shape, dtype) for sh...]
  transfers between devices with their start and end apart: 4 -> 3, of which waited for: 4 -> 3; matrix products, arithmetic and copies ran while one was open for 0% -> 0% of each run, Pallas kernels for 2% -> 4%
where the time goes in v3:
time: 148 us; the launch traced here: 147 us
  blocking collectives  104 us (70%)
  Pallas kernels  13.8 us (9%)
  starting transfers between devices  12.6 us (9%)
  waiting for transfers between devices  12 us (8%)
  local copies, waits for them, and re-layouts  4.18 us (3%)
    all_to_all x7, blocking collectives, swap(): return lax.all_to_all(x, axis, 0, 0)  104 us
    pallas_call x12, Pallas kernels, run(): pl.pallas_call(body, out_shape=[jax.ShapeDtypeStruct(shape, dtype) for sh...  13.2 us
    all_to_all x3, starting transfers between devices, swap(): return lax.all_to_all(x, axis, 0, 0)  12.6 us
    all_to_all x3, waiting for transfers between devices, swap(): return lax.all_to_all(x, axis, 0, 0)  12 us
    unnamed x24, local copies, waits for them, and re-layouts  4.18 us
  transfers between devices with their start and end apart: 3, of which 3 were waited for; matrix products, arithmetic and copies ran while one was open for 0% of the time, Pallas kernels for 4%

profile of v3, /device:TPU:8, one launch (start us, length us, event | category | flops | bytes accessed | tf_op | source)
XLA Modules:
  0.0 147.3 jit_solution(1500223370659439201)
XLA Ops:
  0.6 2.3 %shard_map.126 = (bf16[256,512]{1,0:T(8,128)(2,1)}, bf16[8,64,128]{2,1,0:T(8,128)(2,1)}) custom-call(bf16[4,128,128]{2,1,0:T(8,128)(2,1)} %refs_1_.7, bf16[256,512]{1,0:T(8,128)(2,1)} %refs_4_.1, bf16[256,512]{1,0:T(8,128)(2,1)} %refs_1_.6), custom_call_target="tpu_custom_call" | custom-call | flops 100000000 | bytes 1000000 | tf_op jit(solution)/shard_map/pallas_call | solution.py:40
  2.9 0.0 copy-start
  2.9 5.8 %all-to-all-start = ((bf16[8,64,128]{2,1,0:T(8,128)(2,1)}), bf16[8,64,128]{2,1,0:T(8,128)(2,1)S(1)}, u32[]{:S(2)}, u32[]{:S(2)}) async-start(bf16[8,64,128]{2,1,0:T(8,128)(2,1)} %get-tuple-element.31), calls=%async_computation | async-start | bytes 262144 | tf_op jit(solution)/shard_map/all_to_all | solution.py:20
  8.7 0.0 copy-start.10
  8.7 0.0 copy-done
  8.7 0.7 copy-done.10
  9.4 0.0 copy-start.1
  9.4 0.9 copy-done.1
  10.4 0.0 copy-start.3
  10.4 0.9 copy-done.3
  11.3 0.0 copy-start.6
  11.3 0.9 copy-done.6
  12.2 1.1 shard_map.127
  13.3 2.0 %all-to-all-done.refs_0_.parts_ref = bf16[8,64,128]{2,1,0:T(8,128)(2,1)S(1)} async-done(((bf16[8,64,128]{2,1,0:T(8,128)(2,1)}), bf16[8,64,128]{2,1,0:T(8,128)(2,1)S(1)}, u32[]{:S(2)}, u32[]{:S(2)}) %all-to-all-start) | async-done | bytes 131104 | tf_op jit(solution)/shard_map/all_to_all | solution.py:20
  15.3 28.5 %all_to_all.50.far_ref = bf16[8,64,128]{2,1,0:T(8,128)(2,1)S(1)} all-to-all(bf16[8,64,128]{2,1,0:T(8,128)(2,1)S(1)} %shard_map.128), channel_id=1, replica_groups=mesh['far'=8,'near'=8,'head'=8] {'far'}, dimensions={0} | all-to-all | bytes 262144 | tf_op jit(solution)/shard_map/all_to_all | solution.py:20
  43.8 0.0 copy-start.5
  43.9 10.7 %all_to_all.51.refs_1_.refs_7_ = bf16[8,64,128]{2,1,0:T(8,128)(2,1)S(1)} all-to-all(bf16[8,64,128]{2,1,0:T(8,128)(2,1)S(1)} %shard_map.129), channel_id=1, replica_groups=mesh['far'=8,'near'=8,'head'=8] {'near'}, dimensions={0} | all-to-all | bytes 262144 | tf_op jit(solution)/shard_map/all_to_all | solution.py:20
  54.6 0.0 copy-done.5
  54.6 0.0 copy-start.2
  54.6 0.0 copy-start.4
  54.6 0.4 shard_map.130
  55.0 0.0 copy-start.7
  55.0 9.0 %all_to_all.52.refs_0_ = f32[8,8,256]{2,1,0:T(8,128)S(1)} all-to-all(f32[8,8,256]{2,1,0:T(8,128)S(1)} %get-tuple-element.34), channel_id=1, replica_groups=mesh['far'=8,'near'=8,'head'=8] {'head'}, dimensions={0} | all-to-all | bytes 131072 | tf_op jit(solution)/shard_map/all_to_all | solution.py:20
  64.0 0.0 copy-done.2
  64.0 0.0 copy-done.4
  64.0 0.0 copy-done.7
  64.0 2.6 %shard_map.132 = bf16[8,144,128]{2,1,0:T(8,128)(2,1)} custom-call(f32[8,8,256]{2,1,0:T(8,128)S(1)} %all_to_all.52.refs_0_, f32[256,512]{1,0:T(8,128)S(1)} %get-tuple-element.35.refs_1_, bf16[256,512]{1,0:T(8,128)(2,1)S(1)} %copy-done.5, f32[1,512]{1,0:T(1,128)S(1)} %get-tuple-element.33.refs_4_.refs_3_, ...), custom_call_target="tpu_custom_call" | custom-call | flops 100000000 | bytes 1000000 | tf_op jit(solution)/shard_map/pallas_call | solution.py:40
  66.6 3.4 %all-to-all-start.4 = ((bf16[8,144,128]{2,1,0:T(8,128)(2,1)}), bf16[8,144,128]{2,1,0:T(8,128)(2,1)S(1)}, u32[]{:S(2)}, u32[]{:S(2)}) async-start(bf16[8,144,128]{2,1,0:T(8,128)(2,1)} %shard_map.132), calls=%async_computation.4 | async-start | bytes 589824 | tf_op jit(solution)/shard_map/all_to_all | solution.py:20
  70.1 3.2 %shard_map.131 = (bf16[256,512]{1,0:T(8,128)(2,1)}, bf16[256,512]{1,0:T(8,128)(2,1)}, f32[256,512]{1,0:T(8,128)S(1)}, f32[256,512]{1,0:T(8,128)S(1)}, f32[8,128]{1,0:T(8,128)S(1)}) custom-call(f32[8,8,256]{2,1,0:T(8,128)S(1)} %all_to_all.52.refs_0_, f32[256,512]{1,0:T(8,128)S(1)} %get-tuple-element.35.refs_1_, bf16[256,512]{1,0:T(8,128)(2,1)S(1)} %copy-done.5, ...), custom_call_target="tpu_custom_call" | custom-call | flops 100000000 | bytes 1000000 | tf_op jit(solution)/shard_map/pallas_call | solution.py:40
  73.2 4.5 %all-to-all-done.4.refs_0_.parts_ref = bf16[8,144,128]{2,1,0:T(8,128)(2,1)S(1)} async-done(((bf16[8,144,128]{2,1,0:T(8,128)(2,1)}), bf16[8,144,128]{2,1,0:T(8,128)(2,1)S(1)}, u32[]{:S(2)}, u32[]{:S(2)}) %all-to-all-start.4) | async-done | bytes 294944 | tf_op jit(solution)/shard_map/all_to_all | solution.py:20
  77.7 18.4 %all_to_all.53.far_ref = bf16[8,80,128]{2,1,0:T(8,128)(2,1)S(1)} all-to-all(bf16[8,80,128]{2,1,0:T(8,128)(2,1)S(1)} %shard_map.133), channel_id=1, replica_groups=mesh['far'=8,'near'=8,'head'=8] {'far'}, dimensions={0} | all-to-all | bytes 327680 | tf_op jit(solution)/shard_map/all_to_all | solution.py:20
  96.1 0.0 copy-start.9
  96.1 0.6 shard_map.134
  96.7 0.0 copy-start.8
  96.7 9.9 %all_to_all.54.refs_2_.refs_4_ = bf16[8,64,128]{2,1,0:T(8,128)(2,1)S(1)} all-to-all(bf16[8,64,128]{2,1,0:T(8,128)(2,1)S(1)} %get-tuple-element.40), channel_id=1, replica_groups=mesh['far'=8,'near'=8,'head'=8] {'near'}, dimensions={0} | all-to-all | bytes 262144 | tf_op jit(solution)/shard_map/all_to_all | solution.py:20
  106.7 0.0 copy-done.9
  106.7 0.0 copy-done.8
  106.7 1.7 %shard_map.135 = (bf16[256,512]{1,0:T(8,128)(2,1)S(1)}, bf16[8,64,128]{2,1,0:T(8,128)(2,1)}) custom-call(f32[256,512]{1,0:T(8,128)S(1)} %get-tuple-element.38.refs_0_, bf16[256,512]{1,0:T(8,128)(2,1)S(1)} %copy-done, bf16[8,64,128]{2,1,0:T(8,128)(2,1)S(1)} %all_to_all.54.refs_2_.refs_4_, bf16[4,128,128]{2,1,0:T(8,128)(2,1)S(1)} %copy-done.8, ...), custom_call_target="tpu_custom_call" | custom-call | flops 100000000 | bytes 1000000 | tf_op jit(solution)/shard_map/pallas_call | solution.py:40
  108.3 3.4 %all-to-all-start.7 = ((bf16[8,64,128]{2,1,0:T(8,128)(2,1)}), bf16[8,64,128]{2,1,0:T(8,128)(2,1)S(1)}, u32[]{:S(2)}, u32[]{:S(2)}) async-start(bf16[8,64,128]{2,1,0:T(8,128)(2,1)} %get-tuple-element.45), calls=%async_computation.7 | async-start | bytes 262144 | tf_op jit(solution)/shard_map/all_to_all | solution.py:20
  111.7 1.1 shard_map.136
  112.8 5.5 %all-to-all-done.7.refs_0_ = bf16[8,64,128]{2,1,0:T(8,128)(2,1)S(1)} async-done(((bf16[8,64,128]{2,1,0:T(8,128)(2,1)}), bf16[8,64,128]{2,1,0:T(8,128)(2,1)S(1)}, u32[]{:S(2)}, u32[]{:S(2)}) %all-to-all-start.7) | async-done | bytes 131104 | tf_op jit(solution)/shard_map/all_to_all | solution.py:20
  118.2 0.0 copy-start.11
  118.2 0.7 copy-done.11
  118.9 17.9 %all_to_all.55.refs_0_ = bf16[8,80,128]{2,1,0:T(8,128)(2,1)S(1)} all-to-all(bf16[8,80,128]{2,1,0:T(8,128)(2,1)S(1)} %shard_map.137), channel_id=1, replica_groups=mesh['far'=8,'near'=8,'head'=8] {'far'}, dimensions={0} | all-to-all | bytes 327680 | tf_op jit(solution)/shard_map/all_to_all | solution.py:20
  136.9 9.6 %all_to_all.56.refs_0_ = bf16[8,128,128]{2,1,0:T(8,128)(2,1)S(1)} all-to-all(bf16[8,128,128]{2,1,0:T(8,128)(2,1)S(1)} %shard_map.138), channel_id=1, replica_groups=mesh['far'=8,'near'=8,'head'=8] {'near'}, dimensions={0} | all-to-all | bytes 524288 | tf_op jit(solution)/shard_map/all_to_all | solution.py:20
  146.5 0.8 shard_map.139
  (5 shorter events, 0.2 us)
Async XLA Ops:
  2.9 5.8 %copy-start = (bf16[256,512]{1,0:T(8,128)(2,1)S(1)}, bf16[256,512]{1,0:T(8,128)(2,1)}, u32[]{:S(2)}) copy-start(bf16[256,512]{1,0:T(8,128)(2,1)} %refs_1_.6) | copy-start | bytes 786436
  2.9 12.4 %all-to-all-start = ((bf16[8,64,128]{2,1,0:T(8,128)(2,1)}), bf16[8,64,128]{2,1,0:T(8,128)(2,1)S(1)}, u32[]{:S(2)}, u32[]{:S(2)}) async-start(bf16[8,64,128]{2,1,0:T(8,128)(2,1)} %get-tuple-element.31), calls=%async_computation | async-start | bytes 262144 | tf_op jit(solution)/shard_map/all_to_all | solution.py:20
  8.7 0.7 copy-start.10
  9.4 0.9 copy-start.1
  10.4 0.9 copy-start.3
  11.3 0.9 copy-start.6
  43.8 10.8 %copy-start.5 = (bf16[256,512]{1,0:T(8,128)(2,1)S(1)}, bf16[256,512]{1,0:T(8,128)(2,1)}, u32[]{:S(2)}) copy-start(bf16[256,512]{1,0:T(8,128)(2,1)} %refs_2_.7) | copy-start | bytes 786436
  54.6 9.4 %copy-start.2 = (bf16[256,512]{1,0:T(8,128)(2,1)S(1)}, bf16[256,512]{1,0:T(8,128)(2,1)}, u32[]{:S(2)}) copy-start(bf16[256,512]{1,0:T(8,128)(2,1)} %get-tuple-element.29.refs_0_.refs_6_.refs_3_) | copy-start | bytes 786436
  54.6 9.4 %copy-start.4 = (bf16[256,512]{1,0:T(8,128)(2,1)S(1)}, bf16[256,512]{1,0:T(8,128)(2,1)}, u32[]{:S(2)}) copy-start(bf16[256,512]{1,0:T(8,128)(2,1)} %refs_8_.3) | copy-start | bytes 786436
  55.0 9.0 %copy-start.7 = (bf16[4,128,128]{2,1,0:T(8,128)(2,1)S(1)}, bf16[4,128,128]{2,1,0:T(8,128)(2,1)}, u32[]{:S(2)}) copy-start(bf16[4,128,128]{2,1,0:T(8,128)(2,1)} %refs_9_.3) | copy-start | bytes 393220
  66.6 11.1 %all-to-all-start.4 = ((bf16[8,144,128]{2,1,0:T(8,128)(2,1)}), bf16[8,144,128]{2,1,0:T(8,128)(2,1)S(1)}, u32[]{:S(2)}, u32[]{:S(2)}) async-start(bf16[8,144,128]{2,1,0:T(8,128)(2,1)} %shard_map.132), calls=%async_computation.4 | async-start | bytes 589824 | tf_op jit(solution)/shard_map/all_to_all | solution.py:20
  96.1 10.5 %copy-start.9 = (bf16[256,512]{1,0:T(8,128)(2,1)S(1)}, bf16[256,512]{1,0:T(8,128)(2,1)}, u32[]{:S(2)}) copy-start(bf16[256,512]{1,0:T(8,128)(2,1)} %refs_4_.1) | copy-start | bytes 786436
  96.7 10.0 %copy-start.8 = (bf16[4,128,128]{2,1,0:T(8,128)(2,1)S(1)}, bf16[4,128,128]{2,1,0:T(8,128)(2,1)}, u32[]{:S(2)}) copy-start(bf16[4,128,128]{2,1,0:T(8,128)(2,1)} %refs_1_.7) | copy-start | bytes 393220
  108.3 9.9 %all-to-all-start.7 = ((bf16[8,64,128]{2,1,0:T(8,128)(2,1)}), bf16[8,64,128]{2,1,0:T(8,128)(2,1)S(1)}, u32[]{:S(2)}, u32[]{:S(2)}) async-start(bf16[8,64,128]{2,1,0:T(8,128)(2,1)} %get-tuple-element.45), calls=%async_computation.7 | async-start | bytes 262144 | tf_op jit(solution)/shard_map/all_to_all | solution.py:20
  118.2 0.7 copy-start.11

commit v4 on v3

--- a/solution.py
+++ b/solution.py
@@ -14,6 +14,7 @@
 TOKEN = ((8, 128), F32)
 VMEM_BYTES = 24 * 1024 * 1024
 WHOLE_VMEM = 64 * 1024 * 1024
+MOST_VMEM = 52 * 1024 * 1024
 
 
 def swap(x, axis):
@@ -74,7 +75,9 @@
     slim = chunk // far
     per_head = near // heads
     gain_row = norm_gain.reshape(1, width)
-    group = lax.axis_index("far").reshape(1)
+    place = jnp.stack([lax.axis_index("far"), lax.axis_index("near")])
+    group_keys = lax.all_gather(key_rows, "near")
+    group_values = lax.all_gather(value_rows, "near")
     cols = [slice(h * size, (h + 1) * size) for h in range(heads)]
 
     def put_state(out_ref, h, value, row):
@@ -119,7 +122,7 @@
         query_kernel,
         [((tokens, width), BF), ((tokens, width), F32), ((1, width), F32)],
         [key_feat, feat_query, query_rows, value_rows, gain_row],
-        after=[group],
+        after=[place],
     )
 
     def total_kernel(in_ref, out_ref):
@@ -133,8 +136,8 @@
     (payload,) = run(total_kernel, [((far, chunk, size), BF)], [parts], after=[query_feat])
     parts_far = swap(payload, "far")
 
-    def join(parts_ref, far_ref, group_ref, out_ref, backward):
-        place = group_ref[0]
+    def join(parts_ref, far_ref, place_ref, out_ref, backward):
+        place = place_ref[0]
         state = jnp.zeros((chunk, size), F32)
         for i in range(far):
             keep = (i > place) if backward else (i < place)
@@ -154,10 +157,10 @@
             cost_estimate=pl.CostEstimate(flops=10**6, bytes_accessed=10**6, transcendentals=0),
         )(*ins)
 
-    def prior_kernel(parts_ref, far_ref, group_ref, out_ref):
-        join(parts_ref, far_ref, group_ref, out_ref, False)
-
-    (payload,) = run_join(prior_kernel, [((near, chunk, size), BF)], [parts, parts_far, group])
+    def prior_kernel(parts_ref, far_ref, place_ref, out_ref):
+        join(parts_ref, far_ref, place_ref, out_ref, False)
+
+    (payload,) = run_join(prior_kernel, [((near, chunk, size), BF)], [parts, parts_far, place])
     prior = swap(payload, "near")
 
     def norm_kernel(qf_ref, p_ref, intra_ref, go_ref, gain_ref, pre_ref, out_ref):
@@ -203,7 +206,7 @@
         grad = dot(back, kf_ref[:, at], 1, 0) + dot(delta, get_state(p_ref, h), 1, 1)
         return back, (grad * silu_slope(dot(q_ref[:, at], wq_ref[h], 1, 0))).astype(BF)
 
-    def delta_kernel(st_ref, pre_ref, go_ref, gain_ref, qf_ref, v_ref, kf_ref, p_ref, q_ref, wq_ref, out_ref):
+    def delta_kernel(st_ref, pre_ref, go_ref, gain_ref, qf_ref, v_ref, kf_ref, p_ref, q_ref, wq_ref, k_ref, wk_ref, out_ref):
         inverse, slope = row_factors(st_ref)
         mask = causal_mask(tokens)
         gains = []
@@ -211,23 +214,28 @@
             delta, wide, normed = delta_of(at, inverse, slope, pre_ref, go_ref, gain_ref)
             gains.append(jnp.sum(wide * normed, axis=0, keepdims=True))
             put_state(out_ref, h, dot(qf_ref[:, at], delta, 0, 0), 0)
-            _, grad = query_side(h, at, delta, mask, v_ref, kf_ref, p_ref, q_ref, wq_ref)
+            back, grad = query_side(h, at, delta, mask, v_ref, kf_ref, p_ref, q_ref, wq_ref)
             put_state(out_ref, h, dot(q_ref[:, at], grad, 0, 0), chunk)
+            grad = dot(back, qf_ref[:, at], 0, 0) * silu_slope(dot(k_ref[:, at], wk_ref[h], 1, 0))
+            put_state(out_ref, h, dot(grad.astype(BF), k_ref[:, at], 0, 0), 2 * chunk)
         rest = [jnp.zeros((GAIN_ROWS - heads, size), F32)]
         rows = jnp.concatenate(gains + rest, axis=0).astype(BF)
         for i in range(near):
-            out_ref[i, 2 * chunk :, :] = rows
+            out_ref[i, 3 * chunk :, :] = rows
 
     (payload,) = run(
         delta_kernel,
-        [((near, 2 * chunk + GAIN_ROWS, size), BF)],
-        [stats, pre_norm, grad_out, gain_row, query_feat, value_rows, key_feat, prior, query_rows, feat_query],
+        [((near, 3 * chunk + GAIN_ROWS, size), BF)],
+        [
+            stats, pre_norm, grad_out, gain_row, query_feat, value_rows, key_feat, prior,
+            query_rows, feat_query, key_rows, feat_key,
+        ],
     )
     parts = swap(payload, "near")
 
     def local_kernel(
-        st_ref, pre_ref, go_ref, gain_ref, qf_ref, v_ref, kf_ref, p_ref, q_ref, wq_ref,
-        att_ref, gq_ref, kg_ref, gv_ref, token_ref,
+        st_ref, pre_ref, go_ref, gain_ref, qf_ref, v_ref, kf_ref, p_ref, q_ref, wq_ref, k_ref, wk_ref,
+        att_ref, gq_ref, kg_ref, ks_ref, gv_ref, token_ref,
     ):
         token_ref[...] = jnp.zeros(token_ref.shape, F32)
         inverse, slope = row_factors(st_ref)
@@ -237,21 +245,64 @@
             att_ref[:, at] = (normed * gain_ref[:, at]).astype(BF)
             back, grad = query_side(h, at, delta, mask, v_ref, kf_ref, p_ref, q_ref, wq_ref)
             gq_ref[:, at] = dot(grad, wq_ref[h], 1, 1).astype(BF)
-            kg_ref[:, at] = dot(back, qf_ref[:, at], 0, 0)
+            kg_ref[:, at] = dot(back, qf_ref[:, at], 0, 0).astype(BF)
+            ks_ref[:, at] = silu_slope(dot(k_ref[:, at], wk_ref[h], 1, 0)).astype(BF)
             scores = jnp.where(mask, dot(qf_ref[:, at], kf_ref[:, at], 1, 1), 0.0).astype(BF)
-            gv_ref[:, at] = dot(scores, delta, 0, 0)
-
-    attended, grad_query, key_grad_local, grad_value_local, token = run(
+            gv_ref[:, at] = dot(scores, delta, 0, 0).astype(BF)
+
+    attended, grad_query, key_grad_local, key_slope, grad_value_local, token = run(
         local_kernel,
-        [((tokens, width), BF)] * 2 + [((tokens, width), F32)] * 2 + [TOKEN],
-        [stats, pre_norm, grad_out, gain_row, query_feat, value_rows, key_feat, prior, query_rows, feat_query],
-    )
+        [((tokens, width), BF)] * 5 + [TOKEN],
+        [
+            stats, pre_norm, grad_out, gain_row, query_feat, value_rows, key_feat, prior,
+            query_rows, feat_query, key_rows, feat_key,
+        ],
+    )
+
+    def chunk_kernel(place_ref, wk_ref, keys_ref, values_ref, token_in, k_ref, v_ref, slope_ref, token_ref, sems):
+        head = place_ref[1] // per_head
+        at = pl.ds(pl.multiple_of(head * size, size), size)
+        moves = [
+            pltpu.make_async_copy(keys_ref.at[:, :, at], k_ref, sems.at[0]),
+            pltpu.make_async_copy(values_ref.at[:, :, at], v_ref, sems.at[1]),
+        ]
+        for move in moves:
+            move.start()
+        token_ref[...] = jnp.zeros(token_ref.shape, F32)
+        weights = wk_ref[head]
+        part = place_ref[1] % per_head
+        moves[0].wait()
+        for i in range(near):
+            slope = silu_slope(dot(k_ref[i], weights, 1, 0))
+            mine = slope[:, :chunk]
+            for other in range(1, per_head):
+                mine = jnp.where(part == other, slope[:, other * chunk : (other + 1) * chunk], mine)
+            slope_ref[i] = mine.astype(BF)
+        moves[1].wait()
+
+    whole = pl.BlockSpec(memory_space=pltpu.VMEM)
+    anywhere = pl.BlockSpec(memory_space=pl.ANY)
+    scalars = pl.BlockSpec(memory_space=pltpu.SMEM)
+    chunk_keys, chunk_values, chunk_slope, token = pl.pallas_call(
+        chunk_kernel,
+        out_shape=[
+            jax.ShapeDtypeStruct((near, tokens, size), BF),
+            jax.ShapeDtypeStruct((near, tokens, size), BF),
+            jax.ShapeDtypeStruct((near, tokens, chunk), BF),
+            jax.ShapeDtypeStruct(*TOKEN),
+        ],
+        in_specs=[scalars, whole, anywhere, anywhere, anywhere],
+        out_specs=[whole] * 4,
+        scratch_shapes=[pltpu.SemaphoreType.DMA((2,))],
+        compiler_params=pltpu.CompilerParams(vmem_limit_bytes=MOST_VMEM),
+        cost_estimate=pl.CostEstimate(flops=10**8, bytes_accessed=10**6, transcendentals=0),
+    )(place, feat_key, group_keys, group_values, token)
 
     def back_total_kernel(in_ref, out_ref):
         total = in_ref[0].astype(F32)
         for i in range(1, near):
             total = total + in_ref[i].astype(F32)
-        head_rows, gains = total[:chunk], total[2 * chunk : 2 * chunk + 8]
+        head_rows, gains = total[:chunk], total[3 * chunk : 3 * chunk + 8]
         for i in range(far):
             part = total[chunk + i * slim : chunk + (i + 1) * slim]
             out_ref[i] = jnp.concatenate([head_rows, part, gains], axis=0).astype(BF)
@@ -261,88 +312,63 @@
     )
     parts_far = swap(payload, "far")
 
-    def later_kernel(parts_ref, far_ref, group_ref, out_ref, side_ref, gain_ref):
-        join(parts_ref, far_ref, group_ref, out_ref, True)
+    def later_kernel(parts_ref, far_ref, k_ref, v_ref, slope_ref, place_ref, out_ref, later_ref, gain_ref):
+        join(parts_ref, far_ref, place_ref, later_ref, True)
         side = far_ref[0].astype(F32)[chunk:]
         for i in range(1, far):
             side = side + far_ref[i].astype(F32)[chunk:]
-        side_ref[...] = side
-        for h, at in enumerate(cols):
-            gain_ref[:, at] = side[slim + h : slim + h + 1]
-
-    payload, side, gain_sum = run_join(
-        later_kernel,
-        [((near, chunk, size), BF), ((slim + 8, size), F32), ((1, width), F32)],
-        [parts, parts_far, group],
-    )
-    grad_gain = gain_sum.reshape(width)
-    later = swap(payload, "near")
-
-    def key_kernel(kg_ref, v_ref, l_ref, wk_ref, k_ref, kpg_ref, out_ref):
-        for h, at in enumerate(cols):
-            grad = kg_ref[:, at] + dot(v_ref[:, at], get_state(l_ref, h), 1, 1)
-            grad = (grad * silu_slope(dot(k_ref[:, at], wk_ref[h], 1, 0))).astype(BF)
-            kpg_ref[:, at] = grad
-            put_state(out_ref, h, dot(k_ref[:, at], grad, 0, 0), 0)
-
-    key_pre_grad, payload = run(
-        key_kernel,
-        [((tokens, width), BF), ((near, chunk, size), BF)],
-        [key_grad_local, value_rows, later, feat_key, key_rows],
-    )
-    parts = swap(payload, "near")
-
-    def last_kernel(kpg_ref, wk_ref, gv_ref, kf_ref, l_ref, gk_ref, out_ref, token_ref):
-        token_ref[...] = jnp.zeros(token_ref.shape, F32)
-        for h, at in enumerate(cols):
-            gk_ref[:, at] = dot(kpg_ref[:, at], wk_ref[h], 1, 1).astype(BF)
-            value = gv_ref[:, at] + dot(kf_ref[:, at], get_state(l_ref, h), 1, 0)
-            out_ref[:, at] = value.astype(BF)
-
-    grad_key, grad_value, token = run(
-        last_kernel,
-        [((tokens, width), BF), ((tokens, width), BF), TOKEN],
-        [key_pre_grad, feat_key, grad_value_local, key_feat, later],
-    )
-
-    def weight_total_kernel(in_ref, side_ref, out_ref):
-        total = in_ref[0].astype(F32)
-        for i in range(1, near):
-            total = total + in_ref[i].astype(F32)
+        for h in range(heads):
+            gain_ref[h * size : (h + 1) * size] = side[slim + h]
+        total = jnp.zeros((chunk, size), F32)
+        for i in range(near):
+            grad = dot(v_ref[i], later_ref[i], 1, 1) * slope_ref[i].astype(F32)
+            total = total + dot(grad.astype(BF), k_ref[i], 0, 0)
+            total = total + parts_ref[i].astype(F32)[2 * chunk : 3 * chunk]
         pad = jnp.zeros((8, size), F32)
-        total = jnp.concatenate([total, side_ref[:slim], pad], axis=0).astype(BF)
+        total = jnp.concatenate([total, side[:slim], pad], axis=0).astype(BF)
         for i in range(far):
             out_ref[i] = total
 
-    (payload,) = run(
-        weight_total_kernel,
-        [((far, chunk + slim + 8, size), BF)],
-        [parts, side],
-        after=[token, grad_gain],
+    payload, later, grad_gain = run_join(
+        later_kernel,
+        [((far, chunk + slim + 8, size), BF), ((near, chunk, size), BF), ((width,), F32)],
+        [parts, parts_far, chunk_keys, chunk_values, chunk_slope, place],
     )
     parts_far = swap(payload, "far")
 
-    def weight_kernel(far_ref, out_ref):
+    def weight_kernel(far_ref, later_ref, out_ref):
         total = far_ref[0].astype(F32)[:chunk]
         for i in range(1, far):
             total = total + far_ref[i].astype(F32)[:chunk]
         queries = [far_ref[i].astype(F32)[chunk : chunk + slim] for i in range(far)]
         total = jnp.concatenate([total] + queries, axis=0).astype(BF)
         for i in range(near):
-            out_ref[i] = total
-
-    (payload,) = run(weight_kernel, [((near, 2 * chunk, size), BF)], [parts_far])
+            out_ref[i, :chunk] = later_ref[i]
+            out_ref[i, chunk:] = total
+
+    (payload,) = run(weight_kernel, [((near, 3 * chunk, size), BF)], [parts_far, later])
     done = swap(payload, "near")
 
-    def widen_kernel(in_ref, gq_ref, gk_ref):
-        for h in range(heads):
-            for part in range(per_head):
-                rows = slice(part * chunk, (part + 1) * chunk)
-                gk_ref[h, rows] = in_ref[h * per_head + part, :chunk].astype(F32)
-                gq_ref[h, rows] = in_ref[h * per_head + part, chunk:].astype(F32)
-
-    grad_feat_query, grad_feat_key = run(
-        widen_kernel, [(feat_query.shape, F32), (feat_key.shape, F32)], [done]
+    def last_kernel(
+        in_ref, kg_ref, ks_ref, v_ref, wk_ref, gv_ref, kf_ref, gk_ref, gvalue_ref, gfq_ref, gfk_ref
+    ):
+        for h, at in enumerate(cols):
+            mine = range(h * per_head, (h + 1) * per_head)
+            later = jnp.concatenate([in_ref[j, :chunk] for j in mine], axis=0)
+            grad = kg_ref[:, at].astype(F32) + dot(v_ref[:, at], later, 1, 1)
+            grad = (grad * ks_ref[:, at].astype(F32)).astype(BF)
+            gk_ref[:, at] = dot(grad, wk_ref[h], 1, 1).astype(BF)
+            value = gv_ref[:, at].astype(F32) + dot(kf_ref[:, at], later, 1, 0)
+            gvalue_ref[:, at] = value.astype(BF)
+            rows = [in_ref[j, chunk : 2 * chunk].astype(F32) for j in mine]
+            gfk_ref[h] = jnp.transpose(jnp.concatenate(rows, axis=0))
+            rows = [in_ref[j, 2 * chunk :].astype(F32) for j in mine]
+            gfq_ref[h] = jnp.concatenate(rows, axis=0)
+
+    grad_key, grad_value, grad_feat_query, grad_feat_key = run(
+        last_kernel,
+        [((tokens, width), BF), ((tokens, width), BF), (feat_query.shape, F32), (feat_key.shape, F32)],
+        [done, key_grad_local, key_slope, value_rows, feat_key, grad_value_local, key_feat],
     )
     return (attended, grad_query, grad_key, grad_value, grad_feat_query, grad_feat_key, grad_gain)
 

time: 148 us -> 189 us (1.28)
  waiting for transfers between devices: 12 us -> 33.5 us
  between operations: 0.72 us -> 14.2 us
  Pallas kernels: 13.8 us -> 18.3 us
  starting transfers between devices: 12.6 us -> 9.33 us
  blocking collectives: 104 us -> 107 us
    all_gather x0 -> x2, waiting for transfers between devices: none -> 31.1 us  [the longest x1 31.1 us: shards(): group_values = lax.all_gather(value_rows, 'near')]
    all_to_all x3 -> x2, waiting for transfers between devices: 12 us -> 0.98 us  [swap(): return lax.all_to_all(x, axis, 0, 0)]
    all_to_all x3 -> x2, starting transfers between devices: 12.6 us -> 9.26 us  [swap(): return lax.all_to_all(x, axis, 0, 0)]
    pallas_call x2, Pallas kernels: 0.64 us -> 3.41 us  [run_join(): pl.pallas_call(kernel, out_shape=[jax.ShapeDtypeStruct(shape, dtype) for...]
    all_to_all x7 -> x6, blocking collectives: 104 us -> 107 us  [swap(): return lax.all_to_all(x, axis, 0, 0)]
    pallas_call x0 -> x1, Pallas kernels: none -> 2.46 us  [shards(): pl.pallas_call(chunk_kernel, out_shape=[jax.ShapeDtypeStruct((near, token...]
    unnamed x24 -> x32, local copies, waits for them, and re-layouts: 4.18 us -> 5.88 us
    pallas_call x12 -> x9, Pallas kernels: 13.2 us -> 12.5 us  [run(): pl.pallas_call(body, out_shape=[jax.ShapeDtypeStruct(shape, dtype) for sh...]
  transfers between devices with their start and end apart: 3 -> 4, of which waited for: 3 -> 2; matrix products, arithmetic and copies ran while one was open for 0% -> 0% of each run, Pallas kernels for 4% -> 7%
where the time goes in v4:
time: 189 us; the launch traced here: 188 us
  blocking collectives  107 us (57%)
  waiting for transfers between devices  33.5 us (18%)
  Pallas kernels  18.3 us (10%)
  between operations  14.2 us (8%)
  starting transfers between devices  9.33 us (5%)
  local copies, waits for them, and re-layouts  5.88 us (3%)
    all_to_all x6, blocking collectives, swap(): return lax.all_to_all(x, axis, 0, 0)  107 us
    all_gather x1, waiting for transfers between devices, shards(): group_values = lax.all_gather(value_rows, 'near')  31.1 us
    pallas_call x9, Pallas kernels, run(): pl.pallas_call(body, out_shape=[jax.ShapeDtypeStruct(shape, dtype) for sh...  12.5 us
    all_to_all x2, starting transfers between devices, swap(): return lax.all_to_all(x, axis, 0, 0)  9.26 us
    unnamed x32, local copies, waits for them, and re-layouts  5.88 us
  transfers between devices with their start and end apart: 4, of which 2 were waited for; matrix products, arithmetic and copies ran while one was open for 0% of the time, Pallas kernels for 7%

profile of v4, /device:TPU:8, one launch (start us, length us, event | category | flops | bytes accessed | tf_op | source)
XLA Modules:
  0.0 187.8 jit_solution(13040419915371733287)
XLA Ops:
  7.2 0.0 all-gather.5.cloned.1.call-start
  7.2 0.7 all-gather.5.cloned.1.call-update
  7.9 0.0 all-gather.7.cloned.1.call-start
  7.9 0.7 all-gather.7.cloned.1.call-update
  8.6 2.3 %shard_map.126 = (bf16[256,512]{1,0:T(8,128)(2,1)}, bf16[8,64,128]{2,1,0:T(8,128)(2,1)}) custom-call(bf16[4,128,128]{2,1,0:T(8,128)(2,1)} %refs_4_.1, bf16[256,512]{1,0:T(8,128)(2,1)} %refs_10_.3, bf16[256,512]{1,0:T(8,128)(2,1)} %refs_3_.5), custom_call_target="tpu_custom_call" | custom-call | flops 100000000 | bytes 1000000 | tf_op jit(solution)/shard_map/pallas_call | solution.py:41
  10.9 0.0 copy-start.1
  10.9 5.8 %all-to-all-start = ((bf16[8,64,128]{2,1,0:T(8,128)(2,1)}), bf16[8,64,128]{2,1,0:T(8,128)(2,1)S(1)}, u32[]{:S(2)}, u32[]{:S(2)}) async-start(bf16[8,64,128]{2,1,0:T(8,128)(2,1)} %get-tuple-element.33), calls=%async_computation | async-start | bytes 262144 | tf_op jit(solution)/shard_map/all_to_all | solution.py:21
  16.7 0.1 pad_add_fusion.refs_5_.place_ref
  16.8 0.0 copy-start
  16.8 0.9 copy-done
  17.8 0.0 copy-start.2
  17.8 0.9 copy-done.2
  18.7 0.9 copy-done.6
  19.7 0.9 copy-done.9
  20.6 0.7 copy-done.15
  21.3 0.0 copy-start.7
  21.3 0.0 copy-start.10
  21.3 1.1 shard_map.127
  22.3 1.0 all-to-all-done.refs_0_.parts_ref
  23.3 31.3 %all_to_all.40.far_ref = bf16[8,64,128]{2,1,0:T(8,128)(2,1)S(1)} all-to-all(bf16[8,64,128]{2,1,0:T(8,128)(2,1)S(1)} %shard_map.128), channel_id=1, replica_groups=mesh['far'=8,'near'=8,'head'=8] {'far'}, dimensions={0} | all-to-all | bytes 262144 | tf_op jit(solution)/shard_map/all_to_all | solution.py:21
  54.6 0.6 shard_map.129
  55.2 10.7 %all_to_all.41.refs_1_.refs_7_ = bf16[8,64,128]{2,1,0:T(8,128)(2,1)S(1)} all-to-all(bf16[8,64,128]{2,1,0:T(8,128)(2,1)S(1)} %shard_map.129), channel_id=1, replica_groups=mesh['far'=8,'near'=8,'head'=8] {'near'}, dimensions={0} | all-to-all | bytes 262144 | tf_op jit(solution)/shard_map/all_to_all | solution.py:21
  65.9 0.0 copy-done.8
  65.9 0.4 shard_map.130
  66.3 8.9 %all_to_all.42.refs_0_ = f32[8,8,256]{2,1,0:T(8,128)S(1)} all-to-all(f32[8,8,256]{2,1,0:T(8,128)S(1)} %get-tuple-element.36), channel_id=1, replica_groups=mesh['far'=8,'near'=8,'head'=8] {'head'}, dimensions={0} | all-to-all | bytes 131072 | tf_op jit(solution)/shard_map/all_to_all | solution.py:21
  75.2 0.0 copy-done.1
  75.2 0.0 copy-done.3
  75.2 0.0 copy-done.4
  75.2 0.0 copy-done.5
  75.2 0.0 copy-done.7
  75.2 0.0 copy-done.10
  75.2 3.7 %shard_map.132 = bf16[8,208,128]{2,1,0:T(8,128)(2,1)} custom-call(f32[8,8,256]{2,1,0:T(8,128)S(1)} %all_to_all.42.refs_0_, f32[256,512]{1,0:T(8,128)S(1)} %get-tuple-element.37.refs_1_, bf16[256,512]{1,0:T(8,128)(2,1)S(1)} %copy-done.8, f32[1,512]{1,0:T(1,128)S(1)} %get-tuple-element.35.refs_4_.refs_3_, ...), custom_call_target="tpu_custom_call" | custom-call | flops 100000000 | bytes 1000000 | tf_op jit(solution)/shard_map/pallas_call | solution.py:41
  78.9 3.5 %all-to-all-start.4 = ((bf16[8,208,128]{2,1,0:T(8,128)(2,1)}), bf16[8,208,128]{2,1,0:T(8,128)(2,1)S(1)}, u32[]{:S(2)}, u32[]{:S(2)}) async-start(bf16[8,208,128]{2,1,0:T(8,128)(2,1)} %shard_map.132), calls=%async_computation.4 | async-start | bytes 851968 | tf_op jit(solution)/shard_map/all_to_all | solution.py:21
  82.4 3.3 %shard_map.131 = (bf16[256,512]{1,0:T(8,128)(2,1)}, bf16[256,512]{1,0:T(8,128)(2,1)}, bf16[256,512]{1,0:T(8,128)(2,1)S(1)}, bf16[256,512]{1,0:T(8,128)(2,1)S(1)}...) custom-call(f32[8,8,256]{2,1,0:T(8,128)S(1)} %all_to_all.42.refs_0_, f32[256,512]{1,0:T(8,128)S(1)} %get-tuple-element.37.refs_1_, ...), custom_call_target="tpu_custom_call" | custom-call | flops 100000000 | bytes 1000000 | tf_op jit(solution)/shard_map/pallas_call | solution.py:41
  85.7 0.7 copy-done.11
  86.4 0.7 copy-done.13
  87.1 31.1 %all-gather.7.cloned.1.call-done = bf16[2048,512]{1,0:T(8,128)(2,1)} async-done(((bf16[256,512]{1,0:T(8,128)(2,1)}), bf16[2048,512]{1,0:T(8,128)(2,1)}) %all-gather.7.cloned.1.call-update) | async-done | bytes 2097168 | tf_op jit(solution)/shard_map/all_gather | solution.py:80
  118.2 2.5 %shard_map.133 = (bf16[8,256,128]{2,1,0:T(8,128)(2,1)S(1)}, bf16[8,256,128]{2,1,0:T(8,128)(2,1)S(1)}, bf16[8,256,64]{2,1,0:T(8,128)(2,1)S(1)}, f32[8,128]{1,0:T(8,128)S(1)}) custom-call(s32[2]{0:T(128)S(1)} %pad_add_fusion.refs_5_.place_ref, bf16[4,128,128]{2,1,0:T(8,128)(2,1)S(1)} %copy-done.5, bf16[8,256,512]{2,1,0:T(8,128)(2,1)} %bitcast.6, ...), custom_call_target="tpu_custom_call" | custom-call | flops 100000000 | bytes 1000000 | tf_op jit(solution)/shard_map/pallas_call | solution.py:286
  120.7 0.0 all-to-all-done.4.refs_0_.parts_ref
  120.8 0.0 copy-start.12
  120.8 0.0 copy-start.14
  120.8 27.1 %all_to_all.43.far_ref = bf16[8,80,128]{2,1,0:T(8,128)(2,1)S(1)} all-to-all(bf16[8,80,128]{2,1,0:T(8,128)(2,1)S(1)} %shard_map.134), channel_id=1, replica_groups=mesh['far'=8,'near'=8,'head'=8] {'far'}, dimensions={0} | all-to-all | bytes 327680 | tf_op jit(solution)/shard_map/all_to_all | solution.py:21
  147.9 2.8 %shard_map.135 = (bf16[8,80,128]{2,1,0:T(8,128)(2,1)S(1)}, bf16[8,64,128]{2,1,0:T(8,128)(2,1)S(1)}, f32[512]{0:T(512)}) custom-call(bf16[8,208,128]{2,1,0:T(8,128)(2,1)S(1)} %all-to-all-done.4.refs_0_.parts_ref, bf16[8,80,128]{2,1,0:T(8,128)(2,1)S(1)} %all_to_all.43.far_ref, bf16[8,256,128]{2,1,0:T(8,128)(2,1)S(1)} %get-tuple-element.42.k_ref, ...), custom_call_target="tpu_custom_call" | custom-call | flops 1000000 | bytes 1000000 | tf_op jit(solution)/shard_map/pallas_call | solution.py:151
  150.7 18.2 %all_to_all.44.refs_0_ = bf16[8,80,128]{2,1,0:T(8,128)(2,1)S(1)} all-to-all(bf16[8,80,128]{2,1,0:T(8,128)(2,1)S(1)} %get-tuple-element.45), channel_id=1, replica_groups=mesh['far'=8,'near'=8,'head'=8] {'far'}, dimensions={0} | all-to-all | bytes 327680 | tf_op jit(solution)/shard_map/all_to_all | solution.py:21
  168.9 10.4 %all_to_all.45.refs_0_ = bf16[8,192,128]{2,1,0:T(8,128)(2,1)S(1)} all-to-all(bf16[8,192,128]{2,1,0:T(8,128)(2,1)S(1)} %shard_map.136), channel_id=1, replica_groups=mesh['far'=8,'near'=8,'head'=8] {'near'}, dimensions={0} | all-to-all | bytes 786432 | tf_op jit(solution)/shard_map/all_to_all | solution.py:21
  179.3 0.0 copy-done.12
  179.3 0.0 copy-done.14
  179.3 1.7 shard_map.137
  (13 shorter events, 0.1 us)
Async XLA Ops:
  7.2 80.0 %all-gather.5.cloned.1.call-start = ((), (), s32[]{:S(2)}) async-start(), calls=%async_computation.8 | async-start | bytes 2359296 | tf_op jit(solution)/shard_map/all_gather | solution.py:79
  7.9 110.3 %all-gather.7.cloned.1.call-start = ((), (), s32[]{:S(2)}) async-start(), calls=%async_computation.9 | async-start | bytes 2359296 | tf_op jit(solution)/shard_map/all_gather | solution.py:80
  10.9 64.3 %copy-start.1 = (bf16[256,512]{1,0:T(8,128)(2,1)S(1)}, bf16[256,512]{1,0:T(8,128)(2,1)}, u32[]{:S(2)}) copy-start(bf16[256,512]{1,0:T(8,128)(2,1)} %refs_3_.5) | copy-start | bytes 786436
  10.9 12.4 %all-to-all-start = ((bf16[8,64,128]{2,1,0:T(8,128)(2,1)}), bf16[8,64,128]{2,1,0:T(8,128)(2,1)S(1)}, u32[]{:S(2)}, u32[]{:S(2)}) async-start(bf16[8,64,128]{2,1,0:T(8,128)(2,1)} %get-tuple-element.33), calls=%async_computation | async-start | bytes 262144 | tf_op jit(solution)/shard_map/all_to_all | solution.py:21
  16.8 0.9 copy-start
  17.8 0.9 copy-start.2
  18.7 0.9 copy-start.6
  19.7 0.9 copy-start.9
  20.6 0.7 copy-start.15
  21.3 44.6 %copy-start.8 = (bf16[256,512]{1,0:T(8,128)(2,1)S(1)}, bf16[256,512]{1,0:T(8,128)(2,1)}, u32[]{:S(2)}) copy-start(bf16[256,512]{1,0:T(8,128)(2,1)} %refs_2_.7) | copy-start | bytes 786436
  21.3 54.0 %copy-start.3 = (bf16[256,512]{1,0:T(8,128)(2,1)S(1)}, bf16[256,512]{1,0:T(8,128)(2,1)}, u32[]{:S(2)}) copy-start(bf16[256,512]{1,0:T(8,128)(2,1)} %get-tuple-element.31.refs_0_.refs_6_) | copy-start | bytes 786436
  21.3 54.0 %copy-start.4 = (bf16[256,512]{1,0:T(8,128)(2,1)S(1)}, bf16[256,512]{1,0:T(8,128)(2,1)}, u32[]{:S(2)}) copy-start(bf16[256,512]{1,0:T(8,128)(2,1)} %refs_10_.3) | copy-start | bytes 786436
  21.3 54.0 %copy-start.5 = (bf16[4,128,128]{2,1,0:T(8,128)(2,1)S(1)}, bf16[4,128,128]{2,1,0:T(8,128)(2,1)}, u32[]{:S(2)}) copy-start(bf16[4,128,128]{2,1,0:T(8,128)(2,1)} %refs_4_.1) | copy-start | bytes 393220
  21.3 54.0 %copy-start.7 = (bf16[256,512]{1,0:T(8,128)(2,1)S(1)}, bf16[256,512]{1,0:T(8,128)(2,1)}, u32[]{:S(2)}) copy-start(bf16[256,512]{1,0:T(8,128)(2,1)} %refs_8_.3) | copy-start | bytes 786436
  21.3 54.0 %copy-start.10 = (bf16[4,128,128]{2,1,0:T(8,128)(2,1)S(1)}, bf16[4,128,128]{2,1,0:T(8,128)(2,1)}, u32[]{:S(2)}) copy-start(bf16[4,128,128]{2,1,0:T(8,128)(2,1)} %refs_9_.3) | copy-start | bytes 393220
  78.9 41.8 %all-to-all-start.4 = ((bf16[8,208,128]{2,1,0:T(8,128)(2,1)}), bf16[8,208,128]{2,1,0:T(8,128)(2,1)S(1)}, u32[]{:S(2)}, u32[]{:S(2)}) async-start(bf16[8,208,128]{2,1,0:T(8,128)(2,1)} %shard_map.132), calls=%async_computation.4 | async-start | bytes 851968 | tf_op jit(solution)/shard_map/all_to_all | solution.py:21
  85.7 0.7 copy-start.11
  86.4 0.7 copy-start.13
  120.8 58.6 %copy-start.12 = (bf16[256,512]{1,0:T(8,128)(2,1)S(1)}, bf16[256,512]{1,0:T(8,128)(2,1)}, u32[]{:S(2)}) copy-start(bf16[256,512]{1,0:T(8,128)(2,1)} %copy-done.11) | copy-start | bytes 786436
  120.8 58.5 %copy-start.14 = (bf16[256,512]{1,0:T(8,128)(2,1)S(1)}, bf16[256,512]{1,0:T(8,128)(2,1)}, u32[]{:S(2)}) copy-start(bf16[256,512]{1,0:T(8,128)(2,1)} %copy-done.13) | copy-start | bytes 786436
Sparse Core Ops, SparseCore 0:
  10.1 56.3 all-gather.4
  68.5 49.6 all-gather.6

commit v5 on v4

--- a/solution.py
+++ b/solution.py
@@ -1,3 +1,5 @@
+import math
+
 import jax
 import jax.numpy as jnp
 from jax import lax
@@ -8,7 +10,7 @@
 EPSILON = 1e-05
 BF = jnp.bfloat16
 F32 = jnp.float32
-NEAR = 8
+NEAR = ("row", "pair", "side")
 GAIN_ROWS = 16
 STAT_ROWS = 8
 TOKEN = ((8, 128), F32)
@@ -69,15 +71,13 @@
 def shards(query_rows, key_rows, value_rows, feat_query, feat_key, norm_gain, grad_out):
     tokens, width = query_rows.shape
     heads, size = feat_query.shape[0], feat_query.shape[1]
-    near, far = lax.axis_size("near"), lax.axis_size("far")
+    near, far = math.prod(lax.axis_size(name) for name in NEAR), lax.axis_size("far")
     full_width = width * lax.axis_size("head")
     chunk = heads * size // near
     slim = chunk // far
     per_head = near // heads
     gain_row = norm_gain.reshape(1, width)
-    place = jnp.stack([lax.axis_index("far"), lax.axis_index("near")])
-    group_keys = lax.all_gather(key_rows, "near")
-    group_values = lax.all_gather(value_rows, "near")
+    place = jnp.stack([lax.axis_index("far"), lax.axis_index(NEAR)])
     cols = [slice(h * size, (h + 1) * size) for h in range(heads)]
 
     def put_state(out_ref, h, value, row):
@@ -89,24 +89,27 @@
         parts = [ref[h * per_head + part] for part in range(per_head)]
         return jnp.concatenate(parts, axis=0)
 
-    def state_kernel(w_ref, k_ref, v_ref, kf_ref, out_ref, waits):
+    def state_kernel(w_ref, k_ref, v_ref, kf_ref, out_ref, both_ref, waits):
         waits[0]()
         waits[1]()
         for h, at in enumerate(cols):
             pre = dot(k_ref[:, at], w_ref[h], 1, 0)
             kf_ref[:, at] = (pre / (1.0 + jnp.exp(-pre))).astype(BF)
+        both_ref[:, :width] = k_ref[...]
         waits[2]()
+        both_ref[:, width:] = v_ref[...]
         for h, at in enumerate(cols):
             put_state(out_ref, h, dot(kf_ref[:, at], v_ref[:, at], 0, 0), 0)
 
-    key_feat, payload = run(
+    key_feat, payload, both = run(
         state_kernel,
-        [((tokens, width), BF), ((near, chunk, size), BF)],
+        [((tokens, width), BF), ((near, chunk, size), BF), ((tokens, 2 * width), BF)],
         [],
         fetch=[feat_key, key_rows, value_rows],
         limit=WHOLE_VMEM,
     )
-    parts = swap(payload, "near")
+    gathered = lax.all_gather(both, NEAR[:2])
+    parts = swap(payload, NEAR)
 
     def query_kernel(kf_ref, wq_ref, q_ref, v_ref, gain_ref, qf_ref, intra_ref, gain_out):
         gain_out[...] = gain_ref[...]
@@ -161,7 +164,7 @@
         join(parts_ref, far_ref, place_ref, out_ref, False)
 
     (payload,) = run_join(prior_kernel, [((near, chunk, size), BF)], [parts, parts_far, place])
-    prior = swap(payload, "near")
+    prior = swap(payload, NEAR)
 
     def norm_kernel(qf_ref, p_ref, intra_ref, go_ref, gain_ref, pre_ref, out_ref):
         squares = jnp.zeros((tokens, size), F32)
@@ -231,7 +234,7 @@
             query_rows, feat_query, key_rows, feat_key,
         ],
     )
-    parts = swap(payload, "near")
+    parts = swap(payload, NEAR)
 
     def local_kernel(
         st_ref, pre_ref, go_ref, gain_ref, qf_ref, v_ref, kf_ref, p_ref, q_ref, wq_ref, k_ref, wk_ref,
@@ -259,44 +262,34 @@
         ],
     )
 
-    def chunk_kernel(place_ref, wk_ref, keys_ref, values_ref, token_in, k_ref, v_ref, slope_ref, token_ref, sems):
-        head = place_ref[1] // per_head
-        at = pl.ds(pl.multiple_of(head * size, size), size)
-        moves = [
-            pltpu.make_async_copy(keys_ref.at[:, :, at], k_ref, sems.at[0]),
-            pltpu.make_async_copy(values_ref.at[:, :, at], v_ref, sems.at[1]),
-        ]
+    def pick_kernel(place_ref, both_ref, token_in, out_ref, token_ref, sems):
+        moves = []
+        for i in range(2):
+            at = pl.multiple_of(place_ref[1] // per_head * size + i * width, size)
+            source = both_ref.at[:, :, pl.ds(at, size)]
+            moves.append(pltpu.make_async_copy(source, out_ref.at[i], sems.at[i]))
         for move in moves:
             move.start()
         token_ref[...] = jnp.zeros(token_ref.shape, F32)
-        weights = wk_ref[head]
-        part = place_ref[1] % per_head
-        moves[0].wait()
-        for i in range(near):
-            slope = silu_slope(dot(k_ref[i], weights, 1, 0))
-            mine = slope[:, :chunk]
-            for other in range(1, per_head):
-                mine = jnp.where(part == other, slope[:, other * chunk : (other + 1) * chunk], mine)
-            slope_ref[i] = mine.astype(BF)
-        moves[1].wait()
+        for move in moves:
+            move.wait()
 
     whole = pl.BlockSpec(memory_space=pltpu.VMEM)
     anywhere = pl.BlockSpec(memory_space=pl.ANY)
     scalars = pl.BlockSpec(memory_space=pltpu.SMEM)
-    chunk_keys, chunk_values, chunk_slope, token = pl.pallas_call(
-        chunk_kernel,
+    picked, token = pl.pallas_call(
+        pick_kernel,
         out_shape=[
-            jax.ShapeDtypeStruct((near, tokens, size), BF),
-            jax.ShapeDtypeStruct((near, tokens, size), BF),
-            jax.ShapeDtypeStruct((near, tokens, chunk), BF),
+            jax.ShapeDtypeStruct((2, near // per_head, tokens, size), BF),
             jax.ShapeDtypeStruct(*TOKEN),
         ],
-        in_specs=[scalars, whole, anywhere, anywhere, anywhere],
-        out_specs=[whole] * 4,
+        in_specs=[scalars, anywhere, anywhere],
+        out_specs=[whole] * 2,
         scratch_shapes=[pltpu.SemaphoreType.DMA((2,))],
         compiler_params=pltpu.CompilerParams(vmem_limit_bytes=MOST_VMEM),
         cost_estimate=pl.CostEstimate(flops=10**8, bytes_accessed=10**6, transcendentals=0),
-    )(place, feat_key, group_keys, group_values, token)
+    )(place, gathered, token)
+    other = lax.ppermute(picked, NEAR[2], [(0, 1), (1, 0)])
 
     def back_total_kernel(in_ref, out_ref):
         total = in_ref[0].astype(F32)
@@ -312,7 +305,7 @@
     )
     parts_far = swap(payload, "far")
 
-    def later_kernel(parts_ref, far_ref, k_ref, v_ref, slope_ref, place_ref, out_ref, later_ref, gain_ref):
+    def later_kernel(parts_ref, far_ref, own_ref, other_ref, wk_ref, place_ref, out_ref, later_ref, gain_ref):
         join(parts_ref, far_ref, place_ref, later_ref, True)
         side = far_ref[0].astype(F32)[chunk:]
         for i in range(1, far):
@@ -320,9 +313,16 @@
         for h in range(heads):
             gain_ref[h * size : (h + 1) * size] = side[slim + h]
         total = jnp.zeros((chunk, size), F32)
+        part = place_ref[1] % per_head
+        weights = wk_ref[place_ref[1] // per_head]
+        weights = jnp.where(part == 0, weights[:, :chunk], weights[:, chunk:])
+        for i in range(near // per_head):
+            for ref, offset in ((own_ref, part), (other_ref, 1 - part)):
+                keys = ref[0, i]
+                grad = dot(ref[1, i], later_ref[per_head * i + offset], 1, 1)
+                grad = grad * silu_slope(dot(keys, weights, 1, 0))
+                total = total + dot(grad.astype(BF), keys, 0, 0)
         for i in range(near):
-            grad = dot(v_ref[i], later_ref[i], 1, 1) * slope_ref[i].astype(F32)
-            total = total + dot(grad.astype(BF), k_ref[i], 0, 0)
             total = total + parts_ref[i].astype(F32)[2 * chunk : 3 * chunk]
         pad = jnp.zeros((8, size), F32)
         total = jnp.concatenate([total, side[:slim], pad], axis=0).astype(BF)
@@ -332,7 +332,7 @@
     payload, later, grad_gain = run_join(
         later_kernel,
         [((far, chunk + slim + 8, size), BF), ((near, chunk, size), BF), ((width,), F32)],
-        [parts, parts_far, chunk_keys, chunk_values, chunk_slope, place],
+        [parts, parts_far, picked, other, feat_key, place],
     )
     parts_far = swap(payload, "far")
 
@@ -347,7 +347,7 @@
             out_ref[i, chunk:] = total
 
     (payload,) = run(weight_kernel, [((near, 3 * chunk, size), BF)], [parts_far, later])
-    done = swap(payload, "near")
+    done = swap(payload, NEAR)
 
     def last_kernel(
         in_ref, kg_ref, ks_ref, v_ref, wk_ref, gv_ref, kf_ref, gk_ref, gvalue_ref, gfq_ref, gfk_ref
@@ -375,8 +375,8 @@
 
 def solution(mesh):
     seq, head = mesh.devices.shape
-    split = Mesh(mesh.devices.reshape(seq // NEAR, NEAR, head), ("far", "near", "head"))
-    wide = P(("far", "near"), "head")
+    split = Mesh(mesh.devices.reshape(seq // 8, 2, 2, 2, head), ("far",) + NEAR + ("head",))
+    wide = P(("far",) + NEAR, "head")
     per_head = P("head", None, None)
     in_specs = (wide, wide, wide, per_head, per_head, P("head"), wide)
     out_specs = (wide, wide, wide, wide, per_head, per_head, P("head"))

time: 189 us -> 166 us (0.88)
  waiting for transfers between devices: 33.5 us -> 17.2 us
  blocking collectives: 107 us -> 94.1 us
  starting transfers between devices: 9.33 us -> 16.2 us
    all_gather x2 -> x1, waiting for transfers between devices: 31.1 us -> 0.01 us  [shards(): gathered = lax.all_gather(both, NEAR[:2])]
    all_to_all x6 -> x5, blocking collectives: 107 us -> 94.1 us  [swap(): return lax.all_to_all(x, axis, 0, 0)]
    ppermute x0 -> x1, waiting for transfers between devices: none -> 11.1 us  [shards(): other = lax.ppermute(picked, NEAR[2], [(0, 1), (1, 0)])]
    all_to_all x2 -> x3, waiting for transfers between devices: 0.98 us -> 6.08 us  [swap(): return lax.all_to_all(x, axis, 0, 0)]
    all_to_all x2 -> x3, starting transfers between devices: 9.26 us -> 14.1 us  [swap(): return lax.all_to_all(x, axis, 0, 0)]
    ppermute x0 -> x1, starting transfers between devices: none -> 2.13 us  [shards(): other = lax.ppermute(picked, NEAR[2], [(0, 1), (1, 0)])]
    unnamed x32 -> x28, local copies, waits for them, and re-layouts: 5.88 us -> 5.18 us
  transfers between devices with their start and end apart: 4 -> 5, of which waited for: 2 -> 4; matrix products, arithmetic and copies ran while one was open for 0% -> 0% of each run, Pallas kernels for 7% -> 6%
where the time goes in v5:
time: 166 us; the launch traced here: 165 us
  blocking collectives  94.1 us (57%)
  Pallas kernels  18.4 us (11%)
  waiting for transfers between devices  17.2 us (10%)
  starting transfers between devices  16.2 us (10%)
  between operations  14.2 us (9%)
  local copies, waits for them, and re-layouts  5.18 us (3%)
    all_to_all x5, blocking collectives, swap(): return lax.all_to_all(x, axis, 0, 0)  94.1 us
    all_to_all x3, starting transfers between devices, swap(): return lax.all_to_all(x, axis, 0, 0)  14.1 us
    pallas_call x9, Pallas kernels, run(): pl.pallas_call(body, out_shape=[jax.ShapeDtypeStruct(shape, dtype) for sh...  13.3 us
    ppermute x1, waiting for transfers between devices, shards(): other = lax.ppermute(picked, NEAR[2], [(0, 1), (1, 0)])  11.1 us
    all_to_all x3, waiting for transfers between devices, swap(): return lax.all_to_all(x, axis, 0, 0)  6.08 us
    unnamed x28, local copies, waits for them, and re-layouts  5.18 us
    pallas_call x2, Pallas kernels, run_join(): pl.pallas_call(kernel, out_shape=[jax.ShapeDtypeStruct(shape, dtype) for...  3.44 us
  transfers between devices with their start and end apart: 5, of which 4 were waited for; matrix products, arithmetic and copies ran while one was open for 0% of the time, Pallas kernels for 6%

profile of v5, /device:TPU:8, one launch (start us, length us, event | category | flops | bytes accessed | tf_op | source)
XLA Modules:
  0.0 165.3 jit_solution(16228323191630347209)
XLA Ops:
  7.2 0.0 all-gather.3.cloned.1.call-start
  7.2 2.5 %shard_map.126 = (bf16[256,512]{1,0:T(8,128)(2,1)}, bf16[8,64,128]{2,1,0:T(8,128)(2,1)}, bf16[256,1024]{1,0:T(8,128)(2,1)}) custom-call(bf16[4,128,128]{2,1,0:T(8,128)(2,1)} %refs_4_.1, bf16[256,512]{1,0:T(8,128)(2,1)} %refs_10_.3, bf16[256,512]{1,0:T(8,128)(2,1)} %refs_3_.5), custom_call_target="tpu_custom_call" | custom-call | flops 100000000 | bytes 1000000 | tf_op jit(solution)/shard_map/pallas_call | solution.py:43
  9.7 0.0 copy-start.3
  9.7 0.0 copy-start.4
  9.7 0.0 copy-start.10
  9.7 0.0 all-gather.3.cloned.1.call-update
  9.8 0.0 copy-start.1
  9.8 5.8 %all-to-all-start = ((bf16[8,64,128]{2,1,0:T(8,128)(2,1)}), bf16[8,64,128]{2,1,0:T(8,128)(2,1)S(1)}, u32[]{:S(2)}, u32[]{:S(2)}) async-start(bf16[8,64,128]{2,1,0:T(8,128)(2,1)} %get-tuple-element.32), calls=%async_computation | async-start | bytes 262144 | tf_op jit(solution)/shard_map/all_to_all | solution.py:23
  15.6 0.1 pad_add_fusion.refs_5_.place_ref
  15.7 0.0 copy-start
  15.7 0.9 copy-done
  16.6 0.0 copy-start.2
  16.6 0.9 copy-done.2
  17.6 0.0 copy-start.5
  17.6 0.9 copy-done.5
  18.5 0.0 copy-start.9
  18.5 0.9 copy-done.9
  19.4 0.7 copy-done.13
  20.1 1.1 shard_map.127
  21.2 1.0 all-to-all-done.refs_0_.parts_ref
  22.2 31.3 %all_to_all.40.far_ref = bf16[8,64,128]{2,1,0:T(8,128)(2,1)S(1)} all-to-all(bf16[8,64,128]{2,1,0:T(8,128)(2,1)S(1)} %shard_map.128), channel_id=1, replica_groups=mesh['far'=8,'row'=2,'pair'=2,'side'=2,'head'=8] {'far'}, dimensions={0} | all-to-all | bytes 262144 | tf_op jit(solution)/shard_map/all_to_all | solution.py:23
  53.5 0.6 shard_map.129
  54.1 11.8 %all_to_all.41.refs_1_.refs_7_ = bf16[8,64,128]{2,1,0:T(8,128)(2,1)S(1)} all-to-all(bf16[8,64,128]{2,1,0:T(8,128)(2,1)S(1)} %shard_map.129), channel_id=1, replica_groups=mesh['far'=8,'row'=2,'pair'=2,'side'=2,'head'=8] {'row','pair','side'}, dimensions={0} | all-to-all | bytes 262144 | tf_op jit(solution)/shard_map/all_to_all | solution.py:23
  65.9 0.0 copy-done.8
  65.9 0.4 shard_map.130
  66.3 14.2 %all_to_all.42.refs_0_ = f32[8,8,256]{2,1,0:T(8,128)S(1)} all-to-all(f32[8,8,256]{2,1,0:T(8,128)S(1)} %get-tuple-element.35), channel_id=1, replica_groups=mesh['far'=8,'row'=2,'pair'=2,'side'=2,'head'=8] {'head'}, dimensions={0} | all-to-all | bytes 131072 | tf_op jit(solution)/shard_map/all_to_all | solution.py:23
  80.4 0.0 copy-done.3
  80.4 0.0 copy-done.4
  80.4 0.0 copy-done.10
  80.4 0.0 copy-done.1
  80.5 0.0 copy-done.6
  80.5 0.0 copy-done.7
  80.5 3.7 %shard_map.132 = bf16[8,208,128]{2,1,0:T(8,128)(2,1)} custom-call(f32[8,8,256]{2,1,0:T(8,128)S(1)} %all_to_all.42.refs_0_, f32[256,512]{1,0:T(8,128)S(1)} %get-tuple-element.36.refs_1_, bf16[256,512]{1,0:T(8,128)(2,1)S(1)} %copy-done.8, f32[1,512]{1,0:T(1,128)S(1)} %get-tuple-element.34.refs_4_.refs_3_, ...), custom_call_target="tpu_custom_call" | custom-call | flops 100000000 | bytes 1000000 | tf_op jit(solution)/shard_map/pallas_call | solution.py:43
  84.1 3.5 %all-to-all-start.4 = ((bf16[8,208,128]{2,1,0:T(8,128)(2,1)}), bf16[8,208,128]{2,1,0:T(8,128)(2,1)S(1)}, u32[]{:S(2)}, u32[]{:S(2)}) async-start(bf16[8,208,128]{2,1,0:T(8,128)(2,1)} %shard_map.132), calls=%async_computation.4 | async-start | bytes 851968 | tf_op jit(solution)/shard_map/all_to_all | solution.py:23
  87.6 3.3 %shard_map.131 = (bf16[256,512]{1,0:T(8,128)(2,1)}, bf16[256,512]{1,0:T(8,128)(2,1)}, bf16[256,512]{1,0:T(8,128)(2,1)S(1)}, bf16[256,512]{1,0:T(8,128)(2,1)S(1)}...) custom-call(f32[8,8,256]{2,1,0:T(8,128)S(1)} %all_to_all.42.refs_0_, f32[256,512]{1,0:T(8,128)S(1)} %get-tuple-element.36.refs_1_, ...), custom_call_target="tpu_custom_call" | custom-call | flops 100000000 | bytes 1000000 | tf_op jit(solution)/shard_map/pallas_call | solution.py:43
  91.0 0.7 copy-done.11
  91.7 1.6 shard_map.133
  93.3 3.1 %all-to-all-done.4.refs_0_.parts_ref = bf16[8,208,128]{2,1,0:T(8,128)(2,1)S(1)} async-done(((bf16[8,208,128]{2,1,0:T(8,128)(2,1)}), bf16[8,208,128]{2,1,0:T(8,128)(2,1)S(1)}, u32[]{:S(2)}, u32[]{:S(2)}) %all-to-all-start.4) | async-done | bytes 426016 | tf_op jit(solution)/shard_map/all_to_all | solution.py:23
  96.4 0.7 shard_map.134
  97.1 4.8 %all-to-all-start.5 = ((bf16[8,80,128]{2,1,0:T(8,128)(2,1)}), bf16[8,80,128]{2,1,0:T(8,128)(2,1)S(1)}, u32[]{:S(2)}, u32[]{:S(2)}) async-start(bf16[8,80,128]{2,1,0:T(8,128)(2,1)} %shard_map.134), calls=%async_computation.5 | async-start | bytes 327680 | tf_op jit(solution)/shard_map/all_to_all | solution.py:23
  101.9 2.1 %collective-permute-start = (bf16[2,4,256,128]{3,2,1,0:T(8,128)(2,1)S(1)}, bf16[2,4,256,128]{3,2,1,0:T(8,128)(2,1)S(1)}, u32[]{:S(2)}, u32[]{:S(2)}) collective-permute-start(bf16[2,4,256,128]{3,2,1,0:T(8,128)(2,1)S(1)} %get-tuple-element.42.own_ref), channel_id=1, source_target_pairs={{0,8},{8,0},{1,9},{9,1},{2,10},{10,2},{3,11},{11,3},{4,12},{12,4},... | collective-permute-start | bytes 1572872 | tf_op jit(solution)/shard_map/ppermute | solution.py:292
  104.1 11.1 %collective-permute-done.other_ref = bf16[2,4,256,128]{3,2,1,0:T(8,128)(2,1)S(1)} collective-permute-done((bf16[2,4,256,128]{3,2,1,0:T(8,128)(2,1)S(1)}, bf16[2,4,256,128]{3,2,1,0:T(8,128)(2,1)S(1)}, u32[]{:S(2)}, u32[]{:S(2)}) %collective-permute-start) | collective-permute-done | bytes 524320 | tf_op jit(solution)/shard_map/ppermute | solution.py:292
  115.1 1.9 %all-to-all-done.5.far_ref = bf16[8,80,128]{2,1,0:T(8,128)(2,1)S(1)} async-done(((bf16[8,80,128]{2,1,0:T(8,128)(2,1)}), bf16[8,80,128]{2,1,0:T(8,128)(2,1)S(1)}, u32[]{:S(2)}, u32[]{:S(2)}) %all-to-all-start.5) | async-done | bytes 163872 | tf_op jit(solution)/shard_map/all_to_all | solution.py:23
  117.1 2.8 %shard_map.135 = (bf16[8,80,128]{2,1,0:T(8,128)(2,1)S(1)}, bf16[8,64,128]{2,1,0:T(8,128)(2,1)S(1)}, f32[512]{0:T(512)}) custom-call(bf16[8,208,128]{2,1,0:T(8,128)(2,1)S(1)} %all-to-all-done.4.refs_0_.parts_ref, bf16[8,80,128]{2,1,0:T(8,128)(2,1)S(1)} %all-to-all-done.5.far_ref, bf16[2,4,256,128]{3,2,1,0:T(8,128)(2,1)S(1)} %get-tuple-element.42.own_ref, ...), custom_call_target="tpu_custom_call" | custom-call | flops 1000000 | bytes 1000000 | tf_op jit(solution)/shard_map/pallas_call | solution.py:154
  119.9 25.3 %all_to_all.43.refs_0_ = bf16[8,80,128]{2,1,0:T(8,128)(2,1)S(1)} all-to-all(bf16[8,80,128]{2,1,0:T(8,128)(2,1)S(1)} %get-tuple-element.43), channel_id=1, replica_groups=mesh['far'=8,'row'=2,'pair'=2,'side'=2,'head'=8] {'far'}, dimensions={0} | all-to-all | bytes 327680 | tf_op jit(solution)/shard_map/all_to_all | solution.py:23
  145.3 11.5 %all_to_all.44.refs_0_ = bf16[8,192,128]{2,1,0:T(8,128)(2,1)S(1)} all-to-all(bf16[8,192,128]{2,1,0:T(8,128)(2,1)S(1)} %shard_map.136), channel_id=1, replica_groups=mesh['far'=8,'row'=2,'pair'=2,'side'=2,'head'=8] {'row','pair','side'}, dimensions={0} | all-to-all | bytes 786432 | tf_op jit(solution)/shard_map/all_to_all | solution.py:23
  156.8 0.0 copy-done.12
  156.8 1.7 %shard_map.137 = (bf16[256,512]{1,0:T(8,128)(2,1)}, bf16[256,512]{1,0:T(8,128)(2,1)}, f32[4,128,128]{2,1,0:T(8,128)}, f32[4,128,128]{2,1,0:T(8,128)}) custom-call(bf16[8,192,128]{2,1,0:T(8,128)(2,1)S(1)} %all_to_all.44.refs_0_, bf16[256,512]{1,0:T(8,128)(2,1)S(1)} %get-tuple-element.45.refs_1_, bf16[256,512]{1,0:T(8,128)(2,1)S(1)} %get-tuple-element.46.refs_2_, ...), custom_call_target="tpu_custom_call" | custom-call | flops 100000000 | bytes 1000000 | tf_op jit(solution)/shard_map/pallas_call | solution.py:43
  (9 shorter events, 0.1 us)
Async XLA Ops:
  7.2 84.5 %all-gather.3.cloned.1.call-start = ((), (), s32[]{:S(2)}) async-start(), calls=%async_computation.8 | async-start | bytes 2621440 | tf_op jit(solution)/shard_map/all_gather | solution.py:111
  9.7 70.7 %copy-start.3 = (bf16[256,512]{1,0:T(8,128)(2,1)S(1)}, bf16[256,512]{1,0:T(8,128)(2,1)}, u32[]{:S(2)}) copy-start(bf16[256,512]{1,0:T(8,128)(2,1)} %get-tuple-element.30.refs_0_.refs_6_) | copy-start | bytes 786436
  9.7 70.7 %copy-start.4 = (bf16[4,128,128]{2,1,0:T(8,128)(2,1)S(1)}, bf16[4,128,128]{2,1,0:T(8,128)(2,1)}, u32[]{:S(2)}) copy-start(bf16[4,128,128]{2,1,0:T(8,128)(2,1)} %refs_4_.1) | copy-start | bytes 393220
  9.7 70.7 %copy-start.10 = (bf16[4,128,128]{2,1,0:T(8,128)(2,1)S(1)}, bf16[4,128,128]{2,1,0:T(8,128)(2,1)}, u32[]{:S(2)}) copy-start(bf16[4,128,128]{2,1,0:T(8,128)(2,1)} %refs_9_.3) | copy-start | bytes 393220
  9.8 70.7 %copy-start.1 = (bf16[256,512]{1,0:T(8,128)(2,1)S(1)}, bf16[256,512]{1,0:T(8,128)(2,1)}, u32[]{:S(2)}) copy-start(bf16[256,512]{1,0:T(8,128)(2,1)} %refs_3_.5) | copy-start | bytes 786436
  9.8 12.4 %all-to-all-start = ((bf16[8,64,128]{2,1,0:T(8,128)(2,1)}), bf16[8,64,128]{2,1,0:T(8,128)(2,1)S(1)}, u32[]{:S(2)}, u32[]{:S(2)}) async-start(bf16[8,64,128]{2,1,0:T(8,128)(2,1)} %get-tuple-element.32), calls=%async_computation | async-start | bytes 262144 | tf_op jit(solution)/shard_map/all_to_all | solution.py:23
  15.7 0.9 copy-start
  16.6 0.9 copy-start.2
  17.6 0.9 copy-start.5
  18.5 0.9 copy-start.9
  19.4 0.7 copy-start.13
  20.1 45.8 %copy-start.8 = (bf16[256,512]{1,0:T(8,128)(2,1)S(1)}, bf16[256,512]{1,0:T(8,128)(2,1)}, u32[]{:S(2)}) copy-start(bf16[256,512]{1,0:T(8,128)(2,1)} %refs_2_.7) | copy-start | bytes 786436
  20.1 60.4 %copy-start.6 = (bf16[256,512]{1,0:T(8,128)(2,1)S(1)}, bf16[256,512]{1,0:T(8,128)(2,1)}, u32[]{:S(2)}) copy-start(bf16[256,512]{1,0:T(8,128)(2,1)} %refs_8_.3) | copy-start | bytes 786436
  20.1 60.4 %copy-start.7 = (bf16[256,512]{1,0:T(8,128)(2,1)S(1)}, bf16[256,512]{1,0:T(8,128)(2,1)}, u32[]{:S(2)}) copy-start(bf16[256,512]{1,0:T(8,128)(2,1)} %refs_10_.3) | copy-start | bytes 786436
  84.1 12.3 %all-to-all-start.4 = ((bf16[8,208,128]{2,1,0:T(8,128)(2,1)}), bf16[8,208,128]{2,1,0:T(8,128)(2,1)S(1)}, u32[]{:S(2)}, u32[]{:S(2)}) async-start(bf16[8,208,128]{2,1,0:T(8,128)(2,1)} %shard_map.132), calls=%async_computation.4 | async-start | bytes 851968 | tf_op jit(solution)/shard_map/all_to_all | solution.py:23
  91.0 0.7 copy-start.11
  97.1 59.7 %copy-start.12 = (bf16[256,512]{1,0:T(8,128)(2,1)S(1)}, bf16[256,512]{1,0:T(8,128)(2,1)}, u32[]{:S(2)}) copy-start(bf16[256,512]{1,0:T(8,128)(2,1)} %copy-done.11) | copy-start | bytes 786436
  97.1 19.9 %all-to-all-start.5 = ((bf16[8,80,128]{2,1,0:T(8,128)(2,1)}), bf16[8,80,128]{2,1,0:T(8,128)(2,1)S(1)}, u32[]{:S(2)}, u32[]{:S(2)}) async-start(bf16[8,80,128]{2,1,0:T(8,128)(2,1)} %shard_map.134), calls=%async_computation.5 | async-start | bytes 327680 | tf_op jit(solution)/shard_map/all_to_all | solution.py:23
  101.9 13.2 %collective-permute-start = (bf16[2,4,256,128]{3,2,1,0:T(8,128)(2,1)S(1)}, bf16[2,4,256,128]{3,2,1,0:T(8,128)(2,1)S(1)}, u32[]{:S(2)}, u32[]{:S(2)}) collective-permute-start(bf16[2,4,256,128]{3,2,1,0:T(8,128)(2,1)S(1)} %get-tuple-element.42.own_ref), channel_id=1, source_target_pairs={{0,8},{8,0},{1,9},{9,1},{2,10},{10,2},{3,11},{11,3},{4,12},{12,4},... | collective-permute-start | bytes 1572872 | tf_op jit(solution)/shard_map/ppermute | solution.py:292
Sparse Core Ops, SparseCore 0:
  10.1 61.6 all-gather.2

commit v6 on v4

--- a/solution.py
+++ b/solution.py
@@ -14,7 +14,7 @@
 TOKEN = ((8, 128), F32)
 VMEM_BYTES = 24 * 1024 * 1024
 WHOLE_VMEM = 64 * 1024 * 1024
-MOST_VMEM = 52 * 1024 * 1024
+STATE_VMEM = 63 * 1024 * 1024
 
 
 def swap(x, axis):
@@ -75,9 +75,6 @@
     slim = chunk // far
     per_head = near // heads
     gain_row = norm_gain.reshape(1, width)
-    place = jnp.stack([lax.axis_index("far"), lax.axis_index("near")])
-    group_keys = lax.all_gather(key_rows, "near")
-    group_values = lax.all_gather(value_rows, "near")
     cols = [slice(h * size, (h + 1) * size) for h in range(heads)]
 
     def put_state(out_ref, h, value, row):
@@ -89,55 +86,108 @@
         parts = [ref[h * per_head + part] for part in range(per_head)]
         return jnp.concatenate(parts, axis=0)
 
-    def state_kernel(w_ref, k_ref, v_ref, kf_ref, out_ref, waits):
-        waits[0]()
-        waits[1]()
-        for h, at in enumerate(cols):
-            pre = dot(k_ref[:, at], w_ref[h], 1, 0)
+    def pack_kernel(k_ref, v_ref, out_ref, held_ref, in_sems, out_sems):
+        loads, stores = [], []
+        for h, at in enumerate(cols):
+            for i, ref in enumerate((k_ref, v_ref)):
+                room = held_ref.at[h, pl.ds(i * tokens, tokens), :]
+                loads.append(pltpu.make_async_copy(ref.at[:, at], room, in_sems.at[2 * h + i]))
+        for load in loads:
+            load.start()
+        for h in range(heads):
+            loads[2 * h].wait()
+            loads[2 * h + 1].wait()
+            for part in range(per_head):
+                place = h * per_head + part
+                store = pltpu.make_async_copy(held_ref.at[h], out_ref.at[place], out_sems.at[place])
+                store.start()
+                stores.append(store)
+        for store in stores:
+            store.wait()
+
+    whole = pl.BlockSpec(memory_space=pltpu.VMEM)
+    anywhere = pl.BlockSpec(memory_space=pl.ANY)
+    payload = pl.pallas_call(
+        pack_kernel,
+        out_shape=jax.ShapeDtypeStruct((near, 2 * tokens, size), BF),
+        in_specs=[anywhere, anywhere],
+        out_specs=anywhere,
+        scratch_shapes=[
+            pltpu.VMEM((heads, 2 * tokens, size), BF),
+            pltpu.SemaphoreType.DMA((2 * heads,)),
+            pltpu.SemaphoreType.DMA((near,)),
+        ],
+        compiler_params=pltpu.CompilerParams(vmem_limit_bytes=WHOLE_VMEM),
+        cost_estimate=pl.CostEstimate(flops=10**6, bytes_accessed=10**6, transcendentals=0),
+    )(key_rows, value_rows)
+    group_rows = swap(payload, "near")
+
+    def feature_kernel(k_ref, wk_ref, q_ref, wq_ref, kf_ref, qf_ref):
+        for h, at in enumerate(cols):
+            pre = dot(k_ref[:, at], wk_ref[h], 1, 0)
             kf_ref[:, at] = (pre / (1.0 + jnp.exp(-pre))).astype(BF)
-        waits[2]()
-        for h, at in enumerate(cols):
-            put_state(out_ref, h, dot(kf_ref[:, at], v_ref[:, at], 0, 0), 0)
-
-    key_feat, payload = run(
+            pre = dot(q_ref[:, at], wq_ref[h], 1, 0)
+            qf_ref[:, at] = (pre / (1.0 + jnp.exp(-pre))).astype(BF)
+
+    key_feat, query_feat = run(
+        feature_kernel,
+        [((tokens, width), BF), ((tokens, width), BF)],
+        [key_rows, feat_key, query_rows, feat_query],
+    )
+
+    def chunk_weights(wk_ref):
+        member = lax.axis_index("near")
+        weights = wk_ref[member // per_head]
+        part = member % per_head
+        mine = weights[:, :chunk]
+        for other in range(1, per_head):
+            mine = jnp.where(part == other, weights[:, other * chunk : (other + 1) * chunk], mine)
+        return mine
+
+    def state_kernel(
+        rows_ref, wk_ref, token_ref, parts_ref, slope_ref, out_ref, held_ref, wk_held, sems
+    ):
+        loads = [pltpu.make_async_copy(wk_ref, wk_held, sems.at[near])]
+        for i in range(near):
+            loads.append(pltpu.make_async_copy(rows_ref.at[i], held_ref.at[i], sems.at[i]))
+        for load in loads:
+            load.start()
+        loads[0].wait()
+        weights = chunk_weights(wk_held)
+        total = jnp.zeros((chunk, size), F32)
+        for i in range(near):
+            loads[i + 1].wait()
+            pre = dot(held_ref[i, :tokens], weights, 1, 0)
+            gate = 1.0 / (1.0 + jnp.exp(-pre))
+            slope_ref[i] = (gate * (1.0 + pre * (1.0 - gate))).astype(BF)
+            state = dot((pre * gate).astype(BF), held_ref[i, tokens:], 0, 0)
+            parts_ref[i] = state.astype(BF)
+            total = total + state
+        total = total.astype(BF)
+        for i in range(far):
+            out_ref[i] = total
+
+    parts, chunk_slope, payload = pl.pallas_call(
         state_kernel,
-        [((tokens, width), BF), ((near, chunk, size), BF)],
-        [],
-        fetch=[feat_key, key_rows, value_rows],
-        limit=WHOLE_VMEM,
-    )
-    parts = swap(payload, "near")
-
-    def query_kernel(kf_ref, wq_ref, q_ref, v_ref, gain_ref, qf_ref, intra_ref, gain_out):
-        gain_out[...] = gain_ref[...]
-        mask = causal_mask(tokens)
-        for h, at in enumerate(cols):
-            pre = dot(q_ref[:, at], wq_ref[h], 1, 0)
-            feat = (pre / (1.0 + jnp.exp(-pre))).astype(BF)
-            qf_ref[:, at] = feat
-            scores = jnp.where(mask, dot(feat, kf_ref[:, at], 1, 1), 0.0).astype(BF)
-            intra_ref[:, at] = dot(scores, v_ref[:, at], 1, 0)
-
-    query_feat, intra, gain_row = run(
-        query_kernel,
-        [((tokens, width), BF), ((tokens, width), F32), ((1, width), F32)],
-        [key_feat, feat_query, query_rows, value_rows, gain_row],
-        after=[place],
-    )
-
-    def total_kernel(in_ref, out_ref):
-        total = in_ref[0].astype(F32)
-        for i in range(1, near):
-            total = total + in_ref[i].astype(F32)
-        total = total.astype(BF)
-        for i in range(out_ref.shape[0]):
-            out_ref[i] = total
-
-    (payload,) = run(total_kernel, [((far, chunk, size), BF)], [parts], after=[query_feat])
+        out_shape=[
+            jax.ShapeDtypeStruct((near, chunk, size), BF),
+            jax.ShapeDtypeStruct((near, tokens, chunk), BF),
+            jax.ShapeDtypeStruct((far, chunk, size), BF),
+        ],
+        in_specs=[anywhere, anywhere, anywhere],
+        out_specs=[whole] * 3,
+        scratch_shapes=[
+            pltpu.VMEM((near, 2 * tokens, size), BF),
+            pltpu.VMEM(feat_key.shape, BF),
+            pltpu.SemaphoreType.DMA((near + 1,)),
+        ],
+        compiler_params=pltpu.CompilerParams(vmem_limit_bytes=STATE_VMEM),
+        cost_estimate=pl.CostEstimate(flops=10**8, bytes_accessed=10**6, transcendentals=0),
+    )(group_rows, feat_key, query_feat)
     parts_far = swap(payload, "far")
 
-    def join(parts_ref, far_ref, place_ref, out_ref, backward):
-        place = place_ref[0]
+    def join(parts_ref, far_ref, out_ref, backward):
+        place = lax.axis_index("far")
         state = jnp.zeros((chunk, size), F32)
         for i in range(far):
             keep = (i > place) if backward else (i < place)
@@ -146,31 +196,25 @@
             out_ref[i] = state.astype(BF)
             state = state + parts_ref[i][:chunk].astype(F32)
 
-    def run_join(kernel, outs, ins):
-        whole = pl.BlockSpec(memory_space=pltpu.VMEM)
-        return pl.pallas_call(
-            kernel,
-            out_shape=[jax.ShapeDtypeStruct(shape, dtype) for shape, dtype in outs],
-            in_specs=[whole] * (len(ins) - 1) + [pl.BlockSpec(memory_space=pltpu.SMEM)],
-            out_specs=[whole] * len(outs),
-            compiler_params=pltpu.CompilerParams(vmem_limit_bytes=VMEM_BYTES),
-            cost_estimate=pl.CostEstimate(flops=10**6, bytes_accessed=10**6, transcendentals=0),
-        )(*ins)
-
-    def prior_kernel(parts_ref, far_ref, place_ref, out_ref):
-        join(parts_ref, far_ref, place_ref, out_ref, False)
-
-    (payload,) = run_join(prior_kernel, [((near, chunk, size), BF)], [parts, parts_far, place])
+    def prior_kernel(parts_ref, far_ref, out_ref):
+        join(parts_ref, far_ref, out_ref, False)
+
+    (payload,) = run(prior_kernel, [((near, chunk, size), BF)], [parts, parts_far])
     prior = swap(payload, "near")
 
-    def norm_kernel(qf_ref, p_ref, intra_ref, go_ref, gain_ref, pre_ref, out_ref):
+    def norm_kernel(qf_ref, kf_ref, v_ref, p_ref, go_ref, gain_ref, pre_ref, gain_out, out_ref, waits):
+        mask = causal_mask(tokens)
         squares = jnp.zeros((tokens, size), F32)
         inner = jnp.zeros((tokens, size), F32)
         for h, at in enumerate(cols):
-            pre = intra_ref[:, at] + dot(qf_ref[:, at], get_state(p_ref, h), 1, 0)
+            scores = jnp.where(mask, dot(qf_ref[:, at], kf_ref[:, at], 1, 1), 0.0).astype(BF)
+            pre = dot(scores, v_ref[:, at], 1, 0) + dot(qf_ref[:, at], get_state(p_ref, h), 1, 0)
             pre_ref[:, at] = pre
             squares = squares + pre * pre
+            if h == 0:
+                waits[0]()
             inner = inner + go_ref[:, at].astype(F32) * gain_ref[:, at] * pre
+        gain_out[...] = gain_ref[...]
         squares = jnp.sum(squares, axis=1, keepdims=True)
         inner = jnp.sum(inner, axis=1, keepdims=True)
         lane = lax.broadcasted_iota(jnp.int32, (tokens, size), 1)
@@ -180,10 +224,11 @@
             out_ref[i] = rows
 
     peers = lax.axis_size("head")
-    pre_norm, payload = run(
+    pre_norm, gain_row, payload = run(
         norm_kernel,
-        [((tokens, width), F32), ((peers, STAT_ROWS, tokens), F32)],
-        [query_feat, prior, intra, grad_out, gain_row],
+        [((tokens, width), F32), ((1, width), F32), ((peers, STAT_ROWS, tokens), F32)],
+        [query_feat, key_feat, value_rows, prior, grad_out],
+        fetch=[gain_row],
     )
     stats = swap(payload, "head")
 
@@ -259,45 +304,6 @@
         ],
     )
 
-    def chunk_kernel(place_ref, wk_ref, keys_ref, values_ref, token_in, k_ref, v_ref, slope_ref, token_ref, sems):
-        head = place_ref[1] // per_head
-        at = pl.ds(pl.multiple_of(head * size, size), size)
-        moves = [
-            pltpu.make_async_copy(keys_ref.at[:, :, at], k_ref, sems.at[0]),
-            pltpu.make_async_copy(values_ref.at[:, :, at], v_ref, sems.at[1]),
-        ]
-        for move in moves:
-            move.start()
-        token_ref[...] = jnp.zeros(token_ref.shape, F32)
-        weights = wk_ref[head]
-        part = place_ref[1] % per_head
-        moves[0].wait()
-        for i in range(near):
-            slope = silu_slope(dot(k_ref[i], weights, 1, 0))
-            mine = slope[:, :chunk]
-            for other in range(1, per_head):
-                mine = jnp.where(part == other, slope[:, other * chunk : (other + 1) * chunk], mine)
-            slope_ref[i] = mine.astype(BF)
-        moves[1].wait()
-
-    whole = pl.BlockSpec(memory_space=pltpu.VMEM)
-    anywhere = pl.BlockSpec(memory_space=pl.ANY)
-    scalars = pl.BlockSpec(memory_space=pltpu.SMEM)
-    chunk_keys, chunk_values, chunk_slope, token = pl.pallas_call(
-        chunk_kernel,
-        out_shape=[
-            jax.ShapeDtypeStruct((near, tokens, size), BF),
-            jax.ShapeDtypeStruct((near, tokens, size), BF),
-            jax.ShapeDtypeStruct((near, tokens, chunk), BF),
-            jax.ShapeDtypeStruct(*TOKEN),
-        ],
-        in_specs=[scalars, whole, anywhere, anywhere, anywhere],
-        out_specs=[whole] * 4,
-        scratch_shapes=[pltpu.SemaphoreType.DMA((2,))],
-        compiler_params=pltpu.CompilerParams(vmem_limit_bytes=MOST_VMEM),
-        cost_estimate=pl.CostEstimate(flops=10**8, bytes_accessed=10**6, transcendentals=0),
-    )(place, feat_key, group_keys, group_values, token)
-
     def back_total_kernel(in_ref, out_ref):
         total = in_ref[0].astype(F32)
         for i in range(1, near):
@@ -312,8 +318,8 @@
     )
     parts_far = swap(payload, "far")
 
-    def later_kernel(parts_ref, far_ref, k_ref, v_ref, slope_ref, place_ref, out_ref, later_ref, gain_ref):
-        join(parts_ref, far_ref, place_ref, later_ref, True)
+    def later_kernel(parts_ref, far_ref, rows_ref, slope_ref, out_ref, later_ref, gain_ref):
+        join(parts_ref, far_ref, later_ref, True)
         side = far_ref[0].astype(F32)[chunk:]
         for i in range(1, far):
             side = side + far_ref[i].astype(F32)[chunk:]
@@ -321,18 +327,18 @@
             gain_ref[h * size : (h + 1) * size] = side[slim + h]
         total = jnp.zeros((chunk, size), F32)
         for i in range(near):
-            grad = dot(v_ref[i], later_ref[i], 1, 1) * slope_ref[i].astype(F32)
-            total = total + dot(grad.astype(BF), k_ref[i], 0, 0)
+            grad = dot(rows_ref[i, tokens:], later_ref[i], 1, 1) * slope_ref[i].astype(F32)
+            total = total + dot(grad.astype(BF), rows_ref[i, :tokens], 0, 0)
             total = total + parts_ref[i].astype(F32)[2 * chunk : 3 * chunk]
         pad = jnp.zeros((8, size), F32)
         total = jnp.concatenate([total, side[:slim], pad], axis=0).astype(BF)
         for i in range(far):
             out_ref[i] = total
 
-    payload, later, grad_gain = run_join(
+    payload, later, grad_gain = run(
         later_kernel,
         [((far, chunk + slim + 8, size), BF), ((near, chunk, size), BF), ((width,), F32)],
-        [parts, parts_far, chunk_keys, chunk_values, chunk_slope, place],
+        [parts, parts_far, group_rows, chunk_slope],
     )
     parts_far = swap(payload, "far")
 

time: 189 us -> 151 us (0.80)
  the two profiles are of different devices: /device:TPU:8 before, /device:TPU:2 now
where the time goes in v6:
time: 151 us; the launch traced here: 150 us
  blocking collectives  98.7 us (65%)
  Pallas kernels  20.6 us (14%)
  starting transfers between devices  15.1 us (10%)
  waiting for transfers between devices  11.1 us (7%)
  local copies, waits for them, and re-layouts  3.74 us (2%)
    all_to_all x6, blocking collectives, swap(): return lax.all_to_all(x, axis, 0, 0)  98.7 us
    all_to_all x2, starting transfers between devices, swap(): return lax.all_to_all(x, axis, 0, 0)  15.1 us
    pallas_call x9, Pallas kernels, run(): pl.pallas_call(body, out_shape=[jax.ShapeDtypeStruct(shape, dtype) for sh...  13.8 us
    all_to_all x2, waiting for transfers between devices, swap(): return lax.all_to_all(x, axis, 0, 0)  11.1 us
    pallas_call x1, Pallas kernels, shards(): pl.pallas_call(state_kernel, out_shape=[jax.ShapeDtypeStruct((near, chunk...  4.74 us
    unnamed x34, local copies, waits for them, and re-layouts  3.74 us
  transfers between devices with their start and end apart: 2, of which 2 were waited for; matrix products, arithmetic and copies ran while one was open for 0% of the time, Pallas kernels for 3%

profile of v6, /device:TPU:2, one launch (start us, length us, event | category | flops | bytes accessed | tf_op | source)
XLA Modules:
  0.0 150.0 jit_solution(3793758173596986306)
XLA Ops:
  0.6 2.0 %shard_map.127 = bf16[8,512,128]{2,1,0:T(8,128)(2,1)} custom-call(bf16[256,512]{1,0:T(8,128)(2,1)} %refs_10_.3, bf16[256,512]{1,0:T(8,128)(2,1)} %refs_3_.3), custom_call_target="tpu_custom_call" | custom-call | flops 1000000 | bytes 1000000 | tf_op jit(solution)/shard_map/pallas_call | solution.py:110
  2.6 0.0 copy-start.1
  2.6 0.0 copy-start.4
  2.6 0.0 copy-start.6
  2.7 0.0 copy-start.8
  2.7 10.2 %all-to-all-start = ((bf16[8,512,128]{2,1,0:T(8,128)(2,1)}), bf16[8,512,128]{2,1,0:T(8,128)(2,1)}, u32[]{:S(2)}, u32[]{:S(2)}) async-start(bf16[8,512,128]{2,1,0:T(8,128)(2,1)} %shard_map.127), calls=%async_computation | async-start | bytes 2097152 | tf_op jit(solution)/shard_map/all_to_all | solution.py:21
  12.8 0.0 copy-done.1
  12.8 0.0 copy-done.4
  12.8 0.0 copy-done.6
  12.9 0.0 copy-done.8
  12.9 0.4 shard_map.126
  13.3 0.0 copy-start.2
  13.3 0.7 copy-done.2
  14.0 8.7 %all-to-all-done.rows_ref.refs_2_ = bf16[8,512,128]{2,1,0:T(8,128)(2,1)} async-done(((bf16[8,512,128]{2,1,0:T(8,128)(2,1)}), bf16[8,512,128]{2,1,0:T(8,128)(2,1)}, u32[]{:S(2)}, u32[]{:S(2)}) %all-to-all-start) | async-done | bytes 1048608 | tf_op jit(solution)/shard_map/all_to_all | solution.py:21
  22.7 4.7 %shard_map.128 = (bf16[8,64,128]{2,1,0:T(8,128)(2,1)}, bf16[8,256,64]{2,1,0:T(8,128)(2,1)}, bf16[8,64,128]{2,1,0:T(8,128)(2,1)}) custom-call(bf16[8,512,128]{2,1,0:T(8,128)(2,1)} %all-to-all-done.rows_ref.refs_2_, bf16[4,128,128]{2,1,0:T(8,128)(2,1)} %refs_4_.3, bf16[256,512]{1,0:T(8,128)(2,1)} %copy-done.2), custom_call_target="tpu_custom_call" | custom-call | flops 100000000 | bytes 1000000 | tf_op jit(solution)/shard_map/pallas_call | solution.py:170
  27.5 0.0 copy-start.7
  27.5 30.0 %all_to_all.40.refs_1_ = bf16[8,64,128]{2,1,0:T(8,128)(2,1)S(1)} all-to-all(bf16[8,64,128]{2,1,0:T(8,128)(2,1)} %get-tuple-element.31), channel_id=1, replica_groups=mesh['far'=8,'near'=8,'head'=8] {'far'}, dimensions={0} | all-to-all | bytes 262144 | tf_op jit(solution)/shard_map/all_to_all | solution.py:21
  57.5 0.0 copy-start.15
  57.5 0.9 copy-done.15
  58.4 0.0 copy-start
  58.4 0.0 copy-start.3
  58.4 0.1 shard_map.129
  58.5 9.5 %all_to_all.41.refs_3_.refs_7_ = bf16[8,64,128]{2,1,0:T(8,128)(2,1)S(1)} all-to-all(bf16[8,64,128]{2,1,0:T(8,128)(2,1)S(1)} %shard_map.129), channel_id=1, replica_groups=mesh['far'=8,'near'=8,'head'=8] {'near'}, dimensions={0} | all-to-all | bytes 262144 | tf_op jit(solution)/shard_map/all_to_all | solution.py:21
  67.9 0.0 copy-done.7
  67.9 0.0 copy-done
  67.9 0.0 copy-done.3
  67.9 0.7 copy-done.16
  68.6 1.1 shard_map.130
  69.7 0.0 copy-start.5
  69.7 10.0 %all_to_all.42.refs_0_ = f32[8,8,256]{2,1,0:T(8,128)S(1)} all-to-all(f32[8,8,256]{2,1,0:T(8,128)S(1)} %get-tuple-element.32), channel_id=1, replica_groups=mesh['far'=8,'near'=8,'head'=8] {'head'}, dimensions={0} | all-to-all | bytes 131072 | tf_op jit(solution)/shard_map/all_to_all | solution.py:21
  79.7 0.0 copy-done.9
  79.7 0.0 copy-done.5
  79.7 3.7 %shard_map.132 = bf16[8,208,128]{2,1,0:T(8,128)(2,1)} custom-call(f32[8,8,256]{2,1,0:T(8,128)S(1)} %all_to_all.42.refs_0_, f32[256,512]{1,0:T(8,128)S(1)} %get-tuple-element.33.refs_1_, bf16[256,512]{1,0:T(8,128)(2,1)S(1)} %copy-done.7, f32[1,512]{1,0:T(1,128)S(1)} %get-tuple-element.34.refs_3_, bf16[256,512]{1,0:T(8,128)(2,1)S(1)} %copy-done.3, ...), custom_call_target="tpu_custom_call" | custom-call | flops 100000000 | bytes 1000000 | tf_op jit(solution)/shard_map/pallas_call | solution.py:41
  83.4 4.9 %all-to-all-start.4 = ((bf16[8,208,128]{2,1,0:T(8,128)(2,1)}), bf16[8,208,128]{2,1,0:T(8,128)(2,1)S(1)}, u32[]{:S(2)}, u32[]{:S(2)}) async-start(bf16[8,208,128]{2,1,0:T(8,128)(2,1)} %shard_map.132), calls=%async_computation.4 | async-start | bytes 851968 | tf_op jit(solution)/shard_map/all_to_all | solution.py:21
  88.3 3.3 %shard_map.131 = (bf16[256,512]{1,0:T(8,128)(2,1)}, bf16[256,512]{1,0:T(8,128)(2,1)}, bf16[256,512]{1,0:T(8,128)(2,1)S(1)}, bf16[256,512]{1,0:T(8,128)(2,1)S(1)}...) custom-call(f32[8,8,256]{2,1,0:T(8,128)S(1)} %all_to_all.42.refs_0_, f32[256,512]{1,0:T(8,128)S(1)} %get-tuple-element.33.refs_1_, ...), custom_call_target="tpu_custom_call" | custom-call | flops 100000000 | bytes 1000000 | tf_op jit(solution)/shard_map/pallas_call | solution.py:41
  91.7 0.7 copy-done.11
  92.4 0.7 copy-done.13
  93.1 2.4 %all-to-all-done.4.refs_0_ = bf16[8,208,128]{2,1,0:T(8,128)(2,1)S(1)} async-done(((bf16[8,208,128]{2,1,0:T(8,128)(2,1)}), bf16[8,208,128]{2,1,0:T(8,128)(2,1)S(1)}, u32[]{:S(2)}, u32[]{:S(2)}) %all-to-all-start.4) | async-done | bytes 426016 | tf_op jit(solution)/shard_map/all_to_all | solution.py:21
  95.5 18.8 %all_to_all.43.refs_1_ = bf16[8,80,128]{2,1,0:T(8,128)(2,1)S(1)} all-to-all(bf16[8,80,128]{2,1,0:T(8,128)(2,1)S(1)} %shard_map.133), channel_id=1, replica_groups=mesh['far'=8,'near'=8,'head'=8] {'far'}, dimensions={0} | all-to-all | bytes 327680 | tf_op jit(solution)/shard_map/all_to_all | solution.py:21
  114.3 0.0 copy-done.10
  114.3 3.5 %shard_map.134 = (bf16[8,80,128]{2,1,0:T(8,128)(2,1)S(1)}, bf16[8,64,128]{2,1,0:T(8,128)(2,1)S(1)}, f32[512]{0:T(512)}) custom-call(bf16[8,208,128]{2,1,0:T(8,128)(2,1)S(1)} %all-to-all-done.4.refs_0_, bf16[8,80,128]{2,1,0:T(8,128)(2,1)S(1)} %all_to_all.43.refs_1_, bf16[8,512,128]{2,1,0:T(8,128)(2,1)} %all-to-all-done.rows_ref.refs_2_, ...), custom_call_target="tpu_custom_call" | custom-call | flops 100000000 | bytes 1000000 | tf_op jit(solution)/shard_map/pallas_call | solution.py:41
  117.8 18.0 %all_to_all.44.refs_0_ = bf16[8,80,128]{2,1,0:T(8,128)(2,1)S(1)} all-to-all(bf16[8,80,128]{2,1,0:T(8,128)(2,1)S(1)} %get-tuple-element.39), channel_id=1, replica_groups=mesh['far'=8,'near'=8,'head'=8] {'far'}, dimensions={0} | all-to-all | bytes 327680 | tf_op jit(solution)/shard_map/all_to_all | solution.py:21
  135.9 0.0 copy-start.12
  135.9 0.0 copy-start.14
  135.9 12.4 %all_to_all.45.refs_0_ = bf16[8,192,128]{2,1,0:T(8,128)(2,1)S(1)} all-to-all(bf16[8,192,128]{2,1,0:T(8,128)(2,1)S(1)} %shard_map.135), channel_id=1, replica_groups=mesh['far'=8,'near'=8,'head'=8] {'near'}, dimensions={0} | all-to-all | bytes 786432 | tf_op jit(solution)/shard_map/all_to_all | solution.py:21
  148.4 0.0 copy-done.12
  148.4 0.0 copy-done.14
  148.4 1.7 %shard_map.136 = (bf16[256,512]{1,0:T(8,128)(2,1)}, bf16[256,512]{1,0:T(8,128)(2,1)}, f32[4,128,128]{2,1,0:T(8,128)}, f32[4,128,128]{2,1,0:T(8,128)}) custom-call(bf16[8,192,128]{2,1,0:T(8,128)(2,1)S(1)} %all_to_all.45.refs_0_, bf16[256,512]{1,0:T(8,128)(2,1)S(1)} %get-tuple-element.41.refs_1_, bf16[256,512]{1,0:T(8,128)(2,1)S(1)} %copy-done.12, ...), custom_call_target="tpu_custom_call" | custom-call | flops 100000000 | bytes 1000000 | tf_op jit(solution)/shard_map/pallas_call | solution.py:41
  (7 shorter events, 0.1 us)
Async XLA Ops:
  2.6 10.2 %copy-start.1 = (bf16[256,512]{1,0:T(8,128)(2,1)S(1)}, bf16[256,512]{1,0:T(8,128)(2,1)}, u32[]{:S(2)}) copy-start(bf16[256,512]{1,0:T(8,128)(2,1)} %refs_10_.3) | copy-start | bytes 786436
  2.6 10.2 %copy-start.4 = (bf16[4,128,128]{2,1,0:T(8,128)(2,1)S(1)}, bf16[4,128,128]{2,1,0:T(8,128)(2,1)}, u32[]{:S(2)}) copy-start(bf16[4,128,128]{2,1,0:T(8,128)(2,1)} %refs_4_.3) | copy-start | bytes 393220
  2.6 10.2 %copy-start.6 = (bf16[256,512]{1,0:T(8,128)(2,1)S(1)}, bf16[256,512]{1,0:T(8,128)(2,1)}, u32[]{:S(2)}) copy-start(bf16[256,512]{1,0:T(8,128)(2,1)} %refs_8_.3) | copy-start | bytes 786436
  2.7 10.2 %copy-start.8 = (bf16[4,128,128]{2,1,0:T(8,128)(2,1)S(1)}, bf16[4,128,128]{2,1,0:T(8,128)(2,1)}, u32[]{:S(2)}) copy-start(bf16[4,128,128]{2,1,0:T(8,128)(2,1)} %refs_9_.3) | copy-start | bytes 393220
  2.7 20.1 %all-to-all-start = ((bf16[8,512,128]{2,1,0:T(8,128)(2,1)}), bf16[8,512,128]{2,1,0:T(8,128)(2,1)}, u32[]{:S(2)}, u32[]{:S(2)}) async-start(bf16[8,512,128]{2,1,0:T(8,128)(2,1)} %shard_map.127), calls=%async_computation | async-start | bytes 2097152 | tf_op jit(solution)/shard_map/all_to_all | solution.py:21
  13.3 0.7 copy-start.2
  27.5 40.4 %copy-start.7 = (bf16[256,512]{1,0:T(8,128)(2,1)S(1)}, bf16[256,512]{1,0:T(8,128)(2,1)}, u32[]{:S(2)}) copy-start(bf16[256,512]{1,0:T(8,128)(2,1)} %refs_2_.7) | copy-start | bytes 786436
  57.5 0.9 copy-start.15
  58.4 9.5 %copy-start = (bf16[256,512]{1,0:T(8,128)(2,1)S(1)}, bf16[256,512]{1,0:T(8,128)(2,1)}, u32[]{:S(2)}) copy-start(bf16[256,512]{1,0:T(8,128)(2,1)} %refs_3_.3) | copy-start | bytes 786436
  58.4 9.5 %copy-start.3 = (bf16[256,512]{1,0:T(8,128)(2,1)S(1)}, bf16[256,512]{1,0:T(8,128)(2,1)}, u32[]{:S(2)}) copy-start(bf16[256,512]{1,0:T(8,128)(2,1)} %copy-done.2) | copy-start | bytes 786436
  67.9 0.7 copy-start.16
  68.6 11.1 %copy-start.9 = (bf16[4,128,128]{2,1,0:T(8,128)(2,1)S(1)}, bf16[4,128,128]{2,1,0:T(8,128)(2,1)}, u32[]{:S(2)}) copy-start(bf16[4,128,128]{2,1,0:T(8,128)(2,1)} %refs_9_.3) | copy-start | bytes 393220
  69.7 10.0 %copy-start.5 = (bf16[4,128,128]{2,1,0:T(8,128)(2,1)S(1)}, bf16[4,128,128]{2,1,0:T(8,128)(2,1)}, u32[]{:S(2)}) copy-start(bf16[4,128,128]{2,1,0:T(8,128)(2,1)} %refs_4_.3) | copy-start | bytes 393220
  83.4 12.0 %all-to-all-start.4 = ((bf16[8,208,128]{2,1,0:T(8,128)(2,1)}), bf16[8,208,128]{2,1,0:T(8,128)(2,1)S(1)}, u32[]{:S(2)}, u32[]{:S(2)}) async-start(bf16[8,208,128]{2,1,0:T(8,128)(2,1)} %shard_map.132), calls=%async_computation.4 | async-start | bytes 851968 | tf_op jit(solution)/shard_map/all_to_all | solution.py:21
  91.7 0.7 copy-start.11
  92.4 0.7 copy-start.13
  93.1 21.3 %copy-start.10 = (bf16[8,256,64]{2,1,0:T(8,128)(2,1)S(1)}, bf16[8,256,64]{2,1,0:T(8,128)(2,1)}, u32[]{:S(2)}) copy-start(bf16[8,256,64]{2,1,0:T(8,128)(2,1)} %get-tuple-element.38.refs_3_) | copy-start | bytes 786436
  135.9 12.4 %copy-start.12 = (bf16[256,512]{1,0:T(8,128)(2,1)S(1)}, bf16[256,512]{1,0:T(8,128)(2,1)}, u32[]{:S(2)}) copy-start(bf16[256,512]{1,0:T(8,128)(2,1)} %copy-done.11) | copy-start | bytes 786436
  135.9 12.4 %copy-start.14 = (bf16[256,512]{1,0:T(8,128)(2,1)S(1)}, bf16[256,512]{1,0:T(8,128)(2,1)}, u32[]{:S(2)}) copy-start(bf16[256,512]{1,0:T(8,128)(2,1)} %copy-done.13) | copy-start | bytes 786436

commit v7 on v6

--- a/solution.py
+++ b/solution.py
@@ -60,9 +60,9 @@
     return g * (1.0 + x * (1.0 - g))
 
 
-def causal_mask(count):
-    rows = lax.broadcasted_iota(jnp.int32, (count, count), 0)
-    cols = lax.broadcasted_iota(jnp.int32, (count, count), 1)
+def causal_mask(count, later=0):
+    rows = lax.broadcasted_iota(jnp.int32, (count, count), later)
+    cols = lax.broadcasted_iota(jnp.int32, (count, count), 1 - later)
     return rows >= cols
 
 
@@ -137,12 +137,12 @@
 
     def chunk_weights(wk_ref):
         member = lax.axis_index("near")
-        weights = wk_ref[member // per_head]
+        weights = jnp.transpose(wk_ref[member // per_head].astype(F32))
         part = member % per_head
-        mine = weights[:, :chunk]
+        mine = weights[:chunk]
         for other in range(1, per_head):
-            mine = jnp.where(part == other, weights[:, other * chunk : (other + 1) * chunk], mine)
-        return mine
+            mine = jnp.where(part == other, weights[other * chunk : (other + 1) * chunk], mine)
+        return mine.astype(BF)
 
     def state_kernel(
         rows_ref, wk_ref, token_ref, parts_ref, slope_ref, out_ref, held_ref, wk_held, sems
@@ -157,10 +157,10 @@
         total = jnp.zeros((chunk, size), F32)
         for i in range(near):
             loads[i + 1].wait()
-            pre = dot(held_ref[i, :tokens], weights, 1, 0)
+            pre = dot(weights, held_ref[i, :tokens], 1, 1)
             gate = 1.0 / (1.0 + jnp.exp(-pre))
             slope_ref[i] = (gate * (1.0 + pre * (1.0 - gate))).astype(BF)
-            state = dot((pre * gate).astype(BF), held_ref[i, tokens:], 0, 0)
+            state = dot((pre * gate).astype(BF), held_ref[i, tokens:], 1, 0)
             parts_ref[i] = state.astype(BF)
             total = total + state
         total = total.astype(BF)
@@ -171,7 +171,7 @@
         state_kernel,
         out_shape=[
             jax.ShapeDtypeStruct((near, chunk, size), BF),
-            jax.ShapeDtypeStruct((near, tokens, chunk), BF),
+            jax.ShapeDtypeStruct((near, chunk, tokens), BF),
             jax.ShapeDtypeStruct((far, chunk, size), BF),
         ],
         in_specs=[anywhere, anywhere, anywhere],
@@ -249,19 +249,23 @@
     def query_side(h, at, delta, mask, v_ref, kf_ref, p_ref, q_ref, wq_ref):
         back = jnp.where(mask, dot(delta, v_ref[:, at], 1, 1), 0.0).astype(BF)
         grad = dot(back, kf_ref[:, at], 1, 0) + dot(delta, get_state(p_ref, h), 1, 1)
-        return back, (grad * silu_slope(dot(q_ref[:, at], wq_ref[h], 1, 0))).astype(BF)
+        return (grad * silu_slope(dot(q_ref[:, at], wq_ref[h], 1, 0))).astype(BF)
+
+    def key_side(at, delta, mask, v_ref, qf_ref):
+        back = jnp.where(mask, dot(v_ref[:, at], delta, 1, 1), 0.0).astype(BF)
+        return dot(back, qf_ref[:, at], 1, 0)
 
     def delta_kernel(st_ref, pre_ref, go_ref, gain_ref, qf_ref, v_ref, kf_ref, p_ref, q_ref, wq_ref, k_ref, wk_ref, out_ref):
         inverse, slope = row_factors(st_ref)
-        mask = causal_mask(tokens)
+        mask, turned = causal_mask(tokens), causal_mask(tokens, 1)
         gains = []
         for h, at in enumerate(cols):
             delta, wide, normed = delta_of(at, inverse, slope, pre_ref, go_ref, gain_ref)
             gains.append(jnp.sum(wide * normed, axis=0, keepdims=True))
             put_state(out_ref, h, dot(qf_ref[:, at], delta, 0, 0), 0)
-            back, grad = query_side(h, at, delta, mask, v_ref, kf_ref, p_ref, q_ref, wq_ref)
+            grad = query_side(h, at, delta, mask, v_ref, kf_ref, p_ref, q_ref, wq_ref)
             put_state(out_ref, h, dot(q_ref[:, at], grad, 0, 0), chunk)
-            grad = dot(back, qf_ref[:, at], 0, 0) * silu_slope(dot(k_ref[:, at], wk_ref[h], 1, 0))
+            grad = key_side(at, delta, turned, v_ref, qf_ref) * silu_slope(dot(k_ref[:, at], wk_ref[h], 1, 0))
             put_state(out_ref, h, dot(grad.astype(BF), k_ref[:, at], 0, 0), 2 * chunk)
         rest = [jnp.zeros((GAIN_ROWS - heads, size), F32)]
         rows = jnp.concatenate(gains + rest, axis=0).astype(BF)
@@ -284,16 +288,16 @@
     ):
         token_ref[...] = jnp.zeros(token_ref.shape, F32)
         inverse, slope = row_factors(st_ref)
-        mask = causal_mask(tokens)
+        mask, turned = causal_mask(tokens), causal_mask(tokens, 1)
         for h, at in enumerate(cols):
             delta, _, normed = delta_of(at, inverse, slope, pre_ref, go_ref, gain_ref)
             att_ref[:, at] = (normed * gain_ref[:, at]).astype(BF)
-            back, grad = query_side(h, at, delta, mask, v_ref, kf_ref, p_ref, q_ref, wq_ref)
+            grad = query_side(h, at, delta, mask, v_ref, kf_ref, p_ref, q_ref, wq_ref)
             gq_ref[:, at] = dot(grad, wq_ref[h], 1, 1).astype(BF)
-            kg_ref[:, at] = dot(back, qf_ref[:, at], 0, 0).astype(BF)
+            kg_ref[:, at] = key_side(at, delta, turned, v_ref, qf_ref).astype(BF)
             ks_ref[:, at] = silu_slope(dot(k_ref[:, at], wk_ref[h], 1, 0)).astype(BF)
-            scores = jnp.where(mask, dot(qf_ref[:, at], kf_ref[:, at], 1, 1), 0.0).astype(BF)
-            gv_ref[:, at] = dot(scores, delta, 0, 0).astype(BF)
+            scores = jnp.where(turned, dot(kf_ref[:, at], qf_ref[:, at], 1, 1), 0.0).astype(BF)
+            gv_ref[:, at] = dot(scores, delta, 1, 0).astype(BF)
 
     attended, grad_query, key_grad_local, key_slope, grad_value_local, token = run(
         local_kernel,
@@ -327,8 +331,8 @@
             gain_ref[h * size : (h + 1) * size] = side[slim + h]
         total = jnp.zeros((chunk, size), F32)
         for i in range(near):
-            grad = dot(rows_ref[i, tokens:], later_ref[i], 1, 1) * slope_ref[i].astype(F32)
-            total = total + dot(grad.astype(BF), rows_ref[i, :tokens], 0, 0)
+            grad = dot(later_ref[i], rows_ref[i, tokens:], 1, 1) * slope_ref[i].astype(F32)
+            total = total + dot(grad.astype(BF), rows_ref[i, :tokens], 1, 0)
             total = total + parts_ref[i].astype(F32)[2 * chunk : 3 * chunk]
         pad = jnp.zeros((8, size), F32)
         total = jnp.concatenate([total, side[:slim], pad], axis=0).astype(BF)

time: 151 us -> 150 us (level)
  the two profiles are of different devices: /device:TPU:2 before, /device:TPU:8 now
where the time goes in v7:
time: 150 us; the launch traced here: 149 us
  blocking collectives  98 us (65%)
  Pallas kernels  19.2 us (13%)
  waiting for transfers between devices  18.2 us (12%)
  starting transfers between devices  9.26 us (6%)
  local copies, waits for them, and re-layouts  3.74 us (2%)
    all_to_all x6, blocking collectives, swap(): return lax.all_to_all(x, axis, 0, 0)  98 us
    all_to_all x2, waiting for transfers between devices, swap(): return lax.all_to_all(x, axis, 0, 0)  18.2 us
    pallas_call x9, Pallas kernels, run(): pl.pallas_call(body, out_shape=[jax.ShapeDtypeStruct(shape, dtype) for sh...  13 us
    all_to_all x2, starting transfers between devices, swap(): return lax.all_to_all(x, axis, 0, 0)  9.26 us
    pallas_call x1, Pallas kernels, shards(): pl.pallas_call(state_kernel, out_shape=[jax.ShapeDtypeStruct((near, chunk...  4.19 us
    unnamed x34, local copies, waits for them, and re-layouts  3.74 us
  transfers between devices with their start and end apart: 2, of which 2 were waited for; matrix products, arithmetic and copies ran while one was open for 0% of the time, Pallas kernels for 2%

profile of v7, /device:TPU:8, one launch (start us, length us, event | category | flops | bytes accessed | tf_op | source)
XLA Modules:
  0.0 149.1 jit_solution(2926619966986330797)
XLA Ops:
  0.6 2.0 %shard_map.127 = bf16[8,512,128]{2,1,0:T(8,128)(2,1)} custom-call(bf16[256,512]{1,0:T(8,128)(2,1)} %refs_10_.3, bf16[256,512]{1,0:T(8,128)(2,1)} %refs_3_.3), custom_call_target="tpu_custom_call" | custom-call | flops 1000000 | bytes 1000000 | tf_op jit(solution)/shard_map/pallas_call | solution.py:110
  2.6 0.0 copy-start.1
  2.6 0.0 copy-start.4
  2.6 0.0 copy-start.6
  2.7 0.0 copy-start.8
  2.7 5.8 %all-to-all-start = ((bf16[8,512,128]{2,1,0:T(8,128)(2,1)}), bf16[8,512,128]{2,1,0:T(8,128)(2,1)}, u32[]{:S(2)}, u32[]{:S(2)}) async-start(bf16[8,512,128]{2,1,0:T(8,128)(2,1)} %shard_map.127), calls=%async_computation | async-start | bytes 2097152 | tf_op jit(solution)/shard_map/all_to_all | solution.py:21
  8.5 0.0 copy-done.1
  8.5 0.0 copy-done.4
  8.5 0.0 copy-done.6
  8.5 0.0 copy-done.8
  8.5 0.4 shard_map.126
  8.9 0.0 copy-start.2
  9.0 0.7 copy-done.2
  9.6 13.7 %all-to-all-done.rows_ref.refs_2_ = bf16[8,512,128]{2,1,0:T(8,128)(2,1)} async-done(((bf16[8,512,128]{2,1,0:T(8,128)(2,1)}), bf16[8,512,128]{2,1,0:T(8,128)(2,1)}, u32[]{:S(2)}, u32[]{:S(2)}) %all-to-all-start) | async-done | bytes 1048608 | tf_op jit(solution)/shard_map/all_to_all | solution.py:21
  23.4 4.2 %shard_map.128 = (bf16[8,64,128]{2,1,0:T(8,128)(2,1)}, bf16[8,64,256]{2,1,0:T(8,128)(2,1)}, bf16[8,64,128]{2,1,0:T(8,128)(2,1)}) custom-call(bf16[8,512,128]{2,1,0:T(8,128)(2,1)} %all-to-all-done.rows_ref.refs_2_, bf16[4,128,128]{2,1,0:T(8,128)(2,1)} %refs_4_.3, bf16[256,512]{1,0:T(8,128)(2,1)} %copy-done.2), custom_call_target="tpu_custom_call" | custom-call | flops 100000000 | bytes 1000000 | tf_op jit(solution)/shard_map/pallas_call | solution.py:170
  27.6 0.0 copy-start.7
  27.6 30.6 %all_to_all.40.refs_1_ = bf16[8,64,128]{2,1,0:T(8,128)(2,1)S(1)} all-to-all(bf16[8,64,128]{2,1,0:T(8,128)(2,1)} %get-tuple-element.31), channel_id=1, replica_groups=mesh['far'=8,'near'=8,'head'=8] {'far'}, dimensions={0} | all-to-all | bytes 262144 | tf_op jit(solution)/shard_map/all_to_all | solution.py:21
  58.2 0.0 copy-start.15
  58.2 0.9 copy-done.15
  59.1 0.0 copy-start
  59.1 0.1 shard_map.129
  59.2 9.2 %all_to_all.41.refs_3_.refs_7_ = bf16[8,64,128]{2,1,0:T(8,128)(2,1)S(1)} all-to-all(bf16[8,64,128]{2,1,0:T(8,128)(2,1)S(1)} %shard_map.129), channel_id=1, replica_groups=mesh['far'=8,'near'=8,'head'=8] {'near'}, dimensions={0} | all-to-all | bytes 262144 | tf_op jit(solution)/shard_map/all_to_all | solution.py:21
  68.4 0.0 copy-done.7
  68.4 0.0 copy-done
  68.4 0.0 copy-done.3
  68.4 0.7 copy-done.16
  69.0 1.1 shard_map.130
  70.1 0.0 copy-start.5
  70.2 9.0 %all_to_all.42.refs_0_ = f32[8,8,256]{2,1,0:T(8,128)S(1)} all-to-all(f32[8,8,256]{2,1,0:T(8,128)S(1)} %get-tuple-element.32), channel_id=1, replica_groups=mesh['far'=8,'near'=8,'head'=8] {'head'}, dimensions={0} | all-to-all | bytes 131072 | tf_op jit(solution)/shard_map/all_to_all | solution.py:21
  79.2 0.0 copy-done.9
  79.2 0.0 copy-done.5
  79.2 3.7 %shard_map.132 = bf16[8,208,128]{2,1,0:T(8,128)(2,1)} custom-call(f32[8,8,256]{2,1,0:T(8,128)S(1)} %all_to_all.42.refs_0_, f32[256,512]{1,0:T(8,128)S(1)} %get-tuple-element.33.refs_1_, bf16[256,512]{1,0:T(8,128)(2,1)S(1)} %copy-done.7, f32[1,512]{1,0:T(1,128)S(1)} %get-tuple-element.34.refs_3_, bf16[256,512]{1,0:T(8,128)(2,1)S(1)} %copy-done.3, ...), custom_call_target="tpu_custom_call" | custom-call | flops 100000000 | bytes 1000000 | tf_op jit(solution)/shard_map/pallas_call | solution.py:41
  82.9 3.5 %all-to-all-start.4 = ((bf16[8,208,128]{2,1,0:T(8,128)(2,1)}), bf16[8,208,128]{2,1,0:T(8,128)(2,1)S(1)}, u32[]{:S(2)}, u32[]{:S(2)}) async-start(bf16[8,208,128]{2,1,0:T(8,128)(2,1)} %shard_map.132), calls=%async_computation.4 | async-start | bytes 851968 | tf_op jit(solution)/shard_map/all_to_all | solution.py:21
  86.3 2.9 %shard_map.131 = (bf16[256,512]{1,0:T(8,128)(2,1)}, bf16[256,512]{1,0:T(8,128)(2,1)}, bf16[256,512]{1,0:T(8,128)(2,1)S(1)}, bf16[256,512]{1,0:T(8,128)(2,1)S(1)}...) custom-call(f32[8,8,256]{2,1,0:T(8,128)S(1)} %all_to_all.42.refs_0_, f32[256,512]{1,0:T(8,128)S(1)} %get-tuple-element.33.refs_1_, ...), custom_call_target="tpu_custom_call" | custom-call | flops 100000000 | bytes 1000000 | tf_op jit(solution)/shard_map/pallas_call | solution.py:41
  89.3 0.7 copy-done.10
  90.0 0.7 copy-done.12
  90.7 4.5 %all-to-all-done.4.refs_0_ = bf16[8,208,128]{2,1,0:T(8,128)(2,1)S(1)} async-done(((bf16[8,208,128]{2,1,0:T(8,128)(2,1)}), bf16[8,208,128]{2,1,0:T(8,128)(2,1)S(1)}, u32[]{:S(2)}, u32[]{:S(2)}) %all-to-all-start.4) | async-done | bytes 426016 | tf_op jit(solution)/shard_map/all_to_all | solution.py:21
  95.2 0.0 copy-start.14
  95.2 18.5 %all_to_all.43.refs_1_ = bf16[8,80,128]{2,1,0:T(8,128)(2,1)S(1)} all-to-all(bf16[8,80,128]{2,1,0:T(8,128)(2,1)S(1)} %shard_map.133), channel_id=1, replica_groups=mesh['far'=8,'near'=8,'head'=8] {'far'}, dimensions={0} | all-to-all | bytes 327680 | tf_op jit(solution)/shard_map/all_to_all | solution.py:21
  113.7 0.0 copy-done.14
  113.7 3.0 %shard_map.134 = (bf16[8,80,128]{2,1,0:T(8,128)(2,1)S(1)}, bf16[8,64,128]{2,1,0:T(8,128)(2,1)S(1)}, f32[512]{0:T(512)}) custom-call(bf16[8,208,128]{2,1,0:T(8,128)(2,1)S(1)} %all-to-all-done.4.refs_0_, bf16[8,80,128]{2,1,0:T(8,128)(2,1)S(1)} %all_to_all.43.refs_1_, bf16[8,512,128]{2,1,0:T(8,128)(2,1)} %all-to-all-done.rows_ref.refs_2_, ...), custom_call_target="tpu_custom_call" | custom-call | flops 100000000 | bytes 1000000 | tf_op jit(solution)/shard_map/pallas_call | solution.py:41
  116.7 17.4 %all_to_all.44.refs_0_ = bf16[8,80,128]{2,1,0:T(8,128)(2,1)S(1)} all-to-all(bf16[8,80,128]{2,1,0:T(8,128)(2,1)S(1)} %get-tuple-element.39), channel_id=1, replica_groups=mesh['far'=8,'near'=8,'head'=8] {'far'}, dimensions={0} | all-to-all | bytes 327680 | tf_op jit(solution)/shard_map/all_to_all | solution.py:21
  134.2 0.0 copy-start.11
  134.2 0.0 copy-start.13
  134.2 13.3 %all_to_all.45.refs_0_ = bf16[8,192,128]{2,1,0:T(8,128)(2,1)S(1)} all-to-all(bf16[8,192,128]{2,1,0:T(8,128)(2,1)S(1)} %shard_map.135), channel_id=1, replica_groups=mesh['far'=8,'near'=8,'head'=8] {'near'}, dimensions={0} | all-to-all | bytes 786432 | tf_op jit(solution)/shard_map/all_to_all | solution.py:21
  147.4 0.0 copy-done.11
  147.4 0.0 copy-done.13
  147.5 1.7 %shard_map.136 = (bf16[256,512]{1,0:T(8,128)(2,1)}, bf16[256,512]{1,0:T(8,128)(2,1)}, f32[4,128,128]{2,1,0:T(8,128)}, f32[4,128,128]{2,1,0:T(8,128)}) custom-call(bf16[8,192,128]{2,1,0:T(8,128)(2,1)S(1)} %all_to_all.45.refs_0_, bf16[256,512]{1,0:T(8,128)(2,1)S(1)} %get-tuple-element.41.refs_1_, bf16[256,512]{1,0:T(8,128)(2,1)S(1)} %copy-done.11, ...), custom_call_target="tpu_custom_call" | custom-call | flops 100000000 | bytes 1000000 | tf_op jit(solution)/shard_map/pallas_call | solution.py:41
  (7 shorter events, 0.1 us)
Async XLA Ops:
  2.6 5.8 %copy-start.1 = (bf16[256,512]{1,0:T(8,128)(2,1)S(1)}, bf16[256,512]{1,0:T(8,128)(2,1)}, u32[]{:S(2)}) copy-start(bf16[256,512]{1,0:T(8,128)(2,1)} %refs_10_.3) | copy-start | bytes 786436
  2.6 5.8 %copy-start.4 = (bf16[4,128,128]{2,1,0:T(8,128)(2,1)S(1)}, bf16[4,128,128]{2,1,0:T(8,128)(2,1)}, u32[]{:S(2)}) copy-start(bf16[4,128,128]{2,1,0:T(8,128)(2,1)} %refs_4_.3) | copy-start | bytes 393220
  2.6 5.8 %copy-start.6 = (bf16[256,512]{1,0:T(8,128)(2,1)S(1)}, bf16[256,512]{1,0:T(8,128)(2,1)}, u32[]{:S(2)}) copy-start(bf16[256,512]{1,0:T(8,128)(2,1)} %refs_8_.3) | copy-start | bytes 786436
  2.7 5.8 %copy-start.8 = (bf16[4,128,128]{2,1,0:T(8,128)(2,1)S(1)}, bf16[4,128,128]{2,1,0:T(8,128)(2,1)}, u32[]{:S(2)}) copy-start(bf16[4,128,128]{2,1,0:T(8,128)(2,1)} %refs_9_.3) | copy-start | bytes 393220
  2.7 20.7 %all-to-all-start = ((bf16[8,512,128]{2,1,0:T(8,128)(2,1)}), bf16[8,512,128]{2,1,0:T(8,128)(2,1)}, u32[]{:S(2)}, u32[]{:S(2)}) async-start(bf16[8,512,128]{2,1,0:T(8,128)(2,1)} %shard_map.127), calls=%async_computation | async-start | bytes 2097152 | tf_op jit(solution)/shard_map/all_to_all | solution.py:21
  8.9 0.7 copy-start.2
  27.6 40.8 %copy-start.7 = (bf16[256,512]{1,0:T(8,128)(2,1)S(1)}, bf16[256,512]{1,0:T(8,128)(2,1)}, u32[]{:S(2)}) copy-start(bf16[256,512]{1,0:T(8,128)(2,1)} %refs_2_.7) | copy-start | bytes 786436
  58.2 0.9 copy-start.15
  59.1 9.2 %copy-start = (bf16[256,512]{1,0:T(8,128)(2,1)S(1)}, bf16[256,512]{1,0:T(8,128)(2,1)}, u32[]{:S(2)}) copy-start(bf16[256,512]{1,0:T(8,128)(2,1)} %refs_3_.3) | copy-start | bytes 786436
  59.1 9.2 %copy-start.3 = (bf16[256,512]{1,0:T(8,128)(2,1)S(1)}, bf16[256,512]{1,0:T(8,128)(2,1)}, u32[]{:S(2)}) copy-start(bf16[256,512]{1,0:T(8,128)(2,1)} %copy-done.2) | copy-start | bytes 786436
  68.4 0.7 copy-start.16
  69.0 10.1 %copy-start.9 = (bf16[4,128,128]{2,1,0:T(8,128)(2,1)S(1)}, bf16[4,128,128]{2,1,0:T(8,128)(2,1)}, u32[]{:S(2)}) copy-start(bf16[4,128,128]{2,1,0:T(8,128)(2,1)} %refs_9_.3) | copy-start | bytes 393220
  70.1 9.0 %copy-start.5 = (bf16[4,128,128]{2,1,0:T(8,128)(2,1)S(1)}, bf16[4,128,128]{2,1,0:T(8,128)(2,1)}, u32[]{:S(2)}) copy-start(bf16[4,128,128]{2,1,0:T(8,128)(2,1)} %refs_4_.3) | copy-start | bytes 393220
  82.9 12.3 %all-to-all-start.4 = ((bf16[8,208,128]{2,1,0:T(8,128)(2,1)}), bf16[8,208,128]{2,1,0:T(8,128)(2,1)S(1)}, u32[]{:S(2)}, u32[]{:S(2)}) async-start(bf16[8,208,128]{2,1,0:T(8,128)(2,1)} %shard_map.132), calls=%async_computation.4 | async-start | bytes 851968 | tf_op jit(solution)/shard_map/all_to_all | solution.py:21
  89.3 0.7 copy-start.10
  90.0 0.7 copy-start.12
  95.2 18.5 %copy-start.14 = (bf16[8,64,256]{2,1,0:T(8,128)(2,1)S(1)}, bf16[8,64,256]{2,1,0:T(8,128)(2,1)}, u32[]{:S(2)}) copy-start(bf16[8,64,256]{2,1,0:T(8,128)(2,1)} %get-tuple-element.38.refs_3_) | copy-start | bytes 786436
  134.2 13.3 %copy-start.11 = (bf16[256,512]{1,0:T(8,128)(2,1)S(1)}, bf16[256,512]{1,0:T(8,128)(2,1)}, u32[]{:S(2)}) copy-start(bf16[256,512]{1,0:T(8,128)(2,1)} %copy-done.10) | copy-start | bytes 786436
  134.2 13.3 %copy-start.13 = (bf16[256,512]{1,0:T(8,128)(2,1)S(1)}, bf16[256,512]{1,0:T(8,128)(2,1)}, u32[]{:S(2)}) copy-start(bf16[256,512]{1,0:T(8,128)(2,1)} %copy-done.12) | copy-start | bytes 786436

commit v8 on v3

v8 whole, which is shorter than its diff:
```python
import jax
import jax.numpy as jnp
from jax import lax
from jax.experimental import pallas as pl
from jax.experimental.pallas import tpu as pltpu
from jax.sharding import Mesh, PartitionSpec as P

EPSILON = 1e-05
BF = jnp.bfloat16
F32 = jnp.float32
NEAR = 8
GAIN_ROWS = 16
STAT_ROWS = 8
TOKEN = ((8, 128), F32)
VMEM_BYTES = 24 * 1024 * 1024
WHOLE_VMEM = 64 * 1024 * 1024


def swap(x, axis):
    return lax.all_to_all(x, axis, 0, 0)


def run(kernel, outs, ins, after=(), fetch=(), limit=VMEM_BYTES):
    count, copies = len(ins), len(fetch)

    def body(*refs):
        sources = refs[count : count + copies]
        outputs = refs[count + copies + len(after) : count + copies + len(after) + len(outs)]
        if not copies:
            return kernel(*refs[:count], *outputs)
        held, sems = refs[-copies - 1 : -1], refs[-1]
        moves = [pltpu.make_async_copy(sources[i], held[i], sems.at[i]) for i in range(copies)]
        for move in moves:
            move.start()
        return kernel(*refs[:count], *held, *outputs, [move.wait for move in moves])

    whole = pl.BlockSpec(memory_space=pltpu.VMEM)
    far_off = pl.BlockSpec(memory_space=pl.ANY)
    scratch = [pltpu.VMEM(x.shape, x.dtype) for x in fetch]
    return pl.pallas_call(
        body,
        out_shape=[jax.ShapeDtypeStruct(shape, dtype) for shape, dtype in outs],
        in_specs=[whole] * count
        + [far_off] * copies
        + [far_off] * len(after),
        out_specs=[whole] * len(outs),
        scratch_shapes=scratch + [pltpu.SemaphoreType.DMA((copies,))] if copies else [],
        compiler_params=pltpu.CompilerParams(vmem_limit_bytes=limit),
        cost_estimate=pl.CostEstimate(flops=10**8, bytes_accessed=10**6, transcendentals=0),
    )(*ins, *fetch, *after)


def dot(a, b, over_a, over_b):
    return lax.dot_general(a, b, (((over_a,), (over_b,)), ((), ())), preferred_element_type=F32)


def silu_slope(x):
    g = 1.0 / (1.0 + jnp.exp(-x))
    return g * (1.0 + x * (1.0 - g))


def causal_mask(count, later=0):
    rows = lax.broadcasted_iota(jnp.int32, (count, count), later)
    cols = lax.broadcasted_iota(jnp.int32, (count, count), 1 - later)
    return rows >= cols


def shards(query_rows, key_rows, value_rows, feat_query, feat_key, norm_gain, grad_out):
    tokens, width = query_rows.shape
    heads, size = feat_query.shape[0], feat_query.shape[1]
    near, far = lax.axis_size("near"), lax.axis_size("far")
    full_width = width * lax.axis_size("head")
    chunk = heads * size // near
    slim = chunk // far
    per_head = near // heads
    cols = [slice(h * size, (h + 1) * size) for h in range(heads)]

    def put_state(out_ref, h, value, row):
        for part in range(per_head):
            rows = value[part * chunk : (part + 1) * chunk]
            out_ref[h * per_head + part, row : row + chunk, :] = rows.astype(BF)

    def get_state(ref, h):
        parts = [ref[h * per_head + part] for part in range(per_head)]
        return jnp.concatenate(parts, axis=0)

    def state_kernel(wk_ref, k_ref, v_ref, wq_ref, q_ref, gain_ref, kf_ref, qf_ref, out_ref, row_ref, waits):
        waits[0]()
        waits[1]()
        for h, at in enumerate(cols):
            pre = dot(k_ref[:, at], wk_ref[h], 1, 0)
            kf_ref[:, at] = (pre / (1.0 + jnp.exp(-pre))).astype(BF)
        waits[2]()
        for h, at in enumerate(cols):
            put_state(out_ref, h, dot(kf_ref[:, at], v_ref[:, at], 0, 0), 0)
        for wait in waits[3:]:
            wait()
        for h, at in enumerate(cols):
            pre = dot(q_ref[:, at], wq_ref[h], 1, 0)
            qf_ref[:, at] = (pre / (1.0 + jnp.exp(-pre))).astype(BF)
            row_ref[:, at] = jnp.broadcast_to(gain_ref[at].reshape(1, size), (8, size))

    key_feat, query_feat, payload, gain_rows = run(
        state_kernel,
        [((tokens, width), BF), ((tokens, width), BF), ((near, chunk, size), BF), ((8, width), F32)],
        [],
        fetch=[feat_key, key_rows, value_rows, feat_query, query_rows, norm_gain],
        limit=WHOLE_VMEM,
    )
    parts = swap(payload, "near")

    def total_kernel(in_ref, out_ref):
        total = in_ref[0].astype(F32)
        for i in range(1, near):
            total = total + in_ref[i].astype(F32)
        total = total.astype(BF)
        for i in range(out_ref.shape[0]):
            out_ref[i] = total

    (payload,) = run(total_kernel, [((far, chunk, size), BF)], [parts])
    parts_far = swap(payload, "far")

    def join(parts_ref, far_ref, out_ref, backward):
        place = lax.axis_index("far")
        state = jnp.zeros((chunk, size), F32)
        for i in range(far):
            keep = (i > place) if backward else (i < place)
            state = state + jnp.where(keep, far_ref[i][:chunk].astype(F32), 0.0)
        for i in range(near - 1, -1, -1) if backward else range(near):
            out_ref[i] = state.astype(BF)
            state = state + parts_ref[i][:chunk].astype(F32)

    def prior_kernel(parts_ref, far_ref, out_ref):
        join(parts_ref, far_ref, out_ref, False)

    (payload,) = run(prior_kernel, [((near, chunk, size), BF)], [parts, parts_far])
    prior = swap(payload, "near")

    def norm_kernel(qf_ref, kf_ref, v_ref, p_ref, go_ref, gain_ref, pre_ref, out_ref):
        mask = causal_mask(tokens)
        squares = jnp.zeros((tokens, size), F32)
        inner = jnp.zeros((tokens, size), F32)
        for h, at in enumerate(cols):
            scores = jnp.where(mask, dot(qf_ref[:, at], kf_ref[:, at], 1, 1), 0.0).astype(BF)
            pre = dot(scores, v_ref[:, at], 1, 0) + dot(qf_ref[:, at], get_state(p_ref, h), 1, 0)
            pre_ref[:, at] = pre
            squares = squares + pre * pre
            inner = inner + go_ref[:, at].astype(F32) * gain_ref[:1, at] * pre
        squares = jnp.sum(squares, axis=1, keepdims=True)
        inner = jnp.sum(inner, axis=1, keepdims=True)
        lane = lax.broadcasted_iota(jnp.int32, (tokens, size), 1)
        both = jnp.where(lane == 0, squares, jnp.where(lane == 1, inner, 0.0))
        rows = jnp.transpose(both)[:STAT_ROWS]
        for i in range(out_ref.shape[0]):
            out_ref[i] = rows

    peers = lax.axis_size("head")
    pre_norm, payload = run(
        norm_kernel,
        [((tokens, width), F32), ((peers, STAT_ROWS, tokens), F32)],
        [query_feat, key_feat, value_rows, prior, grad_out, gain_rows],
    )
    stats = swap(payload, "head")

    def row_factors(st_ref):
        rows = st_ref[0]
        for i in range(1, peers):
            rows = rows + st_ref[i]
        rows = jnp.concatenate([rows, jnp.zeros((size - STAT_ROWS, tokens), F32)], axis=0)
        both = jnp.transpose(rows)
        inverse = 1.0 / jnp.sqrt(both[:, 0:1] / full_width + EPSILON)
        return inverse, both[:, 1:2] * inverse / full_width

    def query_side(h, at, delta, mask, v_ref, kf_ref, p_ref, q_ref, wq_ref):
        back = jnp.where(mask, dot(delta, v_ref[:, at], 1, 1), 0.0).astype(BF)
        grad = dot(back, kf_ref[:, at], 1, 0) + dot(delta, get_state(p_ref, h), 1, 1)
        return (grad * silu_slope(dot(q_ref[:, at], wq_ref[h], 1, 0))).astype(BF)

    def delta_kernel(
        st_ref, pre_ref, go_ref, gain_ref, qf_ref, v_ref, kf_ref, p_ref, q_ref, wq_ref, att_ref, delta_ref, out_ref
    ):
        inverse, slope = row_factors(st_ref)
        mask = causal_mask(tokens)
        gains = []
        for h, at in enumerate(cols):
            normed = pre_ref[:, at] * inverse
            wide = go_ref[:, at].astype(F32)
            delta = ((wide * gain_ref[:1, at] - normed * slope) * inverse).astype(BF)
            delta_ref[:, at] = delta
            att_ref[:, at] = (normed * gain_ref[:1, at]).astype(BF)
            gains.append(jnp.sum(wide * normed, axis=0, keepdims=True))
            put_state(out_ref, h, dot(qf_ref[:, at], delta, 0, 0), 0)
            grad = query_side(h, at, delta, mask, v_ref, kf_ref, p_ref, q_ref, wq_ref)
            put_state(out_ref, h, dot(q_ref[:, at], grad, 0, 0), chunk)
        rest = [jnp.zeros((GAIN_ROWS - heads, size), F32)]
        rows = jnp.concatenate(gains + rest, axis=0).astype(BF)
        for i in range(near):
            out_ref[i, 2 * chunk :, :] = rows

    attended, delta, payload = run(
        delta_kernel,
        [((tokens, width), BF), ((tokens, width), BF), ((near, 2 * chunk + GAIN_ROWS, size), BF)],
        [stats, pre_norm, grad_out, gain_rows, query_feat, value_rows, key_feat, prior, query_rows, feat_query],
    )
    parts = swap(payload, "near")

    def back_total_kernel(in_ref, out_ref):
        total = in_ref[0].astype(F32)
        for i in range(1, near):
            total = total + in_ref[i].astype(F32)
        head_rows, gains = total[:chunk], total[2 * chunk : 2 * chunk + 8]
        for i in range(far):
            part = total[chunk + i * slim : chunk + (i + 1) * slim]
            out_ref[i] = jnp.concatenate([head_rows, part, gains], axis=0).astype(BF)

    (payload,) = run(
        back_total_kernel, [((far, chunk + slim + 8, size), BF)], [parts]
    )
    parts_far = swap(payload, "far")

    def later_kernel(parts_ref, far_ref, out_ref, side_ref, gain_ref):
        join(parts_ref, far_ref, out_ref, True)
        side = far_ref[0].astype(F32)[chunk:]
        for i in range(1, far):
            side = side + far_ref[i].astype(F32)[chunk:]
        side_ref[...] = side
        for h, at in enumerate(cols):
            gain_ref[at] = side[slim + h]

    payload, side, grad_gain = run(
        later_kernel,
        [((near, chunk, size), BF), ((slim + 8, size), F32), ((width,), F32)],
        [parts, parts_far],
    )
    later = swap(payload, "near")

    def key_kernel(delta_ref, qf_ref, v_ref, l_ref, wk_ref, k_ref, kpg_ref, out_ref):
        turned = causal_mask(tokens, 1)
        for h, at in enumerate(cols):
            back = jnp.where(turned, dot(v_ref[:, at], delta_ref[:, at], 1, 1), 0.0).astype(BF)
            grad = dot(back, qf_ref[:, at], 1, 0) + dot(v_ref[:, at], get_state(l_ref, h), 1, 1)
            grad = (grad * silu_slope(dot(k_ref[:, at], wk_ref[h], 1, 0))).astype(BF)
            kpg_ref[:, at] = grad
            put_state(out_ref, h, dot(k_ref[:, at], grad, 0, 0), 0)

    key_pre_grad, payload = run(
        key_kernel,
        [((tokens, width), BF), ((near, chunk, size), BF)],
        [delta, query_feat, value_rows, later, feat_key, key_rows],
    )
    parts = swap(payload, "near")

    def last_kernel(
        kpg_ref, wk_ref, l_ref, delta_ref, qf_ref, kf_ref, v_ref, p_ref, q_ref, wq_ref,
        gk_ref, gq_ref, gv_ref, token_ref,
    ):
        token_ref[...] = jnp.zeros(token_ref.shape, F32)
        mask, turned = causal_mask(tokens), causal_mask(tokens, 1)
        for h, at in enumerate(cols):
            gk_ref[:, at] = dot(kpg_ref[:, at], wk_ref[h], 1, 1).astype(BF)
            delta = delta_ref[:, at]
            grad = query_side(h, at, delta, mask, v_ref, kf_ref, p_ref, q_ref, wq_ref)
            gq_ref[:, at] = dot(grad, wq_ref[h], 1, 1).astype(BF)
            scores = jnp.where(turned, dot(kf_ref[:, at], qf_ref[:, at], 1, 1), 0.0).astype(BF)
            value = dot(scores, delta, 1, 0) + dot(kf_ref[:, at], get_state(l_ref, h), 1, 0)
            gv_ref[:, at] = value.astype(BF)

    grad_key, grad_query, grad_value, token = run(
        last_kernel,
        [((tokens, width), BF)] * 3 + [TOKEN],
        [
            key_pre_grad, feat_key, later, delta, query_feat, key_feat, value_rows, prior, query_rows, feat_query,
        ],
    )

    def weight_total_kernel(in_ref, side_ref, out_ref):
        total = in_ref[0].astype(F32)
        for i in range(1, near):
            total = total + in_ref[i].astype(F32)
        pad = jnp.zeros((8, size), F32)
        total = jnp.concatenate([total, side_ref[:slim], pad], axis=0).astype(BF)
        for i in range(far):
            out_ref[i] = total

    (payload,) = run(
        weight_total_kernel,
        [((far, chunk + slim + 8, size), BF)],
        [parts, side],
        after=[token],
    )
    parts_far = swap(payload, "far")

    def weight_kernel(far_ref, out_ref):
        total = far_ref[0].astype(F32)[:chunk]
        for i in range(1, far):
            total = total + far_ref[i].astype(F32)[:chunk]
        queries = [far_ref[i].astype(F32)[chunk : chunk + slim] for i in range(far)]
        total = jnp.concatenate([total] + queries, axis=0).astype(BF)
        for i in range(near):
            out_ref[i] = total

    (payload,) = run(weight_kernel, [((near, 2 * chunk, size), BF)], [parts_far])
    done = swap(payload, "near")

    def widen_kernel(in_ref, gq_ref, gk_ref):
        for h in range(heads):
            for part in range(per_head):
                rows = slice(part * chunk, (part + 1) * chunk)
                gk_ref[h, rows] = in_ref[h * per_head + part, :chunk].astype(F32)
                gq_ref[h, rows] = in_ref[h * per_head + part, chunk:].astype(F32)

    grad_feat_query, grad_feat_key = run(
        widen_kernel, [(feat_query.shape, F32), (feat_key.shape, F32)], [done]
    )
    return (attended, grad_query, grad_key, grad_value, grad_feat_query, grad_feat_key, grad_gain)


def solution(mesh):
    seq, head = mesh.devices.shape
    split = Mesh(mesh.devices.reshape(seq // NEAR, NEAR, head), ("far", "near", "head"))
    wide = P(("far", "near"), "head")
    per_head = P("head", None, None)
    in_specs = (wide, wide, wide, per_head, per_head, P("head"), wide)
    out_specs = (wide, wide, wide, wide, per_head, per_head, P("head"))
    return jax.shard_map(shards, mesh=split, in_specs=in_specs, out_specs=out_specs, check_vma=False)
```

time: 148 us -> 146 us (0.986)
  blocking collectives: 104 us -> 125 us
  starting transfers between devices: 12.6 us -> 3.37 us
  waiting for transfers between devices: 12 us -> 4.24 us
  local copies, waits for them, and re-layouts: 4.18 us -> 0.04 us
  Pallas kernels: 13.8 us -> 11.6 us
    all_to_all x7 -> x9, blocking collectives: 104 us -> 125 us  [swap(): return lax.all_to_all(x, axis, 0, 0)]
    all_to_all x3 -> x1, starting transfers between devices: 12.6 us -> 3.37 us  [swap(): return lax.all_to_all(x, axis, 0, 0)]
    all_to_all x3 -> x1, waiting for transfers between devices: 12 us -> 4.24 us  [swap(): return lax.all_to_all(x, axis, 0, 0)]
    unnamed x24 -> x18, local copies, waits for them, and re-layouts: 4.18 us -> 0.04 us
    pallas_call x12, Pallas kernels: 13.2 us -> 11.6 us  [run(): pl.pallas_call(body, out_shape=[jax.ShapeDtypeStruct(shape, dtype) for sh...]
  transfers between devices with their start and end apart: 3 -> 1, of which waited for: 3 -> 1; matrix products, arithmetic and copies ran while one was open for 0% -> 0% of each run, Pallas kernels for 4% -> 2%
where the time goes in v8:
time: 146 us; the launch traced here: 145 us
  blocking collectives  125 us (86%)
  Pallas kernels  11.6 us (8%)
  waiting for transfers between devices  4.24 us (3%)
  starting transfers between devices  3.37 us (2%)
    all_to_all x9, blocking collectives, swap(): return lax.all_to_all(x, axis, 0, 0)  125 us
    pallas_call x12, Pallas kernels, run(): pl.pallas_call(body, out_shape=[jax.ShapeDtypeStruct(shape, dtype) for sh...  11.6 us
    all_to_all x1, waiting for transfers between devices, swap(): return lax.all_to_all(x, axis, 0, 0)  4.24 us
    all_to_all x1, starting transfers between devices, swap(): return lax.all_to_all(x, axis, 0, 0)  3.37 us
  transfers between devices with their start and end apart: 1, of which 1 were waited for; matrix products, arithmetic and copies ran while one was open for 0% of the time, Pallas kernels for 2%

profile of v8, /device:TPU:8, one launch (start us, length us, event | category | flops | bytes accessed | tf_op | source)
XLA Modules:
  0.0 145.4 jit_solution(10216247204054199896)
XLA Ops:
  0.6 2.7 %shard_map.126 = (bf16[256,512]{1,0:T(8,128)(2,1)}, bf16[256,512]{1,0:T(8,128)(2,1)}, bf16[8,64,128]{2,1,0:T(8,128)(2,1)}, f32[8,512]{1,0:T(8,128)}) custom-call(bf16[4,128,128]{2,1,0:T(8,128)(2,1)} %refs_1_.3, bf16[256,512]{1,0:T(8,128)(2,1)} %refs_5_.5, bf16[256,512]{1,0:T(8,128)(2,1)} %refs_6_.1, bf16[4,128,128]{2,1,0:T(8,128)(2,1)} %refs_9_.3, ...), custom_call_target="tpu_custom_call" | custom-call | flops 100000000 | bytes 1000000 | tf_op jit(solution)/shard_map/pallas_call | solution.py:40
  3.3 12.2 %all_to_all.50.refs_0_ = bf16[8,64,128]{2,1,0:T(8,128)(2,1)S(1)} all-to-all(bf16[8,64,128]{2,1,0:T(8,128)(2,1)} %get-tuple-element.29), channel_id=1, replica_groups=mesh['far'=8,'near'=8,'head'=8] {'near'}, dimensions={0} | all-to-all | bytes 262144 | tf_op jit(solution)/shard_map/all_to_all | solution.py:20
  15.6 0.0 copy-start.6
  15.6 0.0 copy-start.3
  15.6 27.9 %all_to_all.51.refs_1_ = bf16[8,64,128]{2,1,0:T(8,128)(2,1)S(1)} all-to-all(bf16[8,64,128]{2,1,0:T(8,128)(2,1)S(1)} %shard_map.127), channel_id=1, replica_groups=mesh['far'=8,'near'=8,'head'=8] {'far'}, dimensions={0} | all-to-all | bytes 262144 | tf_op jit(solution)/shard_map/all_to_all | solution.py:20
  43.5 0.0 copy-start
  43.5 0.0 copy-start.1
  43.5 0.1 shard_map.128
  43.6 0.0 copy-start.8
  43.6 10.0 %all_to_all.52.refs_3_.refs_7_ = bf16[8,64,128]{2,1,0:T(8,128)(2,1)S(1)} all-to-all(bf16[8,64,128]{2,1,0:T(8,128)(2,1)S(1)} %shard_map.128), channel_id=1, replica_groups=mesh['far'=8,'near'=8,'head'=8] {'near'}, dimensions={0} | all-to-all | bytes 262144 | tf_op jit(solution)/shard_map/all_to_all | solution.py:20
  53.6 0.0 copy-done.6
  53.6 0.0 copy-done.3
  53.6 0.0 copy-done
  53.6 0.0 copy-done.1
  53.6 0.0 copy-done.8
  53.6 0.0 copy-start.2
  53.7 0.8 shard_map.129
  54.5 0.0 copy-start.5
  54.5 9.0 %all_to_all.53.refs_0_ = f32[8,8,256]{2,1,0:T(8,128)S(1)} all-to-all(f32[8,8,256]{2,1,0:T(8,128)S(1)} %get-tuple-element.31), channel_id=1, replica_groups=mesh['far'=8,'near'=8,'head'=8] {'head'}, dimensions={0} | all-to-all | bytes 131072 | tf_op jit(solution)/shard_map/all_to_all | solution.py:20
  63.5 0.0 copy-done.2
  63.5 0.0 copy-done.5
  63.5 2.3 %shard_map.130 = (bf16[256,512]{1,0:T(8,128)(2,1)}, bf16[256,512]{1,0:T(8,128)(2,1)S(1)}, bf16[8,144,128]{2,1,0:T(8,128)(2,1)S(1)}) custom-call(f32[8,8,256]{2,1,0:T(8,128)S(1)} %all_to_all.53.refs_0_, f32[256,512]{1,0:T(8,128)S(1)} %get-tuple-element.32.refs_1_, bf16[256,512]{1,0:T(8,128)(2,1)S(1)} %copy-done.6, f32[8,512]{1,0:T(8,128)S(1)} %copy-done.8, ...), custom_call_target="tpu_custom_call" | custom-call | flops 100000000 | bytes 1000000 | tf_op jit(solution)/shard_map/pallas_call | solution.py:40
  65.7 10.4 %all_to_all.54.refs_0_ = bf16[8,144,128]{2,1,0:T(8,128)(2,1)S(1)} all-to-all(bf16[8,144,128]{2,1,0:T(8,128)(2,1)S(1)} %get-tuple-element.35), channel_id=1, replica_groups=mesh['far'=8,'near'=8,'head'=8] {'near'}, dimensions={0} | all-to-all | bytes 589824 | tf_op jit(solution)/shard_map/all_to_all | solution.py:20
  76.2 17.2 %all_to_all.55.refs_1_ = bf16[8,80,128]{2,1,0:T(8,128)(2,1)S(1)} all-to-all(bf16[8,80,128]{2,1,0:T(8,128)(2,1)S(1)} %shard_map.131), channel_id=1, replica_groups=mesh['far'=8,'near'=8,'head'=8] {'far'}, dimensions={0} | all-to-all | bytes 327680 | tf_op jit(solution)/shard_map/all_to_all | solution.py:20
  93.3 0.0 copy-start.7
  93.3 0.6 shard_map.132
  93.9 0.0 copy-start.4
  93.9 10.8 %all_to_all.56.refs_3_.refs_2_ = bf16[8,64,128]{2,1,0:T(8,128)(2,1)S(1)} all-to-all(bf16[8,64,128]{2,1,0:T(8,128)(2,1)S(1)} %get-tuple-element.36), channel_id=1, replica_groups=mesh['far'=8,'near'=8,'head'=8] {'near'}, dimensions={0} | all-to-all | bytes 262144 | tf_op jit(solution)/shard_map/all_to_all | solution.py:20
  104.7 0.0 copy-done.7
  104.7 0.0 copy-done.4
  104.7 1.9 %shard_map.133 = (bf16[256,512]{1,0:T(8,128)(2,1)S(1)}, bf16[8,64,128]{2,1,0:T(8,128)(2,1)}) custom-call(bf16[256,512]{1,0:T(8,128)(2,1)S(1)} %get-tuple-element.34.refs_0_.refs_3_, bf16[256,512]{1,0:T(8,128)(2,1)S(1)} %copy-done.1, bf16[256,512]{1,0:T(8,128)(2,1)S(1)} %copy-done, bf16[8,64,128]{2,1,0:T(8,128)(2,1)S(1)} %all_to_all.56.refs_3_.refs_2_, ...), custom_call_target="tpu_custom_call" | custom-call | flops 100000000 | bytes 1000000 | tf_op jit(solution)/shard_map/pallas_call | solution.py:40
  106.7 3.4 %all-to-all-start.7 = ((bf16[8,64,128]{2,1,0:T(8,128)(2,1)}), bf16[8,64,128]{2,1,0:T(8,128)(2,1)S(1)}, u32[]{:S(2)}, u32[]{:S(2)}) async-start(bf16[8,64,128]{2,1,0:T(8,128)(2,1)} %get-tuple-element.41), calls=%async_computation.7 | async-start | bytes 262144 | tf_op jit(solution)/shard_map/all_to_all | solution.py:20
  110.1 2.3 %shard_map.134 = (bf16[256,512]{1,0:T(8,128)(2,1)}, bf16[256,512]{1,0:T(8,128)(2,1)}, bf16[256,512]{1,0:T(8,128)(2,1)}, f32[8,128]{1,0:T(8,128)S(1)}) custom-call(bf16[256,512]{1,0:T(8,128)(2,1)S(1)} %get-tuple-element.37.refs_0_, bf16[4,128,128]{2,1,0:T(8,128)(2,1)S(1)} %copy-done.4, bf16[8,64,128]{2,1,0:T(8,128)(2,1)S(1)} %all_to_all.56.refs_3_.refs_2_, ...), custom_call_target="tpu_custom_call" | custom-call | flops 100000000 | bytes 1000000 | tf_op jit(solution)/shard_map/pallas_call | solution.py:40
  112.3 4.2 %all-to-all-done.7.refs_0_ = bf16[8,64,128]{2,1,0:T(8,128)(2,1)S(1)} async-done(((bf16[8,64,128]{2,1,0:T(8,128)(2,1)}), bf16[8,64,128]{2,1,0:T(8,128)(2,1)S(1)}, u32[]{:S(2)}, u32[]{:S(2)}) %all-to-all-start.7) | async-done | bytes 131104 | tf_op jit(solution)/shard_map/all_to_all | solution.py:20
  116.6 18.3 %all_to_all.57.refs_0_ = bf16[8,80,128]{2,1,0:T(8,128)(2,1)S(1)} all-to-all(bf16[8,80,128]{2,1,0:T(8,128)(2,1)S(1)} %shard_map.135), channel_id=1, replica_groups=mesh['far'=8,'near'=8,'head'=8] {'far'}, dimensions={0} | all-to-all | bytes 327680 | tf_op jit(solution)/shard_map/all_to_all | solution.py:20
  134.9 9.6 %all_to_all.58.refs_0_ = bf16[8,128,128]{2,1,0:T(8,128)(2,1)S(1)} all-to-all(bf16[8,128,128]{2,1,0:T(8,128)(2,1)S(1)} %shard_map.136), channel_id=1, replica_groups=mesh['far'=8,'near'=8,'head'=8] {'near'}, dimensions={0} | all-to-all | bytes 524288 | tf_op jit(solution)/shard_map/all_to_all | solution.py:20
  144.5 0.8 shard_map.137
  (4 shorter events, 0.1 us)
Async XLA Ops:
  15.6 38.0 %copy-start.6 = (bf16[256,512]{1,0:T(8,128)(2,1)S(1)}, bf16[256,512]{1,0:T(8,128)(2,1)}, u32[]{:S(2)}) copy-start(bf16[256,512]{1,0:T(8,128)(2,1)} %refs_2_.6) | copy-start | bytes 786436
  15.6 38.0 %copy-start.3 = (bf16[256,512]{1,0:T(8,128)(2,1)S(1)}, bf16[256,512]{1,0:T(8,128)(2,1)}, u32[]{:S(2)}) copy-start(bf16[256,512]{1,0:T(8,128)(2,1)} %get-tuple-element.28.refs_1_.refs_6_.refs_5_) | copy-start | bytes 786436
  43.5 10.1 %copy-start = (bf16[256,512]{1,0:T(8,128)(2,1)S(1)}, bf16[256,512]{1,0:T(8,128)(2,1)}, u32[]{:S(2)}) copy-start(bf16[256,512]{1,0:T(8,128)(2,1)} %refs_6_.1) | copy-start | bytes 786436
  43.5 10.1 %copy-start.1 = (bf16[256,512]{1,0:T(8,128)(2,1)S(1)}, bf16[256,512]{1,0:T(8,128)(2,1)}, u32[]{:S(2)}) copy-start(bf16[256,512]{1,0:T(8,128)(2,1)} %get-tuple-element.27.refs_0_.refs_4_.refs_1_) | copy-start | bytes 786436
  43.6 10.1 %copy-start.8 = (f32[8,512]{1,0:T(8,128)S(1)}, f32[8,512]{1,0:T(8,128)}, u32[]{:S(2)}) copy-start(f32[8,512]{1,0:T(8,128)} %get-tuple-element.30.refs_5_.refs_3_) | copy-start | bytes 49156
  53.6 9.8 %copy-start.2 = (bf16[256,512]{1,0:T(8,128)(2,1)S(1)}, bf16[256,512]{1,0:T(8,128)(2,1)}, u32[]{:S(2)}) copy-start(bf16[256,512]{1,0:T(8,128)(2,1)} %refs_8_.3) | copy-start | bytes 786436
  54.5 9.0 %copy-start.5 = (bf16[4,128,128]{2,1,0:T(8,128)(2,1)S(1)}, bf16[4,128,128]{2,1,0:T(8,128)(2,1)}, u32[]{:S(2)}) copy-start(bf16[4,128,128]{2,1,0:T(8,128)(2,1)} %refs_9_.3) | copy-start | bytes 393220
  93.3 11.4 %copy-start.7 = (bf16[256,512]{1,0:T(8,128)(2,1)S(1)}, bf16[256,512]{1,0:T(8,128)(2,1)}, u32[]{:S(2)}) copy-start(bf16[256,512]{1,0:T(8,128)(2,1)} %refs_5_.5) | copy-start | bytes 786436
  93.9 10.8 %copy-start.4 = (bf16[4,128,128]{2,1,0:T(8,128)(2,1)S(1)}, bf16[4,128,128]{2,1,0:T(8,128)(2,1)}, u32[]{:S(2)}) copy-start(bf16[4,128,128]{2,1,0:T(8,128)(2,1)} %refs_1_.3) | copy-start | bytes 393220
  106.7 9.9 %all-to-all-start.7 = ((bf16[8,64,128]{2,1,0:T(8,128)(2,1)}), bf16[8,64,128]{2,1,0:T(8,128)(2,1)S(1)}, u32[]{:S(2)}, u32[]{:S(2)}) async-start(bf16[8,64,128]{2,1,0:T(8,128)(2,1)} %get-tuple-element.41), calls=%async_computation.7 | async-start | bytes 262144 | tf_op jit(solution)/shard_map/all_to_all | solution.py:20

commit v9 on v8

--- a/solution.py
+++ b/solution.py
@@ -20,34 +20,21 @@
     return lax.all_to_all(x, axis, 0, 0)
 
 
-def run(kernel, outs, ins, after=(), fetch=(), limit=VMEM_BYTES):
-    count, copies = len(ins), len(fetch)
+def run(kernel, outs, ins, after=()):
+    count = len(ins)
 
     def body(*refs):
-        sources = refs[count : count + copies]
-        outputs = refs[count + copies + len(after) : count + copies + len(after) + len(outs)]
-        if not copies:
-            return kernel(*refs[:count], *outputs)
-        held, sems = refs[-copies - 1 : -1], refs[-1]
-        moves = [pltpu.make_async_copy(sources[i], held[i], sems.at[i]) for i in range(copies)]
-        for move in moves:
-            move.start()
-        return kernel(*refs[:count], *held, *outputs, [move.wait for move in moves])
+        kernel(*refs[:count], *refs[count + len(after) :])
 
     whole = pl.BlockSpec(memory_space=pltpu.VMEM)
-    far_off = pl.BlockSpec(memory_space=pl.ANY)
-    scratch = [pltpu.VMEM(x.shape, x.dtype) for x in fetch]
     return pl.pallas_call(
         body,
         out_shape=[jax.ShapeDtypeStruct(shape, dtype) for shape, dtype in outs],
-        in_specs=[whole] * count
-        + [far_off] * copies
-        + [far_off] * len(after),
+        in_specs=[whole] * count + [pl.BlockSpec(memory_space=pl.ANY)] * len(after),
         out_specs=[whole] * len(outs),
-        scratch_shapes=scratch + [pltpu.SemaphoreType.DMA((copies,))] if copies else [],
-        compiler_params=pltpu.CompilerParams(vmem_limit_bytes=limit),
+        compiler_params=pltpu.CompilerParams(vmem_limit_bytes=VMEM_BYTES),
         cost_estimate=pl.CostEstimate(flops=10**8, bytes_accessed=10**6, transcendentals=0),
-    )(*ins, *fetch, *after)
+    )(*ins, *after)
 
 
 def dot(a, b, over_a, over_b):
@@ -84,29 +71,77 @@
         parts = [ref[h * per_head + part] for part in range(per_head)]
         return jnp.concatenate(parts, axis=0)
 
-    def state_kernel(wk_ref, k_ref, v_ref, wq_ref, q_ref, gain_ref, kf_ref, qf_ref, out_ref, row_ref, waits):
-        waits[0]()
-        waits[1]()
+    quarter = tokens // 4
+    blocks = [pl.ds(i * quarter, quarter) for i in range(4)]
+
+    def state_kernel(
+        wk_hbm, k_hbm, v_hbm, wq_hbm, q_hbm, gain_hbm, kf_hbm, qf_hbm, out_hbm, row_hbm,
+        wk_ref, k_ref, v_ref, wq_ref, q_ref, gain_ref, kf_ref, qf_ref, out_ref, row_ref, in_sems, out_sems,
+    ):
+        loads, stores = [], []
+
+        def load(source, target):
+            move = pltpu.make_async_copy(source, target, in_sems.at[len(loads)])
+            move.start()
+            loads.append(move)
+
+        def store(source, target):
+            move = pltpu.make_async_copy(source, target, out_sems.at[len(stores)])
+            move.start()
+            stores.append(move)
+
+        def load_rows(source, target):
+            for rows in blocks:
+                load(source.at[rows, :], target.at[rows, :])
+
+        load(wk_hbm, wk_ref)
+        load_rows(k_hbm, k_ref)
+        load_rows(v_hbm, v_ref)
+        load(wq_hbm, wq_ref)
+        load_rows(q_hbm, q_ref)
+        load(gain_hbm, gain_ref)
+        for move in loads[:5]:
+            move.wait()
         for h, at in enumerate(cols):
             pre = dot(k_ref[:, at], wk_ref[h], 1, 0)
             kf_ref[:, at] = (pre / (1.0 + jnp.exp(-pre))).astype(BF)
-        waits[2]()
+            store(kf_ref.at[:, at], kf_hbm.at[:, at])
+        for move in loads[5:9]:
+            move.wait()
         for h, at in enumerate(cols):
             put_state(out_ref, h, dot(kf_ref[:, at], v_ref[:, at], 0, 0), 0)
-        for wait in waits[3:]:
-            wait()
+            own = pl.ds(h * per_head, per_head)
+            store(out_ref.at[own], out_hbm.at[own])
+        for move in loads[9:]:
+            move.wait()
+        for h, at in enumerate(cols):
+            row_ref[:, at] = jnp.broadcast_to(gain_ref[at].reshape(1, size), (8, size))
+        store(row_ref, row_hbm)
         for h, at in enumerate(cols):
             pre = dot(q_ref[:, at], wq_ref[h], 1, 0)
             qf_ref[:, at] = (pre / (1.0 + jnp.exp(-pre))).astype(BF)
-            row_ref[:, at] = jnp.broadcast_to(gain_ref[at].reshape(1, size), (8, size))
-
-    key_feat, query_feat, payload, gain_rows = run(
+            store(qf_ref.at[:, at], qf_hbm.at[:, at])
+        for move in stores:
+            move.wait()
+
+    anywhere = pl.BlockSpec(memory_space=pl.ANY)
+    inputs = [feat_key, key_rows, value_rows, feat_query, query_rows, norm_gain]
+    results = [
+        jax.ShapeDtypeStruct((tokens, width), BF),
+        jax.ShapeDtypeStruct((tokens, width), BF),
+        jax.ShapeDtypeStruct((near, chunk, size), BF),
+        jax.ShapeDtypeStruct((8, width), F32),
+    ]
+    key_feat, query_feat, payload, gain_rows = pl.pallas_call(
         state_kernel,
-        [((tokens, width), BF), ((tokens, width), BF), ((near, chunk, size), BF), ((8, width), F32)],
-        [],
-        fetch=[feat_key, key_rows, value_rows, feat_query, query_rows, norm_gain],
-        limit=WHOLE_VMEM,
-    )
+        out_shape=results,
+        in_specs=[anywhere] * len(inputs),
+        out_specs=[anywhere] * len(results),
+        scratch_shapes=[pltpu.VMEM(x.shape, x.dtype) for x in inputs + results]
+        + [pltpu.SemaphoreType.DMA((15,)), pltpu.SemaphoreType.DMA((3 * heads + 1,))],
+        compiler_params=pltpu.CompilerParams(vmem_limit_bytes=WHOLE_VMEM),
+        cost_estimate=pl.CostEstimate(flops=10**8, bytes_accessed=10**6, transcendentals=0),
+    )(*inputs)
     parts = swap(payload, "near")
 
     def total_kernel(in_ref, out_ref):
@@ -197,7 +232,7 @@
         for i in range(near):
             out_ref[i, 2 * chunk :, :] = rows
 
-    attended, delta, payload = run(
+    attended_near, delta, payload = run(
         delta_kernel,
         [((tokens, width), BF), ((tokens, width), BF), ((near, 2 * chunk + GAIN_ROWS, size), BF)],
         [stats, pre_norm, grad_out, gain_rows, query_feat, value_rows, key_feat, prior, query_rows, feat_query],
@@ -218,18 +253,16 @@
     )
     parts_far = swap(payload, "far")
 
-    def later_kernel(parts_ref, far_ref, out_ref, side_ref, gain_ref):
+    def later_kernel(parts_ref, far_ref, out_ref, side_ref):
         join(parts_ref, far_ref, out_ref, True)
         side = far_ref[0].astype(F32)[chunk:]
         for i in range(1, far):
             side = side + far_ref[i].astype(F32)[chunk:]
         side_ref[...] = side
-        for h, at in enumerate(cols):
-            gain_ref[at] = side[slim + h]
-
-    payload, side, grad_gain = run(
+
+    payload, side = run(
         later_kernel,
-        [((near, chunk, size), BF), ((slim + 8, size), F32), ((width,), F32)],
+        [((near, chunk, size), BF), ((slim + 8, size), F32)],
         [parts, parts_far],
     )
     later = swap(payload, "near")
@@ -251,9 +284,12 @@
     parts = swap(payload, "near")
 
     def last_kernel(
-        kpg_ref, wk_ref, l_ref, delta_ref, qf_ref, kf_ref, v_ref, p_ref, q_ref, wq_ref,
-        gk_ref, gq_ref, gv_ref, token_ref,
+        kpg_ref, wk_ref, l_ref, delta_ref, qf_ref, kf_ref, v_ref, p_ref, q_ref, wq_ref, att_ref, side_ref,
+        gk_ref, gq_ref, gv_ref, out_ref, gain_ref, token_ref,
     ):
+        out_ref[...] = att_ref[...]
+        for h, at in enumerate(cols):
+            gain_ref[at] = side_ref[slim + h]
         token_ref[...] = jnp.zeros(token_ref.shape, F32)
         mask, turned = causal_mask(tokens), causal_mask(tokens, 1)
         for h, at in enumerate(cols):
@@ -265,11 +301,12 @@
             value = dot(scores, delta, 1, 0) + dot(kf_ref[:, at], get_state(l_ref, h), 1, 0)
             gv_ref[:, at] = value.astype(BF)
 
-    grad_key, grad_query, grad_value, token = run(
+    grad_key, grad_query, grad_value, attended, grad_gain, token = run(
         last_kernel,
-        [((tokens, width), BF)] * 3 + [TOKEN],
+        [((tokens, width), BF)] * 4 + [((width,), F32), TOKEN],
         [
             key_pre_grad, feat_key, later, delta, query_feat, key_feat, value_rows, prior, query_rows, feat_query,
+            attended_near, side,
         ],
     )
 

time: 146 us -> 145 us (level)
    pallas_call x12 -> x11, Pallas kernels: 11.6 us -> 8.09 us  [run(): pl.pallas_call(body, out_shape=[jax.ShapeDtypeStruct(shape, dtype) for sh...]
    pallas_call x0 -> x1, Pallas kernels: none -> 2.79 us  [shards(): pl.pallas_call(state_kernel, out_shape=results, in_specs=[anywhere] * len...]
where the time goes in v9:
time: 145 us
  blocking collectives  125 us (86%)
  Pallas kernels  10.9 us (8%)
  waiting for transfers between devices  4.16 us (3%)
  starting transfers between devices  3.37 us (2%)
    all_to_all x9, blocking collectives, swap(): return lax.all_to_all(x, axis, 0, 0)  125 us
    pallas_call x11, Pallas kernels, run(): pl.pallas_call(body, out_shape=[jax.ShapeDtypeStruct(shape, dtype) for sh...  8.09 us
    all_to_all x1, waiting for transfers between devices, swap(): return lax.all_to_all(x, axis, 0, 0)  4.16 us
    all_to_all x1, starting transfers between devices, swap(): return lax.all_to_all(x, axis, 0, 0)  3.37 us
  transfers between devices with their start and end apart: 1, of which 1 were waited for; matrix products, arithmetic and copies ran while one was open for 0% of the time, Pallas kernels for 2%

profile of v9, /device:TPU:8, one launch (start us, length us, event | category | flops | bytes accessed | tf_op | source)
XLA Modules:
  0.0 144.7 jit_solution(7910039909915212803)
XLA Ops:
  0.6 2.8 %shard_map.126 = (bf16[256,512]{1,0:T(8,128)(2,1)}, bf16[256,512]{1,0:T(8,128)(2,1)}, bf16[8,64,128]{2,1,0:T(8,128)(2,1)}, f32[8,512]{1,0:T(8,128)}) custom-call(bf16[4,128,128]{2,1,0:T(8,128)(2,1)} %refs_1_.1, bf16[256,512]{1,0:T(8,128)(2,1)} %refs_5_.3, bf16[256,512]{1,0:T(8,128)(2,1)} %refs_6_.1, bf16[4,128,128]{2,1,0:T(8,128)(2,1)} %refs_9_.3, ...), custom_call_target="tpu_custom_call" | custom-call | flops 100000000 | bytes 1000000 | tf_op jit(solution)/shard_map/pallas_call | solution.py:135
  3.4 12.2 %all_to_all.50.refs_0_ = bf16[8,64,128]{2,1,0:T(8,128)(2,1)S(1)} all-to-all(bf16[8,64,128]{2,1,0:T(8,128)(2,1)} %get-tuple-element.30), channel_id=1, replica_groups=mesh['far'=8,'near'=8,'head'=8] {'near'}, dimensions={0} | all-to-all | bytes 262144 | tf_op jit(solution)/shard_map/all_to_all | solution.py:20
  15.7 0.0 copy-start.6
  15.7 0.0 copy-start.3
  15.7 27.9 %all_to_all.51.refs_1_ = bf16[8,64,128]{2,1,0:T(8,128)(2,1)S(1)} all-to-all(bf16[8,64,128]{2,1,0:T(8,128)(2,1)S(1)} %shard_map.127), channel_id=1, replica_groups=mesh['far'=8,'near'=8,'head'=8] {'far'}, dimensions={0} | all-to-all | bytes 262144 | tf_op jit(solution)/shard_map/all_to_all | solution.py:20
  43.6 0.0 copy-start
  43.6 0.0 copy-start.1
  43.6 0.1 shard_map.128
  43.7 0.0 copy-start.8
  43.7 10.0 %all_to_all.52.refs_3_.refs_7_ = bf16[8,64,128]{2,1,0:T(8,128)(2,1)S(1)} all-to-all(bf16[8,64,128]{2,1,0:T(8,128)(2,1)S(1)} %shard_map.128), channel_id=1, replica_groups=mesh['far'=8,'near'=8,'head'=8] {'near'}, dimensions={0} | all-to-all | bytes 262144 | tf_op jit(solution)/shard_map/all_to_all | solution.py:20
  53.7 0.0 copy-done.6
  53.7 0.0 copy-done.3
  53.7 0.0 copy-done
  53.7 0.0 copy-done.1
  53.7 0.0 copy-done.8
  53.7 0.0 copy-start.2
  53.8 0.8 shard_map.129
  54.6 0.0 copy-start.5
  54.6 9.0 %all_to_all.53.refs_0_ = f32[8,8,256]{2,1,0:T(8,128)S(1)} all-to-all(f32[8,8,256]{2,1,0:T(8,128)S(1)} %get-tuple-element.32), channel_id=1, replica_groups=mesh['far'=8,'near'=8,'head'=8] {'head'}, dimensions={0} | all-to-all | bytes 131072 | tf_op jit(solution)/shard_map/all_to_all | solution.py:20
  63.6 0.0 copy-done.2
  63.6 0.0 copy-done.5
  63.6 1.9 %shard_map.130 = (bf16[256,512]{1,0:T(8,128)(2,1)S(1)}, bf16[256,512]{1,0:T(8,128)(2,1)S(1)}, bf16[8,144,128]{2,1,0:T(8,128)(2,1)S(1)}) custom-call(f32[8,8,256]{2,1,0:T(8,128)S(1)} %all_to_all.53.refs_0_, f32[256,512]{1,0:T(8,128)S(1)} %get-tuple-element.33.refs_1_, bf16[256,512]{1,0:T(8,128)(2,1)S(1)} %copy-done.6, f32[8,512]{1,0:T(8,128)S(1)} %copy-done.8, ...), custom_call_target="tpu_custom_call" | custom-call | flops 100000000 | bytes 1000000 | tf_op jit(solution)/shard_map/pallas_call | solution.py:30
  65.5 10.4 %all_to_all.54.refs_0_ = bf16[8,144,128]{2,1,0:T(8,128)(2,1)S(1)} all-to-all(bf16[8,144,128]{2,1,0:T(8,128)(2,1)S(1)} %get-tuple-element.35), channel_id=1, replica_groups=mesh['far'=8,'near'=8,'head'=8] {'near'}, dimensions={0} | all-to-all | bytes 589824 | tf_op jit(solution)/shard_map/all_to_all | solution.py:20
  75.9 17.2 %all_to_all.55.refs_1_ = bf16[8,80,128]{2,1,0:T(8,128)(2,1)S(1)} all-to-all(bf16[8,80,128]{2,1,0:T(8,128)(2,1)S(1)} %shard_map.131), channel_id=1, replica_groups=mesh['far'=8,'near'=8,'head'=8] {'far'}, dimensions={0} | all-to-all | bytes 327680 | tf_op jit(solution)/shard_map/all_to_all | solution.py:20
  93.1 0.0 copy-start.7
  93.1 0.1 shard_map.132
  93.2 0.0 copy-start.4
  93.2 10.8 %all_to_all.56.refs_3_.refs_2_ = bf16[8,64,128]{2,1,0:T(8,128)(2,1)S(1)} all-to-all(bf16[8,64,128]{2,1,0:T(8,128)(2,1)S(1)} %get-tuple-element.36), channel_id=1, replica_groups=mesh['far'=8,'near'=8,'head'=8] {'near'}, dimensions={0} | all-to-all | bytes 262144 | tf_op jit(solution)/shard_map/all_to_all | solution.py:20
  104.0 0.0 copy-done.7
  104.0 0.0 copy-done.4
  104.0 1.9 %shard_map.133 = (bf16[256,512]{1,0:T(8,128)(2,1)S(1)}, bf16[8,64,128]{2,1,0:T(8,128)(2,1)}) custom-call(bf16[256,512]{1,0:T(8,128)(2,1)S(1)} %get-tuple-element.34.refs_0_.refs_3_, bf16[256,512]{1,0:T(8,128)(2,1)S(1)} %copy-done.1, bf16[256,512]{1,0:T(8,128)(2,1)S(1)} %copy-done, bf16[8,64,128]{2,1,0:T(8,128)(2,1)S(1)} %all_to_all.56.refs_3_.refs_2_, ...), custom_call_target="tpu_custom_call" | custom-call | flops 100000000 | bytes 1000000 | tf_op jit(solution)/shard_map/pallas_call | solution.py:30
  106.0 3.4 %all-to-all-start.7 = ((bf16[8,64,128]{2,1,0:T(8,128)(2,1)}), bf16[8,64,128]{2,1,0:T(8,128)(2,1)S(1)}, u32[]{:S(2)}, u32[]{:S(2)}) async-start(bf16[8,64,128]{2,1,0:T(8,128)(2,1)} %get-tuple-element.44), calls=%async_computation.7 | async-start | bytes 262144 | tf_op jit(solution)/shard_map/all_to_all | solution.py:20
  109.3 2.4 %shard_map.134 = (bf16[256,512]{1,0:T(8,128)(2,1)}, bf16[256,512]{1,0:T(8,128)(2,1)}, bf16[256,512]{1,0:T(8,128)(2,1)}, bf16[256,512]{1,0:T(8,128)(2,1)}, f32[512]{0:T(512)}, /*index=5*/f32[8,128]{1,0:T(8,128)S(1)}) custom-call(bf16[256,512]{1,0:T(8,128)(2,1)S(1)} %get-tuple-element.37.refs_0_, bf16[4,128,128]{2,1,0:T(8,128)(2,1)S(1)} %copy-done.4, ...), custom_call_target="tpu_custom_call" | custom-call | flops 100000000 | bytes 1000000 | tf_op jit(solution)/shard_map/pallas_call | solution.py:30
  111.7 4.2 %all-to-all-done.7.refs_0_ = bf16[8,64,128]{2,1,0:T(8,128)(2,1)S(1)} async-done(((bf16[8,64,128]{2,1,0:T(8,128)(2,1)}), bf16[8,64,128]{2,1,0:T(8,128)(2,1)S(1)}, u32[]{:S(2)}, u32[]{:S(2)}) %all-to-all-start.7) | async-done | bytes 131104 | tf_op jit(solution)/shard_map/all_to_all | solution.py:20
  115.9 18.3 %all_to_all.57.refs_0_ = bf16[8,80,128]{2,1,0:T(8,128)(2,1)S(1)} all-to-all(bf16[8,80,128]{2,1,0:T(8,128)(2,1)S(1)} %shard_map.135), channel_id=1, replica_groups=mesh['far'=8,'near'=8,'head'=8] {'far'}, dimensions={0} | all-to-all | bytes 327680 | tf_op jit(solution)/shard_map/all_to_all | solution.py:20
  134.2 9.6 %all_to_all.58.refs_0_ = bf16[8,128,128]{2,1,0:T(8,128)(2,1)S(1)} all-to-all(bf16[8,128,128]{2,1,0:T(8,128)(2,1)S(1)} %shard_map.136), channel_id=1, replica_groups=mesh['far'=8,'near'=8,'head'=8] {'near'}, dimensions={0} | all-to-all | bytes 524288 | tf_op jit(solution)/shard_map/all_to_all | solution.py:20
  143.8 0.8 shard_map.137
  (4 shorter events, 0.1 us)
Async XLA Ops:
  15.7 38.0 %copy-start.6 = (bf16[256,512]{1,0:T(8,128)(2,1)S(1)}, bf16[256,512]{1,0:T(8,128)(2,1)}, u32[]{:S(2)}) copy-start(bf16[256,512]{1,0:T(8,128)(2,1)} %refs_2_.4) | copy-start | bytes 786436
  15.7 38.0 %copy-start.3 = (bf16[256,512]{1,0:T(8,128)(2,1)S(1)}, bf16[256,512]{1,0:T(8,128)(2,1)}, u32[]{:S(2)}) copy-start(bf16[256,512]{1,0:T(8,128)(2,1)} %get-tuple-element.29.refs_1_.refs_6_.refs_5_) | copy-start | bytes 786436
  43.6 10.1 %copy-start = (bf16[256,512]{1,0:T(8,128)(2,1)S(1)}, bf16[256,512]{1,0:T(8,128)(2,1)}, u32[]{:S(2)}) copy-start(bf16[256,512]{1,0:T(8,128)(2,1)} %refs_6_.1) | copy-start | bytes 786436
  43.6 10.1 %copy-start.1 = (bf16[256,512]{1,0:T(8,128)(2,1)S(1)}, bf16[256,512]{1,0:T(8,128)(2,1)}, u32[]{:S(2)}) copy-start(bf16[256,512]{1,0:T(8,128)(2,1)} %get-tuple-element.28.refs_0_.refs_4_.refs_1_) | copy-start | bytes 786436
  43.7 10.1 %copy-start.8 = (f32[8,512]{1,0:T(8,128)S(1)}, f32[8,512]{1,0:T(8,128)}, u32[]{:S(2)}) copy-start(f32[8,512]{1,0:T(8,128)} %get-tuple-element.31.refs_5_.refs_3_) | copy-start | bytes 49156
  53.7 9.8 %copy-start.2 = (bf16[256,512]{1,0:T(8,128)(2,1)S(1)}, bf16[256,512]{1,0:T(8,128)(2,1)}, u32[]{:S(2)}) copy-start(bf16[256,512]{1,0:T(8,128)(2,1)} %refs_8_.3) | copy-start | bytes 786436
  54.6 9.0 %copy-start.5 = (bf16[4,128,128]{2,1,0:T(8,128)(2,1)S(1)}, bf16[4,128,128]{2,1,0:T(8,128)(2,1)}, u32[]{:S(2)}) copy-start(bf16[4,128,128]{2,1,0:T(8,128)(2,1)} %refs_9_.3) | copy-start | bytes 393220
  93.1 10.9 %copy-start.7 = (bf16[256,512]{1,0:T(8,128)(2,1)S(1)}, bf16[256,512]{1,0:T(8,128)(2,1)}, u32[]{:S(2)}) copy-start(bf16[256,512]{1,0:T(8,128)(2,1)} %refs_5_.3) | copy-start | bytes 786436
  93.2 10.8 %copy-start.4 = (bf16[4,128,128]{2,1,0:T(8,128)(2,1)S(1)}, bf16[4,128,128]{2,1,0:T(8,128)(2,1)}, u32[]{:S(2)}) copy-start(bf16[4,128,128]{2,1,0:T(8,128)(2,1)} %refs_1_.1) | copy-start | bytes 393220
  106.0 9.9 %all-to-all-start.7 = ((bf16[8,64,128]{2,1,0:T(8,128)(2,1)}), bf16[8,64,128]{2,1,0:T(8,128)(2,1)S(1)}, u32[]{:S(2)}, u32[]{:S(2)}) async-start(bf16[8,64,128]{2,1,0:T(8,128)(2,1)} %get-tuple-element.44), calls=%async_computation.7 | async-start | bytes 262144 | tf_op jit(solution)/shard_map/all_to_all | solution.py:20

commit v10 on v9

--- a/solution.py
+++ b/solution.py
@@ -197,6 +197,18 @@
     )
     stats = swap(payload, "head")
 
+    def slope_kernel(q_ref, wq_ref, k_ref, wk_ref, qs_ref, ks_ref):
+        for h, at in enumerate(cols):
+            qs_ref[:, at] = silu_slope(dot(q_ref[:, at], wq_ref[h], 1, 0)).astype(BF)
+            ks_ref[:, at] = silu_slope(dot(k_ref[:, at], wk_ref[h], 1, 0)).astype(BF)
+
+    query_slope, key_slope = run(
+        slope_kernel,
+        [((tokens, width), BF), ((tokens, width), BF)],
+        [query_rows, feat_query, key_rows, feat_key],
+        after=[pre_norm],
+    )
+
     def row_factors(st_ref):
         rows = st_ref[0]
         for i in range(1, peers):
@@ -206,13 +218,13 @@
         inverse = 1.0 / jnp.sqrt(both[:, 0:1] / full_width + EPSILON)
         return inverse, both[:, 1:2] * inverse / full_width
 
-    def query_side(h, at, delta, mask, v_ref, kf_ref, p_ref, q_ref, wq_ref):
+    def query_side(h, at, delta, mask, v_ref, kf_ref, p_ref, qs_ref):
         back = jnp.where(mask, dot(delta, v_ref[:, at], 1, 1), 0.0).astype(BF)
         grad = dot(back, kf_ref[:, at], 1, 0) + dot(delta, get_state(p_ref, h), 1, 1)
-        return (grad * silu_slope(dot(q_ref[:, at], wq_ref[h], 1, 0))).astype(BF)
+        return (grad * qs_ref[:, at].astype(F32)).astype(BF)
 
     def delta_kernel(
-        st_ref, pre_ref, go_ref, gain_ref, qf_ref, v_ref, kf_ref, p_ref, q_ref, wq_ref, att_ref, delta_ref, out_ref
+        st_ref, pre_ref, go_ref, gain_ref, qf_ref, v_ref, kf_ref, p_ref, q_ref, qs_ref, att_ref, delta_ref, out_ref
     ):
         inverse, slope = row_factors(st_ref)
         mask = causal_mask(tokens)
@@ -225,7 +237,7 @@
             att_ref[:, at] = (normed * gain_ref[:1, at]).astype(BF)
             gains.append(jnp.sum(wide * normed, axis=0, keepdims=True))
             put_state(out_ref, h, dot(qf_ref[:, at], delta, 0, 0), 0)
-            grad = query_side(h, at, delta, mask, v_ref, kf_ref, p_ref, q_ref, wq_ref)
+            grad = query_side(h, at, delta, mask, v_ref, kf_ref, p_ref, qs_ref)
             put_state(out_ref, h, dot(q_ref[:, at], grad, 0, 0), chunk)
         rest = [jnp.zeros((GAIN_ROWS - heads, size), F32)]
         rows = jnp.concatenate(gains + rest, axis=0).astype(BF)
@@ -235,7 +247,7 @@
     attended_near, delta, payload = run(
         delta_kernel,
         [((tokens, width), BF), ((tokens, width), BF), ((near, 2 * chunk + GAIN_ROWS, size), BF)],
-        [stats, pre_norm, grad_out, gain_rows, query_feat, value_rows, key_feat, prior, query_rows, feat_query],
+        [stats, pre_norm, grad_out, gain_rows, query_feat, value_rows, key_feat, prior, query_rows, query_slope],
     )
     parts = swap(payload, "near")
 
@@ -267,24 +279,24 @@
     )
     later = swap(payload, "near")
 
-    def key_kernel(delta_ref, qf_ref, v_ref, l_ref, wk_ref, k_ref, kpg_ref, out_ref):
+    def key_kernel(delta_ref, qf_ref, v_ref, l_ref, ks_ref, k_ref, kpg_ref, out_ref):
         turned = causal_mask(tokens, 1)
         for h, at in enumerate(cols):
             back = jnp.where(turned, dot(v_ref[:, at], delta_ref[:, at], 1, 1), 0.0).astype(BF)
             grad = dot(back, qf_ref[:, at], 1, 0) + dot(v_ref[:, at], get_state(l_ref, h), 1, 1)
-            grad = (grad * silu_slope(dot(k_ref[:, at], wk_ref[h], 1, 0))).astype(BF)
+            grad = (grad * ks_ref[:, at].astype(F32)).astype(BF)
             kpg_ref[:, at] = grad
             put_state(out_ref, h, dot(k_ref[:, at], grad, 0, 0), 0)
 
     key_pre_grad, payload = run(
         key_kernel,
         [((tokens, width), BF), ((near, chunk, size), BF)],
-        [delta, query_feat, value_rows, later, feat_key, key_rows],
+        [delta, query_feat, value_rows, later, key_slope, key_rows],
     )
     parts = swap(payload, "near")
 
     def last_kernel(
-        kpg_ref, wk_ref, l_ref, delta_ref, qf_ref, kf_ref, v_ref, p_ref, q_ref, wq_ref, att_ref, side_ref,
+        kpg_ref, wk_ref, l_ref, delta_ref, qf_ref, kf_ref, v_ref, p_ref, qs_ref, wq_ref, att_ref, side_ref,
         gk_ref, gq_ref, gv_ref, out_ref, gain_ref, token_ref,
     ):
         out_ref[...] = att_ref[...]
@@ -295,7 +307,7 @@
         for h, at in enumerate(cols):
             gk_ref[:, at] = dot(kpg_ref[:, at], wk_ref[h], 1, 1).astype(BF)
             delta = delta_ref[:, at]
-            grad = query_side(h, at, delta, mask, v_ref, kf_ref, p_ref, q_ref, wq_ref)
+            grad = query_side(h, at, delta, mask, v_ref, kf_ref, p_ref, qs_ref)
             gq_ref[:, at] = dot(grad, wq_ref[h], 1, 1).astype(BF)
             scores = jnp.where(turned, dot(kf_ref[:, at], qf_ref[:, at], 1, 1), 0.0).astype(BF)
             value = dot(scores, delta, 1, 0) + dot(kf_ref[:, at], get_state(l_ref, h), 1, 0)
@@ -305,7 +317,7 @@
         last_kernel,
         [((tokens, width), BF)] * 4 + [((width,), F32), TOKEN],
         [
-            key_pre_grad, feat_key, later, delta, query_feat, key_feat, value_rows, prior, query_rows, feat_query,
+            key_pre_grad, feat_key, later, delta, query_feat, key_feat, value_rows, prior, query_slope, feat_query,
             attended_near, side,
         ],
     )
@@ -339,16 +351,31 @@
     (payload,) = run(weight_kernel, [((near, 2 * chunk, size), BF)], [parts_far])
     done = swap(payload, "near")
 
-    def widen_kernel(in_ref, gq_ref, gk_ref):
+    def widen_kernel(in_ref, gq_hbm, gk_hbm, gq_ref, gk_ref, sems):
+        moves = []
         for h in range(heads):
             for part in range(per_head):
                 rows = slice(part * chunk, (part + 1) * chunk)
                 gk_ref[h, rows] = in_ref[h * per_head + part, :chunk].astype(F32)
                 gq_ref[h, rows] = in_ref[h * per_head + part, chunk:].astype(F32)
-
-    grad_feat_query, grad_feat_key = run(
-        widen_kernel, [(feat_query.shape, F32), (feat_key.shape, F32)], [done]
-    )
+            for held, out in ((gk_ref, gk_hbm), (gq_ref, gq_hbm)):
+                move = pltpu.make_async_copy(held.at[h], out.at[h], sems.at[len(moves)])
+                move.start()
+                moves.append(move)
+        for move in moves:
+            move.wait()
+
+    shapes = [jax.ShapeDtypeStruct(x.shape, F32) for x in (feat_query, feat_key)]
+    grad_feat_query, grad_feat_key = pl.pallas_call(
+        widen_kernel,
+        out_shape=shapes,
+        in_specs=[pl.BlockSpec(memory_space=pltpu.VMEM)],
+        out_specs=[anywhere] * 2,
+        scratch_shapes=[pltpu.VMEM(x.shape, F32) for x in shapes]
+        + [pltpu.SemaphoreType.DMA((2 * heads,))],
+        compiler_params=pltpu.CompilerParams(vmem_limit_bytes=VMEM_BYTES),
+        cost_estimate=pl.CostEstimate(flops=10**6, bytes_accessed=10**6, transcendentals=0),
+    )(done)
     return (attended, grad_query, grad_key, grad_value, grad_feat_query, grad_feat_key, grad_gain)
 
 

time: 145 us -> 146 us (level)
  blocking collectives: 125 us -> 116 us
  starting transfers between devices: 3.37 us -> 8.42 us
  waiting for transfers between devices: 4.16 us -> 6.73 us
  Pallas kernels: 10.9 us -> 12.4 us
    all_to_all x9 -> x8, blocking collectives: 125 us -> 116 us  [swap(): return lax.all_to_all(x, axis, 0, 0)]
    all_to_all x1 -> x2, starting transfers between devices: 3.37 us -> 8.42 us  [swap(): return lax.all_to_all(x, axis, 0, 0)]
    all_to_all x1 -> x2, waiting for transfers between devices: 4.16 us -> 6.73 us  [swap(): return lax.all_to_all(x, axis, 0, 0)]
  transfers between devices with their start and end apart: 1 -> 2, of which waited for: 1 -> 2; matrix products, arithmetic and copies ran while one was open for 0% -> 0% of each run, Pallas kernels for 2% -> 2%
where the time goes in v10:
time: 146 us; the launch traced here: 145 us
  blocking collectives  116 us (79%)
  Pallas kernels  12.4 us (8%)
  starting transfers between devices  8.42 us (6%)
  waiting for transfers between devices  6.73 us (5%)
    all_to_all x8, blocking collectives, swap(): return lax.all_to_all(x, axis, 0, 0)  116 us
    pallas_call x11, Pallas kernels, run(): pl.pallas_call(body, out_shape=[jax.ShapeDtypeStruct(shape, dtype) for sh...  8.8 us
    all_to_all x2, starting transfers between devices, swap(): return lax.all_to_all(x, axis, 0, 0)  8.42 us
    all_to_all x2, waiting for transfers between devices, swap(): return lax.all_to_all(x, axis, 0, 0)  6.73 us
  transfers between devices with their start and end apart: 2, of which 2 were waited for; matrix products, arithmetic and copies ran while one was open for 0% of the time, Pallas kernels for 2%

profile of v10, /device:TPU:8, one launch (start us, length us, event | category | flops | bytes accessed | tf_op | source)
XLA Modules:
  0.0 145.4 jit_solution(6205455663484665868)
XLA Ops:
  0.6 2.8 %shard_map.126 = (bf16[256,512]{1,0:T(8,128)(2,1)}, bf16[256,512]{1,0:T(8,128)(2,1)}, bf16[8,64,128]{2,1,0:T(8,128)(2,1)}, f32[8,512]{1,0:T(8,128)}) custom-call(bf16[4,128,128]{2,1,0:T(8,128)(2,1)} %refs_1_.3, bf16[256,512]{1,0:T(8,128)(2,1)} %refs_5_.3, bf16[256,512]{1,0:T(8,128)(2,1)} %refs_6_.1, bf16[4,128,128]{2,1,0:T(8,128)(2,1)} %refs_9_.1, ...), custom_call_target="tpu_custom_call" | custom-call | flops 100000000 | bytes 1000000 | tf_op jit(solution)/shard_map/pallas_call | solution.py:135
  3.4 12.2 %all_to_all.50.refs_0_ = bf16[8,64,128]{2,1,0:T(8,128)(2,1)S(1)} all-to-all(bf16[8,64,128]{2,1,0:T(8,128)(2,1)} %get-tuple-element.32), channel_id=1, replica_groups=mesh['far'=8,'near'=8,'head'=8] {'near'}, dimensions={0} | all-to-all | bytes 262144 | tf_op jit(solution)/shard_map/all_to_all | solution.py:20
  15.7 0.0 copy-start.7
  15.7 0.0 copy-start.3
  15.7 27.9 %all_to_all.51.refs_1_ = bf16[8,64,128]{2,1,0:T(8,128)(2,1)S(1)} all-to-all(bf16[8,64,128]{2,1,0:T(8,128)(2,1)S(1)} %shard_map.127), channel_id=1, replica_groups=mesh['far'=8,'near'=8,'head'=8] {'far'}, dimensions={0} | all-to-all | bytes 262144 | tf_op jit(solution)/shard_map/all_to_all | solution.py:20
  43.6 0.0 copy-start
  43.6 0.0 copy-start.1
  43.6 0.1 shard_map.128
  43.7 0.0 copy-start.10
  43.7 10.0 %all_to_all.52.refs_3_.refs_7_ = bf16[8,64,128]{2,1,0:T(8,128)(2,1)S(1)} all-to-all(bf16[8,64,128]{2,1,0:T(8,128)(2,1)S(1)} %shard_map.128), channel_id=1, replica_groups=mesh['far'=8,'near'=8,'head'=8] {'near'}, dimensions={0} | all-to-all | bytes 262144 | tf_op jit(solution)/shard_map/all_to_all | solution.py:20
  53.7 0.0 copy-done.7
  53.7 0.0 copy-done.3
  53.7 0.0 copy-done
  53.7 0.0 copy-done.1
  53.7 0.0 copy-done.10
  53.7 0.0 copy-start.2
  53.8 0.0 copy-start.4
  53.8 0.0 copy-start.6
  53.8 1.4 shard_map.129
  55.2 0.0 copy-start.5
  55.2 5.0 %all-to-all-start.3 = ((f32[8,8,256]{2,1,0:T(8,128)}), f32[8,8,256]{2,1,0:T(8,128)S(1)}, u32[]{:S(2)}, u32[]{:S(2)}) async-start(f32[8,8,256]{2,1,0:T(8,128)} %get-tuple-element.34), calls=%async_computation.3 | async-start | bytes 131072 | tf_op jit(solution)/shard_map/all_to_all | solution.py:20
  60.3 0.0 copy-done.2
  60.3 0.0 copy-done.4
  60.3 0.0 copy-done.6
  60.3 0.0 copy-done.5
  60.3 0.5 shard_map.130
  60.8 0.0 copy-start.8
  60.8 0.7 copy-done.8
  61.5 2.9 %all-to-all-done.3.refs_0_ = f32[8,8,256]{2,1,0:T(8,128)S(1)} async-done(((f32[8,8,256]{2,1,0:T(8,128)}), f32[8,8,256]{2,1,0:T(8,128)S(1)}, u32[]{:S(2)}, u32[]{:S(2)}) %all-to-all-start.3) | async-done | bytes 65568 | tf_op jit(solution)/shard_map/all_to_all | solution.py:20
  64.4 1.7 %shard_map.131 = (bf16[256,512]{1,0:T(8,128)(2,1)S(1)}, bf16[256,512]{1,0:T(8,128)(2,1)S(1)}, bf16[8,144,128]{2,1,0:T(8,128)(2,1)S(1)}) custom-call(f32[8,8,256]{2,1,0:T(8,128)S(1)} %all-to-all-done.3.refs_0_, f32[256,512]{1,0:T(8,128)S(1)} %get-tuple-element.35.refs_4_.refs_1_, bf16[256,512]{1,0:T(8,128)(2,1)S(1)} %copy-done.7, f32[8,512]{1,0:T(8,128)S(1)} %copy-done.10, ...), custom_call_target="tpu_custom_call" | custom-call | flops 100000000 | bytes 1000000 | tf_op jit(solution)/shard_map/pallas_call | solution.py:30
  66.2 10.4 %all_to_all.53.refs_0_ = bf16[8,144,128]{2,1,0:T(8,128)(2,1)S(1)} all-to-all(bf16[8,144,128]{2,1,0:T(8,128)(2,1)S(1)} %get-tuple-element.38), channel_id=1, replica_groups=mesh['far'=8,'near'=8,'head'=8] {'near'}, dimensions={0} | all-to-all | bytes 589824 | tf_op jit(solution)/shard_map/all_to_all | solution.py:20
  76.6 17.2 %all_to_all.54.refs_1_ = bf16[8,80,128]{2,1,0:T(8,128)(2,1)S(1)} all-to-all(bf16[8,80,128]{2,1,0:T(8,128)(2,1)S(1)} %shard_map.132), channel_id=1, replica_groups=mesh['far'=8,'near'=8,'head'=8] {'far'}, dimensions={0} | all-to-all | bytes 327680 | tf_op jit(solution)/shard_map/all_to_all | solution.py:20
  93.8 0.0 copy-start.9
  93.8 0.1 shard_map.133
  93.8 10.7 %all_to_all.55.refs_3_.refs_2_ = bf16[8,64,128]{2,1,0:T(8,128)(2,1)S(1)} all-to-all(bf16[8,64,128]{2,1,0:T(8,128)(2,1)S(1)} %get-tuple-element.39), channel_id=1, replica_groups=mesh['far'=8,'near'=8,'head'=8] {'near'}, dimensions={0} | all-to-all | bytes 262144 | tf_op jit(solution)/shard_map/all_to_all | solution.py:20
  104.5 0.0 copy-done.9
  104.5 2.2 %shard_map.134 = (bf16[256,512]{1,0:T(8,128)(2,1)S(1)}, bf16[8,64,128]{2,1,0:T(8,128)(2,1)}) custom-call(bf16[256,512]{1,0:T(8,128)(2,1)S(1)} %get-tuple-element.37.refs_0_.refs_3_, bf16[256,512]{1,0:T(8,128)(2,1)S(1)} %copy-done.1, bf16[256,512]{1,0:T(8,128)(2,1)S(1)} %copy-done, bf16[8,64,128]{2,1,0:T(8,128)(2,1)S(1)} %all_to_all.55.refs_3_.refs_2_, ...), custom_call_target="tpu_custom_call" | custom-call | flops 100000000 | bytes 1000000 | tf_op jit(solution)/shard_map/pallas_call | solution.py:30
  106.7 3.4 %all-to-all-start.7 = ((bf16[8,64,128]{2,1,0:T(8,128)(2,1)}), bf16[8,64,128]{2,1,0:T(8,128)(2,1)S(1)}, u32[]{:S(2)}, u32[]{:S(2)}) async-start(bf16[8,64,128]{2,1,0:T(8,128)(2,1)} %get-tuple-element.48), calls=%async_computation.7 | async-start | bytes 262144 | tf_op jit(solution)/shard_map/all_to_all | solution.py:20
  110.1 2.7 %shard_map.135 = (bf16[256,512]{1,0:T(8,128)(2,1)}, bf16[256,512]{1,0:T(8,128)(2,1)}, bf16[256,512]{1,0:T(8,128)(2,1)}, bf16[256,512]{1,0:T(8,128)(2,1)}, f32[512]{0:T(512)}, /*index=5*/f32[8,128]{1,0:T(8,128)S(1)}) custom-call(bf16[256,512]{1,0:T(8,128)(2,1)S(1)} %get-tuple-element.41.refs_0_, bf16[4,128,128]{2,1,0:T(8,128)(2,1)S(1)} %copy-done.5, ...), custom_call_target="tpu_custom_call" | custom-call | flops 100000000 | bytes 1000000 | tf_op jit(solution)/shard_map/pallas_call | solution.py:30
  112.8 3.8 %all-to-all-done.7.refs_0_ = bf16[8,64,128]{2,1,0:T(8,128)(2,1)S(1)} async-done(((bf16[8,64,128]{2,1,0:T(8,128)(2,1)}), bf16[8,64,128]{2,1,0:T(8,128)(2,1)S(1)}, u32[]{:S(2)}, u32[]{:S(2)}) %all-to-all-start.7) | async-done | bytes 131104 | tf_op jit(solution)/shard_map/all_to_all | solution.py:20
  116.6 18.2 %all_to_all.56.refs_0_ = bf16[8,80,128]{2,1,0:T(8,128)(2,1)S(1)} all-to-all(bf16[8,80,128]{2,1,0:T(8,128)(2,1)S(1)} %shard_map.136), channel_id=1, replica_groups=mesh['far'=8,'near'=8,'head'=8] {'far'}, dimensions={0} | all-to-all | bytes 327680 | tf_op jit(solution)/shard_map/all_to_all | solution.py:20
  134.9 9.6 %all_to_all.57.in_ref = bf16[8,128,128]{2,1,0:T(8,128)(2,1)S(1)} all-to-all(bf16[8,128,128]{2,1,0:T(8,128)(2,1)S(1)} %shard_map.137), channel_id=1, replica_groups=mesh['far'=8,'near'=8,'head'=8] {'near'}, dimensions={0} | all-to-all | bytes 524288 | tf_op jit(solution)/shard_map/all_to_all | solution.py:20
  144.6 0.9 shard_map.138
  (4 shorter events, 0.1 us)
Async XLA Ops:
  15.7 38.0 %copy-start.7 = (bf16[256,512]{1,0:T(8,128)(2,1)S(1)}, bf16[256,512]{1,0:T(8,128)(2,1)}, u32[]{:S(2)}) copy-start(bf16[256,512]{1,0:T(8,128)(2,1)} %refs_2_.6) | copy-start | bytes 786436
  15.7 38.0 %copy-start.3 = (bf16[256,512]{1,0:T(8,128)(2,1)S(1)}, bf16[256,512]{1,0:T(8,128)(2,1)}, u32[]{:S(2)}) copy-start(bf16[256,512]{1,0:T(8,128)(2,1)} %get-tuple-element.31.refs_1_.refs_6_.refs_5_) | copy-start | bytes 786436
  43.6 10.1 %copy-start = (bf16[256,512]{1,0:T(8,128)(2,1)S(1)}, bf16[256,512]{1,0:T(8,128)(2,1)}, u32[]{:S(2)}) copy-start(bf16[256,512]{1,0:T(8,128)(2,1)} %refs_6_.1) | copy-start | bytes 786436
  43.6 10.1 %copy-start.1 = (bf16[256,512]{1,0:T(8,128)(2,1)S(1)}, bf16[256,512]{1,0:T(8,128)(2,1)}, u32[]{:S(2)}) copy-start(bf16[256,512]{1,0:T(8,128)(2,1)} %get-tuple-element.30.refs_0_.refs_4_.refs_1_) | copy-start | bytes 786436
  43.7 10.1 %copy-start.10 = (f32[8,512]{1,0:T(8,128)S(1)}, f32[8,512]{1,0:T(8,128)}, u32[]{:S(2)}) copy-start(f32[8,512]{1,0:T(8,128)} %get-tuple-element.33.refs_5_.refs_3_) | copy-start | bytes 49156
  53.7 6.5 %copy-start.2 = (bf16[256,512]{1,0:T(8,128)(2,1)S(1)}, bf16[256,512]{1,0:T(8,128)(2,1)}, u32[]{:S(2)}) copy-start(bf16[256,512]{1,0:T(8,128)(2,1)} %refs_8_.1) | copy-start | bytes 786436
  53.8 6.5 %copy-start.4 = (bf16[256,512]{1,0:T(8,128)(2,1)S(1)}, bf16[256,512]{1,0:T(8,128)(2,1)}, u32[]{:S(2)}) copy-start(bf16[256,512]{1,0:T(8,128)(2,1)} %refs_5_.3) | copy-start | bytes 786436
  53.8 6.5 %copy-start.6 = (bf16[4,128,128]{2,1,0:T(8,128)(2,1)S(1)}, bf16[4,128,128]{2,1,0:T(8,128)(2,1)}, u32[]{:S(2)}) copy-start(bf16[4,128,128]{2,1,0:T(8,128)(2,1)} %refs_9_.1) | copy-start | bytes 393220
  55.2 5.1 %copy-start.5 = (bf16[4,128,128]{2,1,0:T(8,128)(2,1)S(1)}, bf16[4,128,128]{2,1,0:T(8,128)(2,1)}, u32[]{:S(2)}) copy-start(bf16[4,128,128]{2,1,0:T(8,128)(2,1)} %refs_1_.3) | copy-start | bytes 393220
  55.2 9.2 %all-to-all-start.3 = ((f32[8,8,256]{2,1,0:T(8,128)}), f32[8,8,256]{2,1,0:T(8,128)S(1)}, u32[]{:S(2)}, u32[]{:S(2)}) async-start(f32[8,8,256]{2,1,0:T(8,128)} %get-tuple-element.34), calls=%async_computation.3 | async-start | bytes 131072 | tf_op jit(solution)/shard_map/all_to_all | solution.py:20
  60.8 0.7 copy-start.8
  93.8 10.8 %copy-start.9 = (bf16[256,512]{1,0:T(8,128)(2,1)S(1)}, bf16[256,512]{1,0:T(8,128)(2,1)}, u32[]{:S(2)}) copy-start(bf16[256,512]{1,0:T(8,128)(2,1)} %copy-done.8) | copy-start | bytes 786436
  106.7 9.9 %all-to-all-start.7 = ((bf16[8,64,128]{2,1,0:T(8,128)(2,1)}), bf16[8,64,128]{2,1,0:T(8,128)(2,1)S(1)}, u32[]{:S(2)}, u32[]{:S(2)}) async-start(bf16[8,64,128]{2,1,0:T(8,128)(2,1)} %get-tuple-element.48), calls=%async_computation.7 | async-start | bytes 262144 | tf_op jit(solution)/shard_map/all_to_all | solution.py:20

commit v11 on v9

--- a/solution.py
+++ b/solution.py
@@ -41,8 +41,13 @@
     return lax.dot_general(a, b, (((over_a,), (over_b,)), ((), ())), preferred_element_type=F32)
 
 
+def silu(x):
+    half = 0.5 * x
+    return half + half * jnp.tanh(half)
+
+
 def silu_slope(x):
-    g = 1.0 / (1.0 + jnp.exp(-x))
+    g = 0.5 + 0.5 * jnp.tanh(0.5 * x)
     return g * (1.0 + x * (1.0 - g))
 
 
@@ -104,7 +109,7 @@
             move.wait()
         for h, at in enumerate(cols):
             pre = dot(k_ref[:, at], wk_ref[h], 1, 0)
-            kf_ref[:, at] = (pre / (1.0 + jnp.exp(-pre))).astype(BF)
+            kf_ref[:, at] = silu(pre).astype(BF)
             store(kf_ref.at[:, at], kf_hbm.at[:, at])
         for move in loads[5:9]:
             move.wait()
@@ -119,7 +124,7 @@
         store(row_ref, row_hbm)
         for h, at in enumerate(cols):
             pre = dot(q_ref[:, at], wq_ref[h], 1, 0)
-            qf_ref[:, at] = (pre / (1.0 + jnp.exp(-pre))).astype(BF)
+            qf_ref[:, at] = silu(pre).astype(BF)
             store(qf_ref.at[:, at], qf_hbm.at[:, at])
         for move in stores:
             move.wait()

time: 145 us -> 145 us (level)
  no operation moved by 1% of the time
where the time goes in v11:
time: 145 us
  blocking collectives  125 us (86%)
  Pallas kernels  10.8 us (7%)
  waiting for transfers between devices  4.16 us (3%)
  starting transfers between devices  3.37 us (2%)
    all_to_all x9, blocking collectives, swap(): return lax.all_to_all(x, axis, 0, 0)  125 us
    pallas_call x11, Pallas kernels, run(): pl.pallas_call(body, out_shape=[jax.ShapeDtypeStruct(shape, dtype) for sh...  8.08 us
    all_to_all x1, waiting for transfers between devices, swap(): return lax.all_to_all(x, axis, 0, 0)  4.16 us
    all_to_all x1, starting transfers between devices, swap(): return lax.all_to_all(x, axis, 0, 0)  3.37 us
  transfers between devices with their start and end apart: 1, of which 1 were waited for; matrix products, arithmetic and copies ran while one was open for 0% of the time, Pallas kernels for 2%

profile of v11, /device:TPU:8, one launch (start us, length us, event | category | flops | bytes accessed | tf_op | source)
XLA Modules:
  0.0 144.6 jit_solution(6782242533452205797)
XLA Ops:
  0.6 2.7 %shard_map.126 = (bf16[256,512]{1,0:T(8,128)(2,1)}, bf16[256,512]{1,0:T(8,128)(2,1)}, bf16[8,64,128]{2,1,0:T(8,128)(2,1)}, f32[8,512]{1,0:T(8,128)}) custom-call(bf16[4,128,128]{2,1,0:T(8,128)(2,1)} %refs_1_.1, bf16[256,512]{1,0:T(8,128)(2,1)} %refs_5_.3, bf16[256,512]{1,0:T(8,128)(2,1)} %refs_6_.1, bf16[4,128,128]{2,1,0:T(8,128)(2,1)} %refs_9_.3, ...), custom_call_target="tpu_custom_call" | custom-call | flops 100000000 | bytes 1000000 | tf_op jit(solution)/shard_map/pallas_call | solution.py:140
  3.4 12.2 %all_to_all.50.refs_0_ = bf16[8,64,128]{2,1,0:T(8,128)(2,1)S(1)} all-to-all(bf16[8,64,128]{2,1,0:T(8,128)(2,1)} %get-tuple-element.30), channel_id=1, replica_groups=mesh['far'=8,'near'=8,'head'=8] {'near'}, dimensions={0} | all-to-all | bytes 262144 | tf_op jit(solution)/shard_map/all_to_all | solution.py:20
  15.6 0.0 copy-start.6
  15.6 0.0 copy-start.3
  15.6 27.9 %all_to_all.51.refs_1_ = bf16[8,64,128]{2,1,0:T(8,128)(2,1)S(1)} all-to-all(bf16[8,64,128]{2,1,0:T(8,128)(2,1)S(1)} %shard_map.127), channel_id=1, replica_groups=mesh['far'=8,'near'=8,'head'=8] {'far'}, dimensions={0} | all-to-all | bytes 262144 | tf_op jit(solution)/shard_map/all_to_all | solution.py:20
  43.5 0.0 copy-start
  43.5 0.0 copy-start.1
  43.5 0.1 shard_map.128
  43.6 0.0 copy-start.8
  43.6 10.0 %all_to_all.52.refs_3_.refs_7_ = bf16[8,64,128]{2,1,0:T(8,128)(2,1)S(1)} all-to-all(bf16[8,64,128]{2,1,0:T(8,128)(2,1)S(1)} %shard_map.128), channel_id=1, replica_groups=mesh['far'=8,'near'=8,'head'=8] {'near'}, dimensions={0} | all-to-all | bytes 262144 | tf_op jit(solution)/shard_map/all_to_all | solution.py:20
  53.6 0.0 copy-done.6
  53.6 0.0 copy-done.3
  53.6 0.0 copy-done
  53.6 0.0 copy-done.1
  53.7 0.0 copy-done.8
  53.7 0.0 copy-start.2
  53.7 0.8 shard_map.129
  54.5 0.0 copy-start.5
  54.5 9.0 %all_to_all.53.refs_0_ = f32[8,8,256]{2,1,0:T(8,128)S(1)} all-to-all(f32[8,8,256]{2,1,0:T(8,128)S(1)} %get-tuple-element.32), channel_id=1, replica_groups=mesh['far'=8,'near'=8,'head'=8] {'head'}, dimensions={0} | all-to-all | bytes 131072 | tf_op jit(solution)/shard_map/all_to_all | solution.py:20
  63.5 0.0 copy-done.2
  63.5 0.0 copy-done.5
  63.5 1.9 %shard_map.130 = (bf16[256,512]{1,0:T(8,128)(2,1)S(1)}, bf16[256,512]{1,0:T(8,128)(2,1)S(1)}, bf16[8,144,128]{2,1,0:T(8,128)(2,1)S(1)}) custom-call(f32[8,8,256]{2,1,0:T(8,128)S(1)} %all_to_all.53.refs_0_, f32[256,512]{1,0:T(8,128)S(1)} %get-tuple-element.33.refs_1_, bf16[256,512]{1,0:T(8,128)(2,1)S(1)} %copy-done.6, f32[8,512]{1,0:T(8,128)S(1)} %copy-done.8, ...), custom_call_target="tpu_custom_call" | custom-call | flops 100000000 | bytes 1000000 | tf_op jit(solution)/shard_map/pallas_call | solution.py:30
  65.4 10.4 %all_to_all.54.refs_0_ = bf16[8,144,128]{2,1,0:T(8,128)(2,1)S(1)} all-to-all(bf16[8,144,128]{2,1,0:T(8,128)(2,1)S(1)} %get-tuple-element.35), channel_id=1, replica_groups=mesh['far'=8,'near'=8,'head'=8] {'near'}, dimensions={0} | all-to-all | bytes 589824 | tf_op jit(solution)/shard_map/all_to_all | solution.py:20
  75.8 17.2 %all_to_all.55.refs_1_ = bf16[8,80,128]{2,1,0:T(8,128)(2,1)S(1)} all-to-all(bf16[8,80,128]{2,1,0:T(8,128)(2,1)S(1)} %shard_map.131), channel_id=1, replica_groups=mesh['far'=8,'near'=8,'head'=8] {'far'}, dimensions={0} | all-to-all | bytes 327680 | tf_op jit(solution)/shard_map/all_to_all | solution.py:20
  93.0 0.0 copy-start.7
  93.0 0.1 shard_map.132
  93.1 0.0 copy-start.4
  93.1 10.8 %all_to_all.56.refs_3_.refs_2_ = bf16[8,64,128]{2,1,0:T(8,128)(2,1)S(1)} all-to-all(bf16[8,64,128]{2,1,0:T(8,128)(2,1)S(1)} %get-tuple-element.36), channel_id=1, replica_groups=mesh['far'=8,'near'=8,'head'=8] {'near'}, dimensions={0} | all-to-all | bytes 262144 | tf_op jit(solution)/shard_map/all_to_all | solution.py:20
  103.9 0.0 copy-done.7
  103.9 0.0 copy-done.4
  103.9 1.9 %shard_map.133 = (bf16[256,512]{1,0:T(8,128)(2,1)S(1)}, bf16[8,64,128]{2,1,0:T(8,128)(2,1)}) custom-call(bf16[256,512]{1,0:T(8,128)(2,1)S(1)} %get-tuple-element.34.refs_0_.refs_3_, bf16[256,512]{1,0:T(8,128)(2,1)S(1)} %copy-done.1, bf16[256,512]{1,0:T(8,128)(2,1)S(1)} %copy-done, bf16[8,64,128]{2,1,0:T(8,128)(2,1)S(1)} %all_to_all.56.refs_3_.refs_2_, ...), custom_call_target="tpu_custom_call" | custom-call | flops 100000000 | bytes 1000000 | tf_op jit(solution)/shard_map/pallas_call | solution.py:30
  105.9 3.4 %all-to-all-start.7 = ((bf16[8,64,128]{2,1,0:T(8,128)(2,1)}), bf16[8,64,128]{2,1,0:T(8,128)(2,1)S(1)}, u32[]{:S(2)}, u32[]{:S(2)}) async-start(bf16[8,64,128]{2,1,0:T(8,128)(2,1)} %get-tuple-element.44), calls=%async_computation.7 | async-start | bytes 262144 | tf_op jit(solution)/shard_map/all_to_all | solution.py:20
  109.3 2.4 %shard_map.134 = (bf16[256,512]{1,0:T(8,128)(2,1)}, bf16[256,512]{1,0:T(8,128)(2,1)}, bf16[256,512]{1,0:T(8,128)(2,1)}, bf16[256,512]{1,0:T(8,128)(2,1)}, f32[512]{0:T(512)}, /*index=5*/f32[8,128]{1,0:T(8,128)S(1)}) custom-call(bf16[256,512]{1,0:T(8,128)(2,1)S(1)} %get-tuple-element.37.refs_0_, bf16[4,128,128]{2,1,0:T(8,128)(2,1)S(1)} %copy-done.4, ...), custom_call_target="tpu_custom_call" | custom-call | flops 100000000 | bytes 1000000 | tf_op jit(solution)/shard_map/pallas_call | solution.py:30
  111.6 4.2 %all-to-all-done.7.refs_0_ = bf16[8,64,128]{2,1,0:T(8,128)(2,1)S(1)} async-done(((bf16[8,64,128]{2,1,0:T(8,128)(2,1)}), bf16[8,64,128]{2,1,0:T(8,128)(2,1)S(1)}, u32[]{:S(2)}, u32[]{:S(2)}) %all-to-all-start.7) | async-done | bytes 131104 | tf_op jit(solution)/shard_map/all_to_all | solution.py:20
  115.8 18.3 %all_to_all.57.refs_0_ = bf16[8,80,128]{2,1,0:T(8,128)(2,1)S(1)} all-to-all(bf16[8,80,128]{2,1,0:T(8,128)(2,1)S(1)} %shard_map.135), channel_id=1, replica_groups=mesh['far'=8,'near'=8,'head'=8] {'far'}, dimensions={0} | all-to-all | bytes 327680 | tf_op jit(solution)/shard_map/all_to_all | solution.py:20
  134.1 9.6 %all_to_all.58.refs_0_ = bf16[8,128,128]{2,1,0:T(8,128)(2,1)S(1)} all-to-all(bf16[8,128,128]{2,1,0:T(8,128)(2,1)S(1)} %shard_map.136), channel_id=1, replica_groups=mesh['far'=8,'near'=8,'head'=8] {'near'}, dimensions={0} | all-to-all | bytes 524288 | tf_op jit(solution)/shard_map/all_to_all | solution.py:20
  143.8 0.8 shard_map.137
  (4 shorter events, 0.1 us)
Async XLA Ops:
  15.6 38.0 %copy-start.6 = (bf16[256,512]{1,0:T(8,128)(2,1)S(1)}, bf16[256,512]{1,0:T(8,128)(2,1)}, u32[]{:S(2)}) copy-start(bf16[256,512]{1,0:T(8,128)(2,1)} %refs_2_.4) | copy-start | bytes 786436
  15.6 38.0 %copy-start.3 = (bf16[256,512]{1,0:T(8,128)(2,1)S(1)}, bf16[256,512]{1,0:T(8,128)(2,1)}, u32[]{:S(2)}) copy-start(bf16[256,512]{1,0:T(8,128)(2,1)} %get-tuple-element.29.refs_1_.refs_6_.refs_5_) | copy-start | bytes 786436
  43.5 10.1 %copy-start = (bf16[256,512]{1,0:T(8,128)(2,1)S(1)}, bf16[256,512]{1,0:T(8,128)(2,1)}, u32[]{:S(2)}) copy-start(bf16[256,512]{1,0:T(8,128)(2,1)} %refs_6_.1) | copy-start | bytes 786436
  43.5 10.1 %copy-start.1 = (bf16[256,512]{1,0:T(8,128)(2,1)S(1)}, bf16[256,512]{1,0:T(8,128)(2,1)}, u32[]{:S(2)}) copy-start(bf16[256,512]{1,0:T(8,128)(2,1)} %get-tuple-element.28.refs_0_.refs_4_.refs_1_) | copy-start | bytes 786436
  43.6 10.1 %copy-start.8 = (f32[8,512]{1,0:T(8,128)S(1)}, f32[8,512]{1,0:T(8,128)}, u32[]{:S(2)}) copy-start(f32[8,512]{1,0:T(8,128)} %get-tuple-element.31.refs_5_.refs_3_) | copy-start | bytes 49156
  53.7 9.8 %copy-start.2 = (bf16[256,512]{1,0:T(8,128)(2,1)S(1)}, bf16[256,512]{1,0:T(8,128)(2,1)}, u32[]{:S(2)}) copy-start(bf16[256,512]{1,0:T(8,128)(2,1)} %refs_8_.3) | copy-start | bytes 786436
  54.5 9.0 %copy-start.5 = (bf16[4,128,128]{2,1,0:T(8,128)(2,1)S(1)}, bf16[4,128,128]{2,1,0:T(8,128)(2,1)}, u32[]{:S(2)}) copy-start(bf16[4,128,128]{2,1,0:T(8,128)(2,1)} %refs_9_.3) | copy-start | bytes 393220
  93.0 10.9 %copy-start.7 = (bf16[256,512]{1,0:T(8,128)(2,1)S(1)}, bf16[256,512]{1,0:T(8,128)(2,1)}, u32[]{:S(2)}) copy-start(bf16[256,512]{1,0:T(8,128)(2,1)} %refs_5_.3) | copy-start | bytes 786436
  93.1 10.8 %copy-start.4 = (bf16[4,128,128]{2,1,0:T(8,128)(2,1)S(1)}, bf16[4,128,128]{2,1,0:T(8,128)(2,1)}, u32[]{:S(2)}) copy-start(bf16[4,128,128]{2,1,0:T(8,128)(2,1)} %refs_1_.1) | copy-start | bytes 393220
  105.9 9.9 %all-to-all-start.7 = ((bf16[8,64,128]{2,1,0:T(8,128)(2,1)}), bf16[8,64,128]{2,1,0:T(8,128)(2,1)S(1)}, u32[]{:S(2)}, u32[]{:S(2)}) async-start(bf16[8,64,128]{2,1,0:T(8,128)(2,1)} %get-tuple-element.44), calls=%async_computation.7 | async-start | bytes 262144 | tf_op jit(solution)/shard_map/all_to_all | solution.py:20
